TPU v7x, 512 devices: a whole 4x4x16 slice. The times are simulated.
512 devices in a mesh: dp: 32 (over z, core), tensor: 16 (over y, x).
Axes of the slice: x: 4, y: 4, z: 16, core: 2. Of those that a mesh axis runs over, the one named last changes fastest.
Arguments:
- hidden: bfloat16 [4096, 18432], P('dp', 'tensor'), may hold values from -80 to 80
- out_grad: bfloat16 [4096, 4608], P('dp'), may hold values from -80 to 80
- live: int32 [32], P('dp'), may hold values 0 or 1
Outputs:
- clipped_grad: float32 [18432, 4608], P('tensor', 'dp')
- norms: float32 [32], P('dp')
All inputs are finite; a program needn't handle non-finite values. No bound on the sum of `live` on one device may be relied on, other than what follows from the above.
Results may differ from a plain program's by a relative error of at most 0.0021.
Values may be sent and summed in bfloat16 or wider, within the bound.
No kernel may reach another device: no remote copies, remote signals or barrier semaphores. Data moves between devices by JAX's collectives and lax.ppermute only.
A program may use at most 64 MiB of HBM per device.

v0:
```python
import math

import jax
import jax.numpy as jnp
from jax import lax
from jax.sharding import PartitionSpec as P

D = 4608
UNITS = 18432


def per_device(hidden, out_grad, live):
    seq_rows = hidden.shape[0]
    gram_h = jnp.dot(hidden, hidden.T, preferred_element_type=jnp.float32)
    gram_g = jnp.dot(out_grad, out_grad.T, preferred_element_type=jnp.float32)
    total = lax.psum(jnp.sum(gram_h * gram_g), "tensor")
    q_value = total / (float(seq_rows) * float(UNITS) * float(D))
    norms = jnp.sqrt(q_value).reshape(1)
    clip = live.astype(jnp.float32)[0] * jnp.minimum(1.0, 1.0 / jnp.sqrt(q_value + 1e-06))
    scaled = (out_grad.astype(jnp.float32) * clip).astype(jnp.bfloat16)
    columns = lax.all_to_all(scaled, "dp", split_axis=1, concat_axis=0, tiled=True)
    gathered = lax.all_gather(hidden, "dp", axis=0, tiled=True)
    grad = lax.dot_general(
        gathered, columns, (((0,), (0,)), ((), ())), preferred_element_type=jnp.float32
    )
    grad = grad / math.sqrt(lax.axis_size("dp") * seq_rows)
    return (grad, norms)


def solution(mesh):
    placed = (P("dp", "tensor"), P("dp", None), P("dp"))
    return jax.shard_map(
        per_device,
        mesh=mesh,
        in_specs=placed,
        out_specs=(P("tensor", "dp"), P("dp")),
        check_vma=False,
    )
```

profile of v0, /device:TPU:1, one launch (start us, length us, event | category | flops | bytes accessed | tf_op | source)
XLA Modules:
  0.0 156.8 jit_solution(18418863634601969593)
XLA Ops:
  7.2 0.0 all-gather.2.cloned.1.call-start
  7.2 0.7 all-gather.2.cloned.1.call-update
  7.9 1.3 fusion.4
  9.2 0.0 copy-start
  9.2 2.9 %fusion.3 = f32[]{:T(128)} fusion(f32[128,128]{1,0:T(8,128)S(1)} %fusion.4, bf16[128,4608]{1,0:T(8,128)(2,1)} %param.4), kind=kOutput, calls=%fused_computation.6 | convolution fusion | flops 151027712 | bytes 1245188 | tf_op jit(solution)/shard_map/dot_general | solution.py:15
  12.2 34.9 %psum.7 = f32[]{:T(128)} all-reduce(f32[]{:T(128)} %fusion.3), channel_id=1, replica_groups=mesh['dp'=32,'tensor'=16] {'tensor'}, use_global_device_ids=true, to_apply=%region_1.0 | all-reduce | flops 1 | bytes 8 | tf_op jit(solution)/shard_map/psum | solution.py:16
  47.0 0.0 copy-done
  47.0 0.7 copy.5
  49.1 1.2 multiply_convert_fusion
  50.3 23.1 %all-to-all-start = ((bf16[128,32,144]{0,2,1:T(8,128)(2,1)}), bf16[128,32,144]{0,2,1:T(8,128)(2,1)S(1)}, u32[]{:S(2)}, u32[]{:S(2)}) async-start(bf16[128,32,144]{0,2,1:T(8,128)(2,1)} %bitcast.1), calls=%async_computation | async-start | bytes 2359296 | tf_op jit(solution)/shard_map/all_to_all | solution.py:21
  73.5 69.0 %all-to-all-done = bf16[128,32,144]{0,2,1:T(8,128)(2,1)S(1)} async-done(((bf16[128,32,144]{0,2,1:T(8,128)(2,1)}), bf16[128,32,144]{0,2,1:T(8,128)(2,1)S(1)}, u32[]{:S(2)}, u32[]{:S(2)}) %all-to-all-start) | async-done | bytes 1179680 | tf_op jit(solution)/shard_map/all_to_all | solution.py:21
  142.6 0.0 all-gather.2.cloned.1.call-done
  142.6 6.2 %fusion = f32[1152,144]{0,1:T(8,128)} fusion(bf16[4096,1152]{1,0:T(8,128)(2,1)} %all-gather.2.cloned.1.call-done, bf16[128,32,144]{0,2,1:T(8,128)(2,1)S(1)} %all-to-all-done), kind=kOutput, calls=%fused_computation.1 | convolution fusion | flops 1359120384 | bytes 11280384 | tf_op jit(solution)/shard_map/dot_general | solution.py:23
Async XLA Ops:
  7.2 135.4 %all-gather.2.cloned.1.call-start = ((), (), s32[]{:S(2)}) async-start(), calls=%async_computation.1 | async-start | bytes 9732096 | tf_op jit(solution)/shard_map/all_gather | solution.py:22
  9.2 37.8 %copy-start = (bf16[128,4608]{1,0:T(8,128)(2,1)S(1)}, bf16[128,4608]{1,0:T(8,128)(2,1)}, u32[]{:S(2)}) copy-start(bf16[128,4608]{1,0:T(8,128)(2,1)} %param.4) | copy-start | bytes 3538948
  50.3 92.2 %all-to-all-start = ((bf16[128,32,144]{0,2,1:T(8,128)(2,1)}), bf16[128,32,144]{0,2,1:T(8,128)(2,1)S(1)}, u32[]{:S(2)}, u32[]{:S(2)}) async-start(bf16[128,32,144]{0,2,1:T(8,128)(2,1)} %bitcast.1), calls=%async_computation | async-start | bytes 2359296 | tf_op jit(solution)/shard_map/all_to_all | solution.py:21
Sparse Core Ops, SparseCore 0:
  10.1 130.6 all-gather.1
where the time goes:
time: 158 us; the launch traced here: 157 us
  waiting for transfers between devices  69.7 us (44%)
  blocking collectives  34.9 us (22%)
  starting transfers between devices  23.2 us (15%)
  between operations  16.6 us (11%)
  matrix products  10.5 us (7%)
    all_to_all x1, waiting for transfers between devices, per_device(): lax.all_to_all(scaled, 'dp', split_axis=1, concat_axis=0, tiled=True)  69 us
    psum x1, blocking collectives, per_device(): total = lax.psum(jnp.sum(gram_h * gram_g), 'tensor')  34.9 us
    all_to_all x1, starting transfers between devices, per_device(): lax.all_to_all(scaled, 'dp', split_axis=1, concat_axis=0, tiled=True)  23.1 us
    dot_general x1, matrix products, per_device(): lax.dot_general(gathered, columns, (((0,), (0,)), ((), ())), preferred_el...  6.22 us
  transfers between devices with their start and end apart: 2, of which 1 were waited for; matrix products, arithmetic and copies ran while one was open for 4% of the time, Pallas kernels for 0%

commit v1 on v0

v1 whole, which is shorter than its diff:
```python
import math

import jax
import jax.numpy as jnp
from jax import lax
from jax.experimental import pallas as pl
from jax.experimental.pallas import tpu as pltpu
from jax.sharding import Mesh, PartitionSpec as P

D = 4608
UNITS = 18432
SEQ = 128
NZ, NC, NY, NX = 16, 2, 4, 4
NT = NY * NX
CHIP = D // NZ
OWN = CHIP // NC
TAIL = 16
HOPS = NZ // 2

LINE = ("z", "core")
PLANE = ("y", "x")
ALL = ("z", "core", "y", "x")
STEP = [(z * 2, (z + 1) % NZ * 2) for z in range(NZ)]
STEP += [(z * 2 + 1, (z - 1) % NZ * 2 + 1) for z in range(NZ)]
SWAP = [(0, 1), (1, 0)]


def spread_pairs():
    pairs = []
    for z in range(NZ):
        for c in range(NC):
            for t in range(NT):
                to_z = (z + t if c == 0 else z - t) % NZ
                to_c = c if t <= HOPS else 1 - c
                pairs.append(((z * NC + c) * NT + t, (to_z * NC + to_c) * NT + t))
    return pairs


def vmem():
    return pl.BlockSpec(memory_space=pltpu.VMEM)


def smem():
    return pl.BlockSpec(memory_space=pltpu.SMEM)


def call(kernel, outs, ins, name, flops, scratch=(), aliases=None):
    moved = sum(math.prod(a.shape) * a.dtype.itemsize for a in list(ins) + list(outs))
    return pl.pallas_call(
        kernel,
        out_shape=outs,
        in_specs=[smem() if a.dtype == jnp.int32 else vmem() for a in ins],
        out_specs=[vmem() for _ in outs],
        scratch_shapes=list(scratch),
        input_output_aliases=aliases or {},
        compiler_params=pltpu.CompilerParams(vmem_limit_bytes=40 * 1024 * 1024),
        cost_estimate=pl.CostEstimate(flops=flops, bytes_accessed=moved, transcendentals=0),
        name=name,
    )(*ins)


def gram_kernel(h_ref, g_ref, p_ref):
    dims = (((1,), (1,)), ((), ()))
    h, g = h_ref[...], g_ref[...]
    gram_h = lax.dot_general(h, h, dims, preferred_element_type=jnp.float32)
    gram_g = lax.dot_general(g, g, dims, preferred_element_type=jnp.float32)
    p_ref[...] = jnp.full(p_ref.shape, jnp.sum(gram_h * gram_g), jnp.float32)


def pack_kernel(to_ref, g_ref, out_ref, turned):
    start = to_ref[0] * CHIP
    base = pl.multiple_of(start // 128 * 128, 128)
    window = g_ref[:, pl.ds(base, 384)].astype(jnp.float32)
    turned[...] = window.T
    out_ref[...] = turned[pl.ds(pl.multiple_of(start - base, 32), CHIP), :].astype(jnp.bfloat16)


def bundle_kernel(own_ref, other_ref, block_ref, out_ref):
    sub = lax.broadcasted_iota(jnp.int32, (NZ, 128), 0)
    lane = lax.broadcasted_iota(jnp.int32, (NZ, 128), 1)

    def in_lanes(row):
        mine = jnp.where(lane == sub, own_ref[:, row, :], 0.0)
        others = jnp.where(lane == sub + NZ, other_ref[:, row, :], 0.0)
        return jnp.sum(mine + others, axis=0, keepdims=True)

    part, live = in_lanes(0), in_lanes(1)
    high = part.astype(jnp.bfloat16).astype(jnp.float32)
    middle = (part - high).astype(jnp.bfloat16).astype(jnp.float32)
    low = part - high - middle
    rows = lax.broadcasted_iota(jnp.int32, (TAIL, 128), 0)
    tail = jnp.where(rows == 0, high, jnp.where(rows == 1, middle, jnp.where(rows == 2, low, jnp.where(rows == 3, live, 0.0))))
    tail = tail.astype(jnp.bfloat16)
    block = block_ref[...]
    for t in range(NT):
        out_ref[t, 0:CHIP, :] = block
        out_ref[t, CHIP:CHIP + TAIL, :] = tail


def scale_kernel(at_ref, got_ref, s_ref, norm_ref):
    z, core = at_ref[0], at_ref[1]
    sign = 1 - 2 * core
    tails = got_ref[:, CHIP:CHIP + TAIL, :].astype(jnp.float32)
    total = jnp.sum(tails, axis=0)
    q = (total[0:1] + total[1:2] + total[2:3]) / (float(SEQ) * float(UNITS) * float(D))
    live = tails[0, 3:4, :]
    clip = live * jnp.minimum(1.0, 1.0 / jnp.sqrt(q + 1e-06))
    lane = lax.broadcasted_iota(jnp.int32, (1, 128), 1)

    def pick(row, at):
        return jnp.sum(jnp.where(lane == at, row, 0.0), axis=1, keepdims=True)

    norm_ref[...] = jnp.broadcast_to(pick(jnp.sqrt(q), z), norm_ref.shape)
    own = pl.multiple_of(core * OWN, 16)
    other = pl.multiple_of((1 - core) * OWN, 16)
    for t in range(NT):
        hops = t if t <= HOPS else NZ - t
        at = lax.rem(z - sign * hops + NZ, NZ) + (0 if t <= HOPS else NZ)
        factor = pick(clip, at)
        s_ref[t, 0:OWN, :] = (got_ref[t, pl.ds(own, OWN), :].astype(jnp.float32) * factor).astype(jnp.bfloat16)
        s_ref[t, OWN:CHIP, :] = (got_ref[t, pl.ds(other, OWN), :].astype(jnp.float32) * factor).astype(jnp.bfloat16)


def product(s_ref, hop, p, q):
    if q is None:
        return jnp.dot(s_ref[hop], p[...], preferred_element_type=jnp.float32)
    left = jnp.concatenate([s_ref[hop], s_ref[NZ - hop]], axis=1)
    right = jnp.concatenate([p[...], q[...]], axis=0)
    return jnp.dot(left, right, preferred_element_type=jnp.float32)


def matmul(s, hops, ps, qs, acc, last):
    blocks = [b for hop in hops for b in (ps[hop], qs[hop]) if b is not None]
    ins = [s] + blocks + ([acc] if acc is not None else [])
    units = blocks[0].shape[1]

    def kernel(*refs):
        s_ref, rest = refs[0], list(refs[1:])
        taken = [(hop, rest.pop(0), rest.pop(0) if qs[hop] is not None else None) for hop in hops]
        total = rest.pop(0)[...] if acc is not None else None
        for hop, p, q in taken:
            term = product(s_ref, hop, p, q)
            total = term if total is None else total + term
        if last:
            rest[0][...] = total[0:OWN]
            rest[1][...] = total[OWN:CHIP]
        else:
            rest[0][...] = total

    if last:
        outs = [jax.ShapeDtypeStruct((OWN, units), jnp.float32)] * 2
    else:
        outs = [jax.ShapeDtypeStruct((CHIP, units), jnp.float32)]
    flops = 2 * CHIP * units * SEQ * len(blocks)
    return call(kernel, outs, ins, "products", flops)


def per_device(hidden, out_grad, live):
    z, core = lax.axis_index("z"), lax.axis_index("core")
    t = lax.axis_index(PLANE)
    units = hidden.shape[1]

    ps, qs = [hidden], [None]
    p, q = hidden, None
    p = lax.ppermute(p, LINE, STEP)
    q = lax.ppermute(hidden, "core", SWAP)
    ps.append(p)
    for hop in range(1, HOPS):
        q = lax.ppermute(q, LINE, STEP)
        qs.append(q)
        p = lax.ppermute(p, LINE, STEP)
        ps.append(p)
    qs.append(None)

    to = lax.rem(z + (1 - 2 * core) * t + NZ, NZ).astype(jnp.int32).reshape(1)
    [block] = call(pack_kernel, [jax.ShapeDtypeStruct((CHIP, SEQ), jnp.bfloat16)], [to, out_grad], "pack", 0,
                   scratch=[pltpu.VMEM((384, SEQ), jnp.float32)])
    block = lax.ppermute(block, ALL, spread_pairs())

    [part] = call(gram_kernel, [jax.ShapeDtypeStruct((8, 128), jnp.float32)], [hidden, out_grad], "grams",
                  2 * SEQ * SEQ * (units + D))
    row = lax.broadcasted_iota(jnp.int32, (8, 128), 0)
    part = jnp.where(row == 0, part, jnp.where(row == 1, live.astype(jnp.float32)[0], 0.0))
    parts = lax.all_to_all(jnp.broadcast_to(part[None], (NZ, 8, 128)), "z", 0, 0, tiled=True)
    others = lax.ppermute(parts, "core", SWAP)

    [bundle] = call(bundle_kernel, [jax.ShapeDtypeStruct((NT, CHIP + TAIL, SEQ), jnp.bfloat16)], [parts, others, block], "bundle", 0)
    got = lax.all_to_all(bundle, PLANE, 0, 0, tiled=False)

    at = jnp.stack([z, core]).astype(jnp.int32)
    s, norm = call(scale_kernel, [jax.ShapeDtypeStruct((NT, CHIP, SEQ), jnp.bfloat16), jax.ShapeDtypeStruct((8, 128), jnp.float32)],
                   [at, got], "scale", 0)

    [acc] = matmul(s, range(0, 6), ps, qs, None, False)
    [acc] = matmul(s, range(6, 8), ps, qs, acc, False)
    mine, theirs = matmul(s, range(8, 9), ps, qs, acc, True)
    total = mine + lax.ppermute(theirs, "core", SWAP)
    grad = (total / math.sqrt(NZ * NC * SEQ)).T
    return grad, norm[0, 0:1]


def solution(mesh):
    grid = Mesh(mesh.devices.reshape(NZ, NC, NY, NX), ALL)
    return jax.shard_map(
        per_device,
        mesh=grid,
        in_specs=(P(LINE, PLANE), P(LINE, None), P(LINE)),
        out_specs=(P(PLANE, LINE), P(LINE)),
        check_vma=False,
    )
```

time: 158 us -> 125 us (0.79)
  starting transfers between devices: 23.2 us -> 97.9 us
  waiting for transfers between devices: 69.7 us -> 8.61 us
  blocking collectives: 34.9 us -> 0 us
  between operations: 16.6 us -> 1.68 us
  matrix products: 10.5 us -> 0 us
  Pallas kernels: 0 us -> 8.16 us
  local copies, waits for them, and re-layouts: 0.73 us -> 6.5 us
    ppermute x0 -> x19, starting transfers between devices: none -> 79.9 us  [the longest x7 27.9 us: per_device(): q = lax.ppermute(q, LINE, STEP)]
    all_to_all x1 -> x2, waiting for transfers between devices: 69 us -> 3.31 us  [the longest x1 3.31 us: per_device(): lax.all_to_all(jnp.broadcast_to(part[None], (NZ, 8, 128)), 'z', 0, 0, til...]
    psum x1 -> x0, blocking collectives: 34.9 us -> none  [per_device(): total = lax.psum(jnp.sum(gram_h * gram_g), 'tensor')]
    dot_general x3 -> x0, matrix products: 10.5 us -> none  [the longest x1 6.22 us: per_device(): lax.dot_general(gathered, columns, (((0,), (0,)), ((), ())), preferred_el...]
    pallas_call x0 -> x7, Pallas kernels: none -> 8.16 us  [call(): pl.pallas_call(kernel, out_shape=outs, in_specs=[smem() if a.dtype == jnp...]
    ppermute x0 -> x19, waiting for transfers between devices: none -> 5.3 us  [the longest x7 1.9 us: per_device(): q = lax.ppermute(q, LINE, STEP)]
    all_to_all x1 -> x2, starting transfers between devices: 23.1 us -> 18.1 us  [the longest x1 12.3 us: per_device(): got = lax.all_to_all(bundle, PLANE, 0, 0, tiled=False)]
    unnamed x3 -> x24, local copies, waits for them, and re-layouts: 0.73 us -> 5.35 us
  transfers between devices with their start and end apart: 2 -> 21, of which waited for: 1 -> 5; matrix products, arithmetic and copies ran while one was open for 4% -> 1% of each run, Pallas kernels for 0% -> 6%
where the time goes in v1:
time: 125 us; the launch traced here: 124 us
  starting transfers between devices  97.9 us (78%)
  waiting for transfers between devices  8.61 us (7%)
  Pallas kernels  8.16 us (7%)
  local copies, waits for them, and re-layouts  6.5 us (5%)
  between operations  1.68 us (1%)
    ppermute x7, starting transfers between devices, per_device(): q = lax.ppermute(q, LINE, STEP)  27.9 us
    ppermute x8, starting transfers between devices, per_device(): p = lax.ppermute(p, LINE, STEP)  26.8 us
    all_to_all x1, starting transfers between devices, per_device(): got = lax.all_to_all(bundle, PLANE, 0, 0, tiled=False)  12.3 us
    ppermute x1, starting transfers between devices, per_device(): total = mine + lax.ppermute(theirs, 'core', SWAP)  9.5 us
    ppermute x1, starting transfers between devices, per_device(): q = lax.ppermute(hidden, 'core', SWAP)  8.79 us
    pallas_call x7, Pallas kernels, call(): pl.pallas_call(kernel, out_shape=outs, in_specs=[smem() if a.dtype == jnp...  8.16 us
    ppermute x1, starting transfers between devices, per_device(): others = lax.ppermute(parts, 'core', SWAP)  6.22 us
    all_to_all x1, starting transfers between devices, per_device(): lax.all_to_all(jnp.broadcast_to(part[None], (NZ, 8, 128)), 'z', 0, 0, til...  5.71 us
  transfers between devices with their start and end apart: 21, of which 5 were waited for; matrix products, arithmetic and copies ran while one was open for 1% of the time, Pallas kernels for 6%

profile of v1, /device:TPU:1, one launch (start us, length us, event | category | flops | bytes accessed | tf_op | source)
XLA Modules:
  0.0 124.0 jit_solution(15804161085778249893)
XLA Ops:
  0.6 8.8 %collective-permute-start.10 = (bf16[128,1152]{1,0:T(8,128)(2,1)}, bf16[128,1152]{1,0:T(8,128)(2,1)S(1)}, u32[]{:S(2)}, u32[]{:S(2)}) collective-permute-start(bf16[128,1152]{1,0:T(8,128)(2,1)} %refs_1_.1), channel_id=1, source_target_pairs={{0,16},{16,0},{1,17},{17,1},{2,18},{18,2},{3,19},{19,3},{4,20},{20... | collective-permute-start | bytes 884744 | tf_op jit(solution)/shard_map/ppermute | solution.py:166
  9.4 5.8 %collective-permute-start.2 = (bf16[128,1152]{1,0:T(8,128)(2,1)}, bf16[128,1152]{1,0:T(8,128)(2,1)S(1)}, u32[]{:S(2)}, u32[]{:S(2)}) collective-permute-start(bf16[128,1152]{1,0:T(8,128)(2,1)} %refs_1_.1), channel_id=1, source_target_pairs={{0,32},{32,64},{64,96},{96,128},{128,160},{160,192},{192,224},{224... | collective-permute-start | bytes 884744 | tf_op jit(solution)/shard_map/ppermute | solution.py:165
  15.2 2.6 %collective-permute-start.11 = (bf16[128,1152]{1,0:T(8,128)(2,1)S(1)}, bf16[128,1152]{1,0:T(8,128)(2,1)S(1)}, u32[]{:S(2)}, u32[]{:S(2)}) collective-permute-start(bf16[128,1152]{1,0:T(8,128)(2,1)S(1)} %collective-permute-done.10), channel_id=1, source_target_pairs={{0,32},{32,64},{64,96},{96,128},{128,160},{160,192},{192,224},{224... | collective-permute-start | bytes 884744 | tf_op jit(solution)/shard_map/ppermute | solution.py:169
  17.8 1.3 %collective-permute-done.2.refs_2_ = bf16[128,1152]{1,0:T(8,128)(2,1)S(1)} collective-permute-done((bf16[128,1152]{1,0:T(8,128)(2,1)}, bf16[128,1152]{1,0:T(8,128)(2,1)S(1)}, u32[]{:S(2)}, u32[]{:S(2)}) %collective-permute-start.2) | collective-permute-done | bytes 294944 | tf_op jit(solution)/shard_map/ppermute | solution.py:165
  19.1 4.9 %collective-permute-start.3 = (bf16[128,1152]{1,0:T(8,128)(2,1)S(1)}, bf16[128,1152]{1,0:T(8,128)(2,1)S(1)}, u32[]{:S(2)}, u32[]{:S(2)}) collective-permute-start(bf16[128,1152]{1,0:T(8,128)(2,1)S(1)} %collective-permute-done.2.refs_2_), channel_id=1, source_target_pairs={{0,32},{32,64},{64,96},{96,128},{128,160},{160,192},{192,224},{224... | collective-permute-start | bytes 884744 | tf_op jit(solution)/shard_map/ppermute | solution.py:171
  24.7 1.3 %copy-done = bf16[128,4608]{1,0:T(8,128)(2,1)S(1)} copy-done((bf16[128,4608]{1,0:T(8,128)(2,1)S(1)}, bf16[128,4608]{1,0:T(8,128)(2,1)}, u32[]{:S(2)}) %copy-start) | copy-done | bytes 1179672
  26.0 1.0 copy-done.2
  26.9 0.7 grams.1
  27.7 1.9 %collective-permute-start.12 = (bf16[128,1152]{1,0:T(8,128)(2,1)S(1)}, bf16[128,1152]{1,0:T(8,128)(2,1)S(1)}, u32[]{:S(2)}, u32[]{:S(2)}) collective-permute-start(bf16[128,1152]{1,0:T(8,128)(2,1)S(1)} %collective-permute-done.11.refs_3_), channel_id=1, source_target_pairs={{0,32},{32,64},{64,96},{96,128},{128,160},{160,192},{192,224},{224... | collective-permute-start | bytes 884744 | tf_op jit(solution)/shard_map/ppermute | solution.py:169
  29.6 3.1 %collective-permute-start.4 = (bf16[128,1152]{1,0:T(8,128)(2,1)S(1)}, bf16[128,1152]{1,0:T(8,128)(2,1)S(1)}, u32[]{:S(2)}, u32[]{:S(2)}) collective-permute-start(bf16[128,1152]{1,0:T(8,128)(2,1)S(1)} %collective-permute-done.3.refs_4_), channel_id=1, source_target_pairs={{0,32},{32,64},{64,96},{96,128},{128,160},{160,192},{192,224},{224... | collective-permute-start | bytes 884744 | tf_op jit(solution)/shard_map/ppermute | solution.py:171
  32.7 0.1 broadcast_select_fusion
  32.8 0.6 broadcast_in_dim.16
  33.4 5.7 %all-to-all-start = ((f32[16,8,128]{2,1,0:T(8,128)}), f32[16,8,128]{2,1,0:T(8,128)S(1)}, u32[]{:S(2)}, u32[]{:S(2)}) async-start(f32[16,8,128]{2,1,0:T(8,128)} %broadcast_in_dim.16), calls=%async_computation | async-start | bytes 131072 | tf_op jit(solution)/shard_map/all_to_all | solution.py:184
  39.2 4.5 %collective-permute-start.13 = (bf16[128,1152]{1,0:T(8,128)(2,1)S(1)}, bf16[128,1152]{1,0:T(8,128)(2,1)S(1)}, u32[]{:S(2)}, u32[]{:S(2)}) collective-permute-start(bf16[128,1152]{1,0:T(8,128)(2,1)S(1)} %collective-permute-done.12.refs_5_), channel_id=1, source_target_pairs={{0,32},{32,64},{64,96},{96,128},{128,160},{160,192},{192,224},{224... | collective-permute-start | bytes 884744 | tf_op jit(solution)/shard_map/ppermute | solution.py:169
  43.7 3.1 %collective-permute-start.5 = (bf16[128,1152]{1,0:T(8,128)(2,1)S(1)}, bf16[128,1152]{1,0:T(8,128)(2,1)}, u32[]{:S(2)}, u32[]{:S(2)}) collective-permute-start(bf16[128,1152]{1,0:T(8,128)(2,1)S(1)} %collective-permute-done.4.refs_6_), channel_id=1, source_target_pairs={{0,32},{32,64},{64,96},{96,128},{128,160},{160,192},{192,224},{224... | collective-permute-start | bytes 884744 | tf_op jit(solution)/shard_map/ppermute | solution.py:171
  46.8 0.1 pack.1
  46.9 0.7 collective-permute-start.1
  47.6 3.3 %all-to-all-done.own_ref = f32[16,8,128]{2,1,0:T(8,128)S(1)} async-done(((f32[16,8,128]{2,1,0:T(8,128)}), f32[16,8,128]{2,1,0:T(8,128)S(1)}, u32[]{:S(2)}, u32[]{:S(2)}) %all-to-all-start) | async-done | bytes 65568 | tf_op jit(solution)/shard_map/all_to_all | solution.py:184
  50.9 6.2 %collective-permute-start = (f32[16,8,128]{2,1,0:T(8,128)S(1)}, f32[16,8,128]{2,1,0:T(8,128)S(1)}, u32[]{:S(2)}, u32[]{:S(2)}) collective-permute-start(f32[16,8,128]{2,1,0:T(8,128)S(1)} %all-to-all-done.own_ref), channel_id=1, source_target_pairs={{0,16},{16,0},{1,17},{17,1},{2,18},{18,2},{3,19},{19,3},{4,20},{20... | collective-permute-start | bytes 196616 | tf_op jit(solution)/shard_map/ppermute | solution.py:185
  57.2 0.9 collective-permute-done.other_ref
  58.0 1.2 %bundle.1 = bf16[16,304,128]{2,1,0:T(8,128)(2,1)} custom-call(f32[16,8,128]{2,1,0:T(8,128)S(1)} %all-to-all-done.own_ref, f32[16,8,128]{2,1,0:T(8,128)S(1)} %collective-permute-done.other_ref, bf16[288,128]{1,0:T(8,128)(2,1)S(1)} %collective-permute-done.1.block_ref), custom_call_target="tpu_custom_call" | custom-call | bytes 1449984 | tf_op jit(solution)/shard_map/bundle/pallas_call | solution.py:49
  59.3 12.3 %all-to-all-start.1 = ((bf16[16,304,128]{2,1,0:T(8,128)(2,1)}), bf16[16,304,128]{2,1,0:T(8,128)(2,1)S(1)}, u32[]{:S(2)}, u32[]{:S(2)}) async-start(bf16[16,304,128]{2,1,0:T(8,128)(2,1)} %bundle.1), calls=%async_computation.1 | async-start | bytes 2490368 | tf_op jit(solution)/shard_map/all_to_all | solution.py:188
  71.6 0.0 copy-start.3
  71.6 4.1 %collective-permute-start.14 = (bf16[128,1152]{1,0:T(8,128)(2,1)S(1)}, bf16[128,1152]{1,0:T(8,128)(2,1)S(1)}, u32[]{:S(2)}, u32[]{:S(2)}) collective-permute-start(bf16[128,1152]{1,0:T(8,128)(2,1)S(1)} %collective-permute-done.13.refs_7_), channel_id=1, source_target_pairs={{0,32},{32,64},{64,96},{96,128},{128,160},{160,192},{192,224},{224... | collective-permute-start | bytes 884744 | tf_op jit(solution)/shard_map/ppermute | solution.py:169
  75.7 1.9 %collective-permute-start.6 = (bf16[128,1152]{1,0:T(8,128)(2,1)}, bf16[128,1152]{1,0:T(8,128)(2,1)S(1)}, u32[]{:S(2)}, u32[]{:S(2)}) collective-permute-start(bf16[128,1152]{1,0:T(8,128)(2,1)} %collective-permute-done.5.refs_8_), channel_id=1, source_target_pairs={{0,32},{32,64},{64,96},{96,128},{128,160},{160,192},{192,224},{224... | collective-permute-start | bytes 884744 | tf_op jit(solution)/shard_map/ppermute | solution.py:171
  77.7 1.9 %collective-permute-done.14.refs_9_ = bf16[128,1152]{1,0:T(8,128)(2,1)S(1)} collective-permute-done((bf16[128,1152]{1,0:T(8,128)(2,1)S(1)}, bf16[128,1152]{1,0:T(8,128)(2,1)S(1)}, u32[]{:S(2)}, u32[]{:S(2)}) %collective-permute-start.14) | collective-permute-done | bytes 294944 | tf_op jit(solution)/shard_map/ppermute | solution.py:169
  79.5 5.1 %collective-permute-start.15 = (bf16[128,1152]{1,0:T(8,128)(2,1)S(1)}, bf16[128,1152]{1,0:T(8,128)(2,1)S(1)}, u32[]{:S(2)}, u32[]{:S(2)}) collective-permute-start(bf16[128,1152]{1,0:T(8,128)(2,1)S(1)} %collective-permute-done.14.refs_9_), channel_id=1, source_target_pairs={{0,32},{32,64},{64,96},{96,128},{128,160},{160,192},{192,224},{224... | collective-permute-start | bytes 884744 | tf_op jit(solution)/shard_map/ppermute | solution.py:169
  84.7 0.7 copy-done.4
  85.4 2.4 %collective-permute-start.7 = (bf16[128,1152]{1,0:T(8,128)(2,1)S(1)}, bf16[128,1152]{1,0:T(8,128)(2,1)S(1)}, u32[]{:S(2)}, u32[]{:S(2)}) collective-permute-start(bf16[128,1152]{1,0:T(8,128)(2,1)S(1)} %collective-permute-done.6.refs_10_), channel_id=1, source_target_pairs={{0,32},{32,64},{64,96},{96,128},{128,160},{160,192},{192,224},{224... | collective-permute-start | bytes 884744 | tf_op jit(solution)/shard_map/ppermute | solution.py:171
  87.8 0.7 copy-done.6
  88.5 4.8 %collective-permute-start.16 = (bf16[128,1152]{1,0:T(8,128)(2,1)S(1)}, bf16[128,1152]{1,0:T(8,128)(2,1)}, u32[]{:S(2)}, u32[]{:S(2)}) collective-permute-start(bf16[128,1152]{1,0:T(8,128)(2,1)S(1)} %collective-permute-done.15.refs_11_), channel_id=1, source_target_pairs={{0,32},{32,64},{64,96},{96,128},{128,160},{160,192},{192,224},{224... | collective-permute-start | bytes 884744 | tf_op jit(solution)/shard_map/ppermute | solution.py:169
  93.4 0.7 copy-done.8
  94.1 2.4 %collective-permute-start.8 = (bf16[128,1152]{1,0:T(8,128)(2,1)S(1)}, bf16[128,1152]{1,0:T(8,128)(2,1)}, u32[]{:S(2)}, u32[]{:S(2)}) collective-permute-start(bf16[128,1152]{1,0:T(8,128)(2,1)S(1)} %collective-permute-done.7.refs_1_), channel_id=1, source_target_pairs={{0,32},{32,64},{64,96},{96,128},{128,160},{160,192},{192,224},{224... | collective-permute-start | bytes 884744 | tf_op jit(solution)/shard_map/ppermute | solution.py:171
  96.5 0.7 copy-done.10
  97.2 4.9 %collective-permute-start.17 = (bf16[128,1152]{1,0:T(8,128)(2,1)}, bf16[128,1152]{1,0:T(8,128)(2,1)}, u32[]{:S(2)}, u32[]{:S(2)}) collective-permute-start(bf16[128,1152]{1,0:T(8,128)(2,1)} %collective-permute-done.16.refs_2_), channel_id=1, source_target_pairs={{0,32},{32,64},{64,96},{96,128},{128,160},{160,192},{192,224},{224... | collective-permute-start | bytes 884744 | tf_op jit(solution)/shard_map/ppermute | solution.py:169
  102.1 3.1 %collective-permute-start.9 = (bf16[128,1152]{1,0:T(8,128)(2,1)}, bf16[128,1152]{1,0:T(8,128)(2,1)}, u32[]{:S(2)}, u32[]{:S(2)}) collective-permute-start(bf16[128,1152]{1,0:T(8,128)(2,1)} %collective-permute-done.8.refs_3_), channel_id=1, source_target_pairs={{0,32},{32,64},{64,96},{96,128},{128,160},{160,192},{192,224},{224... | collective-permute-start | bytes 884744 | tf_op jit(solution)/shard_map/ppermute | solution.py:171
  105.3 0.1 pad_add_fusion.at_ref
  105.4 0.9 scale.1
  106.2 0.1 copy-done.5
  106.3 0.1 copy-done.7
  106.4 0.1 copy-done.9
  106.5 2.3 %products.3.refs_5_ = f32[288,1152]{1,0:T(8,128)S(1)} custom-call(bf16[16,288,128]{2,1,0:T(8,128)(2,1)S(1)} %get-tuple-element.6.refs_0_, bf16[128,1152]{1,0:T(8,128)(2,1)S(1)} %copy-done.3, bf16[128,1152]{1,0:T(8,128)(2,1)S(1)} %collective-permute-done.2.refs_2_, bf16[128,1152]{1,0:T(8,128)(2,1)S(1)} %collective-permute-done.11.refs_3_, ...), custom_call_target="tpu_custom_call" | custom-call | flops 934281216 | bytes 5750784 | tf_op jit(solution)/shard_map/products/pallas_call | solution.py:49
  108.8 1.7 %products.4.refs_2_ = f32[288,1152]{1,0:T(8,128)S(1)} custom-call(bf16[16,288,128]{2,1,0:T(8,128)(2,1)S(1)} %get-tuple-element.6.refs_0_, bf16[128,1152]{1,0:T(8,128)(2,1)S(1)} %copy-done.11, bf16[128,1152]{1,0:T(8,128)(2,1)} %collective-permute-done.16.refs_2_, bf16[128,1152]{1,0:T(8,128)(2,1)} %collective-permute-done.8.refs_3_, ...), custom_call_target="tpu_custom_call" | custom-call | flops 339738624 | bytes 5013504 | tf_op jit(solution)/shard_map/products/pallas_call | solution.py:49
  110.5 1.3 %products.5 = (f32[144,1152]{1,0:T(8,128)S(1)}, f32[144,1152]{1,0:T(8,128)S(1)}) custom-call(bf16[16,288,128]{2,1,0:T(8,128)(2,1)S(1)} %get-tuple-element.6.refs_0_, bf16[128,1152]{1,0:T(8,128)(2,1)} %collective-permute-done.9.refs_1_, f32[288,1152]{1,0:T(8,128)S(1)} %products.4.refs_2_), custom_call_target="tpu_custom_call" | custom-call | flops 84934656 | bytes 4128768 | tf_op jit(solution)/shard_map/products/pallas_call | solution.py:49
  111.8 9.5 %collective-permute-start.18 = (f32[144,1152]{1,0:T(8,128)S(1)}, f32[144,1152]{1,0:T(8,128)S(1)}, u32[]{:S(2)}, u32[]{:S(2)}) collective-permute-start(f32[144,1152]{1,0:T(8,128)S(1)} %get-tuple-element.8), channel_id=1, source_target_pairs={{0,16},{16,0},{1,17},{17,1},{2,18},{18,2},{3,19},{19,3},{4,20},{20... | collective-permute-start | bytes 1990664 | tf_op jit(solution)/shard_map/ppermute | solution.py:197
  121.3 0.5 slice.3
  121.8 1.2 collective-permute-done.18
  123.0 0.9 multiply_bitcast_fusion
  (32 shorter events, 0.1 us)
Async XLA Ops:
  0.6 14.6 %collective-permute-start.10 = (bf16[128,1152]{1,0:T(8,128)(2,1)}, bf16[128,1152]{1,0:T(8,128)(2,1)S(1)}, u32[]{:S(2)}, u32[]{:S(2)}) collective-permute-start(bf16[128,1152]{1,0:T(8,128)(2,1)} %refs_1_.1), channel_id=1, source_target_pairs={{0,16},{16,0},{1,17},{17,1},{2,18},{18,2},{3,19},{19,3},{4,20},{20... | collective-permute-start | bytes 884744 | tf_op jit(solution)/shard_map/ppermute | solution.py:166
  9.4 9.7 %collective-permute-start.2 = (bf16[128,1152]{1,0:T(8,128)(2,1)}, bf16[128,1152]{1,0:T(8,128)(2,1)S(1)}, u32[]{:S(2)}, u32[]{:S(2)}) collective-permute-start(bf16[128,1152]{1,0:T(8,128)(2,1)} %refs_1_.1), channel_id=1, source_target_pairs={{0,32},{32,64},{64,96},{96,128},{128,160},{160,192},{192,224},{224... | collective-permute-start | bytes 884744 | tf_op jit(solution)/shard_map/ppermute | solution.py:165
  15.2 12.5 %collective-permute-start.11 = (bf16[128,1152]{1,0:T(8,128)(2,1)S(1)}, bf16[128,1152]{1,0:T(8,128)(2,1)S(1)}, u32[]{:S(2)}, u32[]{:S(2)}) collective-permute-start(bf16[128,1152]{1,0:T(8,128)(2,1)S(1)} %collective-permute-done.10), channel_id=1, source_target_pairs={{0,32},{32,64},{64,96},{96,128},{128,160},{160,192},{192,224},{224... | collective-permute-start | bytes 884744 | tf_op jit(solution)/shard_map/ppermute | solution.py:169
  19.1 10.5 %collective-permute-start.3 = (bf16[128,1152]{1,0:T(8,128)(2,1)S(1)}, bf16[128,1152]{1,0:T(8,128)(2,1)S(1)}, u32[]{:S(2)}, u32[]{:S(2)}) collective-permute-start(bf16[128,1152]{1,0:T(8,128)(2,1)S(1)} %collective-permute-done.2.refs_2_), channel_id=1, source_target_pairs={{0,32},{32,64},{64,96},{96,128},{128,160},{160,192},{192,224},{224... | collective-permute-start | bytes 884744 | tf_op jit(solution)/shard_map/ppermute | solution.py:171
  24.7 1.3 %copy-start = (bf16[128,4608]{1,0:T(8,128)(2,1)S(1)}, bf16[128,4608]{1,0:T(8,128)(2,1)}, u32[]{:S(2)}) copy-start(bf16[128,4608]{1,0:T(8,128)(2,1)} %g_ref.3) | copy-start | bytes 3538948
  26.0 1.0 copy-start.2
  26.9 19.9 %copy-start.1 = (bf16[128,4608]{1,0:T(8,128)(2,1)S(1)}, bf16[128,4608]{1,0:T(8,128)(2,1)}, u32[]{:S(2)}) copy-start(bf16[128,4608]{1,0:T(8,128)(2,1)} %g_ref.3) | copy-start | bytes 3538948
  27.7 11.5 %collective-permute-start.12 = (bf16[128,1152]{1,0:T(8,128)(2,1)S(1)}, bf16[128,1152]{1,0:T(8,128)(2,1)S(1)}, u32[]{:S(2)}, u32[]{:S(2)}) collective-permute-start(bf16[128,1152]{1,0:T(8,128)(2,1)S(1)} %collective-permute-done.11.refs_3_), channel_id=1, source_target_pairs={{0,32},{32,64},{64,96},{96,128},{128,160},{160,192},{192,224},{224... | collective-permute-start | bytes 884744 | tf_op jit(solution)/shard_map/ppermute | solution.py:169
  29.6 14.1 %collective-permute-start.4 = (bf16[128,1152]{1,0:T(8,128)(2,1)S(1)}, bf16[128,1152]{1,0:T(8,128)(2,1)S(1)}, u32[]{:S(2)}, u32[]{:S(2)}) collective-permute-start(bf16[128,1152]{1,0:T(8,128)(2,1)S(1)} %collective-permute-done.3.refs_4_), channel_id=1, source_target_pairs={{0,32},{32,64},{64,96},{96,128},{128,160},{160,192},{192,224},{224... | collective-permute-start | bytes 884744 | tf_op jit(solution)/shard_map/ppermute | solution.py:171
  33.4 17.5 %all-to-all-start = ((f32[16,8,128]{2,1,0:T(8,128)}), f32[16,8,128]{2,1,0:T(8,128)S(1)}, u32[]{:S(2)}, u32[]{:S(2)}) async-start(f32[16,8,128]{2,1,0:T(8,128)} %broadcast_in_dim.16), calls=%async_computation | async-start | bytes 131072 | tf_op jit(solution)/shard_map/all_to_all | solution.py:184
  39.2 32.5 %collective-permute-start.13 = (bf16[128,1152]{1,0:T(8,128)(2,1)S(1)}, bf16[128,1152]{1,0:T(8,128)(2,1)S(1)}, u32[]{:S(2)}, u32[]{:S(2)}) collective-permute-start(bf16[128,1152]{1,0:T(8,128)(2,1)S(1)} %collective-permute-done.12.refs_5_), channel_id=1, source_target_pairs={{0,32},{32,64},{64,96},{96,128},{128,160},{160,192},{192,224},{224... | collective-permute-start | bytes 884744 | tf_op jit(solution)/shard_map/ppermute | solution.py:169
  43.7 32.0 %collective-permute-start.5 = (bf16[128,1152]{1,0:T(8,128)(2,1)S(1)}, bf16[128,1152]{1,0:T(8,128)(2,1)}, u32[]{:S(2)}, u32[]{:S(2)}) collective-permute-start(bf16[128,1152]{1,0:T(8,128)(2,1)S(1)} %collective-permute-done.4.refs_6_), channel_id=1, source_target_pairs={{0,32},{32,64},{64,96},{96,128},{128,160},{160,192},{192,224},{224... | collective-permute-start | bytes 884744 | tf_op jit(solution)/shard_map/ppermute | solution.py:171
  46.9 10.2 %collective-permute-start.1 = (bf16[288,128]{1,0:T(8,128)(2,1)S(1)}, bf16[288,128]{1,0:T(8,128)(2,1)S(1)}, u32[]{:S(2)}, u32[]{:S(2)}) collective-permute-start(bf16[288,128]{1,0:T(8,128)(2,1)S(1)} %pack.1), channel_id=1, source_target_pairs={{0,0},{1,33},{2,66},{3,99},{4,132},{5,165},{6,198},{7,231},{8,264}... | collective-permute-start | bytes 221192 | tf_op jit(solution)/shard_map/ppermute | solution.py:178
  50.9 7.1 %collective-permute-start = (f32[16,8,128]{2,1,0:T(8,128)S(1)}, f32[16,8,128]{2,1,0:T(8,128)S(1)}, u32[]{:S(2)}, u32[]{:S(2)}) collective-permute-start(f32[16,8,128]{2,1,0:T(8,128)S(1)} %all-to-all-done.own_ref), channel_id=1, source_target_pairs={{0,16},{16,0},{1,17},{17,1},{2,18},{18,2},{3,19},{19,3},{4,20},{20... | collective-permute-start | bytes 196616 | tf_op jit(solution)/shard_map/ppermute | solution.py:185
  59.3 46.1 %all-to-all-start.1 = ((bf16[16,304,128]{2,1,0:T(8,128)(2,1)}), bf16[16,304,128]{2,1,0:T(8,128)(2,1)S(1)}, u32[]{:S(2)}, u32[]{:S(2)}) async-start(bf16[16,304,128]{2,1,0:T(8,128)(2,1)} %bundle.1), calls=%async_computation.1 | async-start | bytes 2490368 | tf_op jit(solution)/shard_map/all_to_all | solution.py:188
  71.6 34.6 %copy-start.3 = (bf16[128,1152]{1,0:T(8,128)(2,1)S(1)}, bf16[128,1152]{1,0:T(8,128)(2,1)}, u32[]{:S(2)}) copy-start(bf16[128,1152]{1,0:T(8,128)(2,1)} %refs_1_.1) | copy-start | bytes 884740
  71.6 7.9 %collective-permute-start.14 = (bf16[128,1152]{1,0:T(8,128)(2,1)S(1)}, bf16[128,1152]{1,0:T(8,128)(2,1)S(1)}, u32[]{:S(2)}, u32[]{:S(2)}) collective-permute-start(bf16[128,1152]{1,0:T(8,128)(2,1)S(1)} %collective-permute-done.13.refs_7_), channel_id=1, source_target_pairs={{0,32},{32,64},{64,96},{96,128},{128,160},{160,192},{192,224},{224... | collective-permute-start | bytes 884744 | tf_op jit(solution)/shard_map/ppermute | solution.py:169
  75.7 9.7 %collective-permute-start.6 = (bf16[128,1152]{1,0:T(8,128)(2,1)}, bf16[128,1152]{1,0:T(8,128)(2,1)S(1)}, u32[]{:S(2)}, u32[]{:S(2)}) collective-permute-start(bf16[128,1152]{1,0:T(8,128)(2,1)} %collective-permute-done.5.refs_8_), channel_id=1, source_target_pairs={{0,32},{32,64},{64,96},{96,128},{128,160},{160,192},{192,224},{224... | collective-permute-start | bytes 884744 | tf_op jit(solution)/shard_map/ppermute | solution.py:171
  79.5 9.0 %collective-permute-start.15 = (bf16[128,1152]{1,0:T(8,128)(2,1)S(1)}, bf16[128,1152]{1,0:T(8,128)(2,1)S(1)}, u32[]{:S(2)}, u32[]{:S(2)}) collective-permute-start(bf16[128,1152]{1,0:T(8,128)(2,1)S(1)} %collective-permute-done.14.refs_9_), channel_id=1, source_target_pairs={{0,32},{32,64},{64,96},{96,128},{128,160},{160,192},{192,224},{224... | collective-permute-start | bytes 884744 | tf_op jit(solution)/shard_map/ppermute | solution.py:169
  84.7 0.7 copy-start.4
  85.4 8.7 %collective-permute-start.7 = (bf16[128,1152]{1,0:T(8,128)(2,1)S(1)}, bf16[128,1152]{1,0:T(8,128)(2,1)S(1)}, u32[]{:S(2)}, u32[]{:S(2)}) collective-permute-start(bf16[128,1152]{1,0:T(8,128)(2,1)S(1)} %collective-permute-done.6.refs_10_), channel_id=1, source_target_pairs={{0,32},{32,64},{64,96},{96,128},{128,160},{160,192},{192,224},{224... | collective-permute-start | bytes 884744 | tf_op jit(solution)/shard_map/ppermute | solution.py:171
  87.8 0.7 copy-start.6
  88.5 8.7 %collective-permute-start.16 = (bf16[128,1152]{1,0:T(8,128)(2,1)S(1)}, bf16[128,1152]{1,0:T(8,128)(2,1)}, u32[]{:S(2)}, u32[]{:S(2)}) collective-permute-start(bf16[128,1152]{1,0:T(8,128)(2,1)S(1)} %collective-permute-done.15.refs_11_), channel_id=1, source_target_pairs={{0,32},{32,64},{64,96},{96,128},{128,160},{160,192},{192,224},{224... | collective-permute-start | bytes 884744 | tf_op jit(solution)/shard_map/ppermute | solution.py:169
  93.3 0.7 copy-start.8
  94.1 8.0 %collective-permute-start.8 = (bf16[128,1152]{1,0:T(8,128)(2,1)S(1)}, bf16[128,1152]{1,0:T(8,128)(2,1)}, u32[]{:S(2)}, u32[]{:S(2)}) collective-permute-start(bf16[128,1152]{1,0:T(8,128)(2,1)S(1)} %collective-permute-done.7.refs_1_), channel_id=1, source_target_pairs={{0,32},{32,64},{64,96},{96,128},{128,160},{160,192},{192,224},{224... | collective-permute-start | bytes 884744 | tf_op jit(solution)/shard_map/ppermute | solution.py:171
  96.5 0.7 copy-start.10
  97.2 11.6 %collective-permute-start.17 = (bf16[128,1152]{1,0:T(8,128)(2,1)}, bf16[128,1152]{1,0:T(8,128)(2,1)}, u32[]{:S(2)}, u32[]{:S(2)}) collective-permute-start(bf16[128,1152]{1,0:T(8,128)(2,1)} %collective-permute-done.16.refs_2_), channel_id=1, source_target_pairs={{0,32},{32,64},{64,96},{96,128},{128,160},{160,192},{192,224},{224... | collective-permute-start | bytes 884744 | tf_op jit(solution)/shard_map/ppermute | solution.py:169
  102.1 8.4 %collective-permute-start.9 = (bf16[128,1152]{1,0:T(8,128)(2,1)}, bf16[128,1152]{1,0:T(8,128)(2,1)}, u32[]{:S(2)}, u32[]{:S(2)}) collective-permute-start(bf16[128,1152]{1,0:T(8,128)(2,1)} %collective-permute-done.8.refs_3_), channel_id=1, source_target_pairs={{0,32},{32,64},{64,96},{96,128},{128,160},{160,192},{192,224},{224... | collective-permute-start | bytes 884744 | tf_op jit(solution)/shard_map/ppermute | solution.py:171
  105.4 1.0 copy-start.5
  105.4 1.1 copy-start.7
  105.4 1.1 copy-start.9
  106.5 2.3 %copy-start.11 = (bf16[128,1152]{1,0:T(8,128)(2,1)S(1)}, bf16[128,1152]{1,0:T(8,128)(2,1)}, u32[]{:S(2)}) copy-start(bf16[128,1152]{1,0:T(8,128)(2,1)} %copy-done.10) | copy-start | bytes 884740
  111.8 11.2 %collective-permute-start.18 = (f32[144,1152]{1,0:T(8,128)S(1)}, f32[144,1152]{1,0:T(8,128)S(1)}, u32[]{:S(2)}, u32[]{:S(2)}) collective-permute-start(f32[144,1152]{1,0:T(8,128)S(1)} %get-tuple-element.8), channel_id=1, source_target_pairs={{0,16},{16,0},{1,17},{17,1},{2,18},{18,2},{3,19},{19,3},{4,20},{20... | collective-permute-start | bytes 1990664 | tf_op jit(solution)/shard_map/ppermute | solution.py:197

commit v2 on v0

v2 whole, which is shorter than its diff:
```python
import math

import jax
import jax.numpy as jnp
from jax import lax
from jax.experimental import pallas as pl
from jax.experimental.pallas import tpu as pltpu
from jax.sharding import Mesh, PartitionSpec as P

D = 4608
UNITS = 18432
SEQ = 128
NZ, NC, NY, NX = 16, 2, 4, 4
NT = NY * NX
CHIP = D // NZ
OWN = CHIP // NC
HOPS = NZ // 2

LINE = ("z", "core")
PLANE = ("y", "x")
ALL = ("z", "core", "y", "x")
SWAP = [(0, 1), (1, 0)]


def spread_pairs():
    pairs = []
    for z in range(NZ):
        for c in range(NC):
            for t in range(NT):
                to = (z + t if c == 0 else z - t) % NZ
                pairs.append(((z * NC + c) * NT + t, (to * NC + c) * NT + t))
    return pairs


def vmem():
    return pl.BlockSpec(memory_space=pltpu.VMEM)


def smem():
    return pl.BlockSpec(memory_space=pltpu.SMEM)


def call(kernel, outs, ins, name, flops, scratch=(), far=False):
    moved = sum(math.prod(a.shape) * a.dtype.itemsize for a in list(ins) + list(outs))
    return pl.pallas_call(
        kernel,
        out_shape=outs,
        in_specs=[smem() if a.dtype == jnp.int32 else pl.BlockSpec(memory_space=pl.ANY) if far else vmem() for a in ins],
        out_specs=[vmem() for _ in outs],
        scratch_shapes=list(scratch),
        compiler_params=pltpu.CompilerParams(vmem_limit_bytes=16 * 1024 * 1024),
        cost_estimate=pl.CostEstimate(flops=flops, bytes_accessed=moved, transcendentals=0),
        name=name,
    )(*ins)


def gram_kernel(to_ref, h_hbm, g_hbm, part_ref, turned_ref, h_ref, g_ref, turned, h_sem, g_sem):
    h_copy = pltpu.make_async_copy(h_hbm, h_ref, h_sem)
    g_copy = pltpu.make_async_copy(g_hbm, g_ref, g_sem)
    h_copy.start()
    g_copy.start()
    dims = (((1,), (1,)), ((), ()))
    h_copy.wait()
    gram_h = lax.dot_general(h_ref[...], h_ref[...], dims, preferred_element_type=jnp.float32)
    g_copy.wait()
    gram_g = lax.dot_general(g_ref[...], g_ref[...], dims, preferred_element_type=jnp.float32)
    part_ref[...] = jnp.full(part_ref.shape, jnp.sum(gram_h * gram_g), jnp.float32)
    start = to_ref[0] * CHIP
    base = pl.multiple_of(start // 128 * 128, 128)
    turned[...] = g_ref[:, pl.ds(base, 384)].astype(jnp.float32).T
    turned_ref[...] = turned[pl.ds(pl.multiple_of(start - base, 32), CHIP), :]


def clip_kernel(live_ref, parts_ref, turned_ref, block_ref, norm_ref):
    total = jnp.sum(parts_ref[...], axis=0)[0:1, :]
    q = total / (float(SEQ) * float(UNITS) * float(D))
    live = live_ref[0].astype(jnp.float32)
    clip = live * jnp.minimum(1.0, 1.0 / jnp.sqrt(q + 1e-06))
    norm_ref[...] = jnp.broadcast_to(jnp.sqrt(q), norm_ref.shape)
    block_ref[...] = (turned_ref[...] * clip).astype(jnp.bfloat16)


def spread_kernel(block_ref, out_ref):
    block = block_ref[...]
    for t in range(NT):
        out_ref[t] = block


def product_kernel(at_ref, s_ref, h_ref, mine_ref, theirs_ref, total_ref):
    z, core = at_ref[0], at_ref[1]
    sign = 1 - 2 * core
    step = pl.program_id(0)

    def columns(of):
        return s_ref[lax.rem(sign * (z - of) + NZ, NZ)]

    left = jnp.concatenate([columns(2 * step), columns(2 * step + 1)], axis=1)
    right = h_ref[...].reshape(2 * SEQ, h_ref.shape[2])
    term = jnp.dot(left, right, preferred_element_type=jnp.float32)

    @pl.when(step == 0)
    def _():
        total_ref[...] = term

    @pl.when(step > 0)
    def _():
        total_ref[...] += term

    @pl.when(step == NZ // 2 - 1)
    def _():
        mine_ref[...] = total_ref[pl.ds(pl.multiple_of(core * OWN, 8), OWN), :]
        theirs_ref[...] = total_ref[pl.ds(pl.multiple_of((1 - core) * OWN, 8), OWN), :]


def products(at, s, gathered):
    units = gathered.shape[2]
    half = jax.ShapeDtypeStruct((OWN, units), jnp.float32)
    return pl.pallas_call(
        product_kernel,
        out_shape=[half, half],
        grid=(NZ // 2,),
        in_specs=[smem(), vmem(), pl.BlockSpec((2, SEQ, units), lambda i: (i, 0, 0))],
        out_specs=[vmem(), vmem()],
        scratch_shapes=[pltpu.VMEM((CHIP, units), jnp.float32)],
        compiler_params=pltpu.CompilerParams(vmem_limit_bytes=16 * 1024 * 1024),
        cost_estimate=pl.CostEstimate(
            flops=2 * CHIP * units * NZ * SEQ,
            bytes_accessed=gathered.size * 2 + s.size * 2 + 8 * OWN * units,
            transcendentals=0,
        ),
        name="products",
    )(at, s, gathered)


def per_device(hidden, out_grad, live):
    z, core = lax.axis_index("z"), lax.axis_index("core")
    t = lax.axis_index(PLANE)
    units = hidden.shape[1]
    gathered = lax.all_gather(hidden, "z", axis=0, tiled=False)

    to = lax.rem(z + (1 - 2 * core) * t + NZ, NZ).astype(jnp.int32).reshape(1)
    part, turned = call(
        gram_kernel,
        [jax.ShapeDtypeStruct((NT, 8, 128), jnp.float32), jax.ShapeDtypeStruct((CHIP, SEQ), jnp.float32)],
        [to, hidden, out_grad], "grams", 2 * SEQ * SEQ * (units + D),
        scratch=[pltpu.VMEM(hidden.shape, hidden.dtype), pltpu.VMEM(out_grad.shape, out_grad.dtype),
                 pltpu.VMEM((384, SEQ), jnp.float32), pltpu.SemaphoreType.DMA, pltpu.SemaphoreType.DMA],
        far=True,
    )
    parts = lax.all_to_all(part, PLANE, 0, 0, tiled=False)
    block, norm = call(
        clip_kernel,
        [jax.ShapeDtypeStruct((CHIP, SEQ), jnp.bfloat16), jax.ShapeDtypeStruct((8, 128), jnp.float32)],
        [live, parts, turned], "clip", 0,
    )
    block = lax.ppermute(block, ALL, spread_pairs())
    [spread] = call(spread_kernel, [jax.ShapeDtypeStruct((NT, CHIP, SEQ), jnp.bfloat16)], [block], "spread", 0)
    s = lax.all_to_all(spread, PLANE, 0, 0, tiled=False)

    mine, theirs = products(jnp.stack([z, core]).astype(jnp.int32), s, gathered)
    total = mine + lax.ppermute(theirs, "core", SWAP)
    grad = (total / math.sqrt(NZ * NC * SEQ)).T
    return grad, norm[0, 0:1]


def solution(mesh):
    grid = Mesh(mesh.devices.reshape(NZ, NC, NY, NX), ALL)
    return jax.shard_map(
        per_device,
        mesh=grid,
        in_specs=(P(LINE, PLANE), P(LINE, None), P(LINE)),
        out_specs=(P(PLANE, LINE), P(LINE)),
        check_vma=False,
    )
```

time: 158 us -> 119 us (0.75)
  the two profiles are of different devices: /device:TPU:1 before, /device:TPU:19 now
where the time goes in v2:
time: 119 us; the launch traced here: 118 us
  waiting for transfers between devices  51.8 us (44%)
  starting transfers between devices  37.8 us (32%)
  between operations  14.7 us (12%)
  Pallas kernels  7.84 us (7%)
  local copies, waits for them, and re-layouts  5.07 us (4%)
    all_gather x1, waiting for transfers between devices, per_device(): gathered = lax.all_gather(hidden, 'z', axis=0, tiled=False)  29.1 us
    all_to_all x1, waiting for transfers between devices, per_device(): s = lax.all_to_all(spread, PLANE, 0, 0, tiled=False)  13.7 us
    ppermute x1, starting transfers between devices, per_device(): block = lax.ppermute(block, ALL, spread_pairs())  12.9 us
    all_to_all x1, starting transfers between devices, per_device(): s = lax.all_to_all(spread, PLANE, 0, 0, tiled=False)  9.17 us
    ppermute x1, starting transfers between devices, per_device(): total = mine + lax.ppermute(theirs, 'core', SWAP)  9.02 us
    all_to_all x1, starting transfers between devices, per_device(): parts = lax.all_to_all(part, PLANE, 0, 0, tiled=False)  6.7 us
    pallas_call x1, Pallas kernels, products(): pl.pallas_call(product_kernel, out_shape=[half, half], grid=(NZ // 2,), i...  4.67 us
    unnamed x6, local copies, waits for them, and re-layouts  4.56 us
  transfers between devices with their start and end apart: 5, of which 5 were waited for; matrix products, arithmetic and copies ran while one was open for 0% of the time, Pallas kernels for 3%

profile of v2, /device:TPU:19, one launch (start us, length us, event | category | flops | bytes accessed | tf_op | source)
XLA Modules:
  0.0 118.2 jit_solution(18173569158319190307)
XLA Ops:
  7.2 0.0 all-gather.3.cloned.1.call-start
  7.2 0.7 all-gather.3.cloned.1.call-update
  7.9 0.0 copy-start.1
  7.9 1.3 %copy-done.1 = bf16[128,4608]{1,0:T(8,128)(2,1)S(1)} copy-done((bf16[128,4608]{1,0:T(8,128)(2,1)S(1)}, bf16[128,4608]{1,0:T(8,128)(2,1)}, u32[]{:S(2)}) %copy-start.1) | copy-done | bytes 1179672
  9.2 0.0 copy-start.2
  9.2 1.0 copy-done.2
  10.1 1.9 %grams.1 = (f32[16,8,128]{2,1,0:T(8,128)}, f32[288,128]{1,0:T(8,128)S(1)}) custom-call(s32[1]{0:T(128)} %bitcast.2.to_ref, bf16[128,1152]{1,0:T(8,128)(2,1)S(1)} %copy-done.2, bf16[128,4608]{1,0:T(8,128)(2,1)S(1)} %copy-done.1), custom_call_target="tpu_custom_call" | custom-call | flops 188743680 | bytes 1687556 | tf_op jit(solution)/shard_map/grams/pallas_call | solution.py:45
  12.1 6.7 %all-to-all-start = ((f32[16,8,128]{2,1,0:T(8,128)}), f32[16,8,128]{2,1,0:T(8,128)S(1)}, u32[]{:S(2)}, u32[]{:S(2)}) async-start(f32[16,8,128]{2,1,0:T(8,128)} %get-tuple-element.8), calls=%async_computation | async-start | bytes 131072 | tf_op jit(solution)/shard_map/all_to_all | solution.py:150
  19.4 3.0 %all-to-all-done.parts_ref = f32[16,8,128]{2,1,0:T(8,128)S(1)} async-done(((f32[16,8,128]{2,1,0:T(8,128)}), f32[16,8,128]{2,1,0:T(8,128)S(1)}, u32[]{:S(2)}, u32[]{:S(2)}) %all-to-all-start) | async-done | bytes 65568 | tf_op jit(solution)/shard_map/all_to_all | solution.py:150
  22.5 12.9 %collective-permute-start = (bf16[288,128]{1,0:T(8,128)(2,1)S(1)}, bf16[288,128]{1,0:T(8,128)(2,1)S(1)}, u32[]{:S(2)}, u32[]{:S(2)}) collective-permute-start(bf16[288,128]{1,0:T(8,128)(2,1)S(1)} %get-tuple-element.10), channel_id=1, source_target_pairs={{0,0},{1,33},{2,66},{3,99},{4,132},{5,165},{6,198},{7,231},{8,264}... | collective-permute-start | bytes 221192 | tf_op jit(solution)/shard_map/ppermute | solution.py:156
  35.4 4.2 %collective-permute-done.block_ref = bf16[288,128]{1,0:T(8,128)(2,1)S(1)} collective-permute-done((bf16[288,128]{1,0:T(8,128)(2,1)S(1)}, bf16[288,128]{1,0:T(8,128)(2,1)S(1)}, u32[]{:S(2)}, u32[]{:S(2)}) %collective-permute-start) | collective-permute-done | bytes 73760 | tf_op jit(solution)/shard_map/ppermute | solution.py:156
  39.5 1.2 %spread.1 = bf16[16,288,128]{2,1,0:T(8,128)(2,1)} custom-call(bf16[288,128]{1,0:T(8,128)(2,1)S(1)} %collective-permute-done.block_ref), custom_call_target="tpu_custom_call" | custom-call | bytes 1253376 | tf_op jit(solution)/shard_map/spread/pallas_call | solution.py:45
  40.7 9.2 %all-to-all-start.1 = ((bf16[16,288,128]{2,1,0:T(8,128)(2,1)}), bf16[16,288,128]{2,1,0:T(8,128)(2,1)S(1)}, u32[]{:S(2)}, u32[]{:S(2)}) async-start(bf16[16,288,128]{2,1,0:T(8,128)(2,1)} %spread.1), calls=%async_computation.1 | async-start | bytes 2359296 | tf_op jit(solution)/shard_map/all_to_all | solution.py:158
  49.9 0.1 pad_add_fusion.at_ref
  50.0 13.7 %all-to-all-done.1.s_ref = bf16[16,288,128]{2,1,0:T(8,128)(2,1)S(1)} async-done(((bf16[16,288,128]{2,1,0:T(8,128)(2,1)}), bf16[16,288,128]{2,1,0:T(8,128)(2,1)S(1)}, u32[]{:S(2)}, u32[]{:S(2)}) %all-to-all-start.1) | async-done | bytes 1179680 | tf_op jit(solution)/shard_map/all_to_all | solution.py:158
  63.6 29.1 %all-gather.3.cloned.1.call-done = bf16[2048,1152]{1,0:T(8,128)(2,1)} async-done(((bf16[128,1152]{1,0:T(8,128)(2,1)}), bf16[2048,1152]{1,0:T(8,128)(2,1)}) %all-gather.3.cloned.1.call-update) | async-done | bytes 4718608 | tf_op jit(solution)/shard_map/all_gather | solution.py:139
  92.7 0.0 copy-start
  92.7 2.3 %copy-done = bf16[2048,1152]{1,0:T(8,128)(2,1)S(1)} copy-done((bf16[2048,1152]{1,0:T(8,128)(2,1)S(1)}, bf16[2048,1152]{1,0:T(8,128)(2,1)}, u32[]{:S(2)}) %copy-start) | copy-done | bytes 4718616
  95.0 4.7 %products.1 = (f32[144,1152]{1,0:T(8,128)S(1)}, f32[144,1152]{1,0:T(8,128)S(1)}) custom-call(s32[2]{0:T(128)S(1)} %pad_add_fusion.at_ref, bf16[16,288,128]{2,1,0:T(8,128)(2,1)S(1)} %all-to-all-done.1.s_ref, bf16[16,128,1152]{2,1,0:T(8,128)(2,1)S(1)} %bitcast.7), custom_call_target="tpu_custom_call" | custom-call | flops 1358954496 | bytes 7225344 | tf_op jit(solution)/shard_map/products/pallas_call | solution.py:118
  99.7 9.0 %collective-permute-start.1 = (f32[144,1152]{1,0:T(8,128)S(1)}, f32[144,1152]{1,0:T(8,128)S(1)}, u32[]{:S(2)}, u32[]{:S(2)}) collective-permute-start(f32[144,1152]{1,0:T(8,128)S(1)} %get-tuple-element.12), channel_id=1, source_target_pairs={{0,16},{16,0},{1,17},{17,1},{2,18},{18,2},{3,19},{19,3},{4,20},{20... | collective-permute-start | bytes 1990664 | tf_op jit(solution)/shard_map/ppermute | solution.py:161
  108.8 0.5 slice.3
  109.3 1.2 %collective-permute-done.1 = f32[144,1152]{1,0:T(8,128)S(1)} collective-permute-done((f32[144,1152]{1,0:T(8,128)S(1)}, f32[144,1152]{1,0:T(8,128)S(1)}, u32[]{:S(2)}, u32[]{:S(2)}) %collective-permute-start.1) | collective-permute-done | bytes 663584 | tf_op jit(solution)/shard_map/ppermute | solution.py:161
  110.5 0.9 multiply_bitcast_fusion
  (1 shorter events, 0.0 us)
Async XLA Ops:
  7.2 85.5 %all-gather.3.cloned.1.call-start = ((), (), s32[]{:S(2)}) async-start(), calls=%async_computation.2 | async-start | bytes 5013504 | tf_op jit(solution)/shard_map/all_gather | solution.py:139
  7.9 1.3 %copy-start.1 = (bf16[128,4608]{1,0:T(8,128)(2,1)S(1)}, bf16[128,4608]{1,0:T(8,128)(2,1)}, u32[]{:S(2)}) copy-start(bf16[128,4608]{1,0:T(8,128)(2,1)} %g_hbm.1) | copy-start | bytes 3538948
  9.2 1.0 copy-start.2
  12.1 10.3 %all-to-all-start = ((f32[16,8,128]{2,1,0:T(8,128)}), f32[16,8,128]{2,1,0:T(8,128)S(1)}, u32[]{:S(2)}, u32[]{:S(2)}) async-start(f32[16,8,128]{2,1,0:T(8,128)} %get-tuple-element.8), calls=%async_computation | async-start | bytes 131072 | tf_op jit(solution)/shard_map/all_to_all | solution.py:150
  22.5 17.0 %collective-permute-start = (bf16[288,128]{1,0:T(8,128)(2,1)S(1)}, bf16[288,128]{1,0:T(8,128)(2,1)S(1)}, u32[]{:S(2)}, u32[]{:S(2)}) collective-permute-start(bf16[288,128]{1,0:T(8,128)(2,1)S(1)} %get-tuple-element.10), channel_id=1, source_target_pairs={{0,0},{1,33},{2,66},{3,99},{4,132},{5,165},{6,198},{7,231},{8,264}... | collective-permute-start | bytes 221192 | tf_op jit(solution)/shard_map/ppermute | solution.py:156
  40.7 22.9 %all-to-all-start.1 = ((bf16[16,288,128]{2,1,0:T(8,128)(2,1)}), bf16[16,288,128]{2,1,0:T(8,128)(2,1)S(1)}, u32[]{:S(2)}, u32[]{:S(2)}) async-start(bf16[16,288,128]{2,1,0:T(8,128)(2,1)} %spread.1), calls=%async_computation.1 | async-start | bytes 2359296 | tf_op jit(solution)/shard_map/all_to_all | solution.py:158
  92.7 2.3 %copy-start = (bf16[2048,1152]{1,0:T(8,128)(2,1)S(1)}, bf16[2048,1152]{1,0:T(8,128)(2,1)}, u32[]{:S(2)}) copy-start(bf16[2048,1152]{1,0:T(8,128)(2,1)} %all-gather.3.cloned.1.call-done) | copy-start | bytes 14155780
  99.7 10.7 %collective-permute-start.1 = (f32[144,1152]{1,0:T(8,128)S(1)}, f32[144,1152]{1,0:T(8,128)S(1)}, u32[]{:S(2)}, u32[]{:S(2)}) collective-permute-start(f32[144,1152]{1,0:T(8,128)S(1)} %get-tuple-element.12), channel_id=1, source_target_pairs={{0,16},{16,0},{1,17},{17,1},{2,18},{18,2},{3,19},{19,3},{4,20},{20... | collective-permute-start | bytes 1990664 | tf_op jit(solution)/shard_map/ppermute | solution.py:161
Sparse Core Ops, SparseCore 0:
  10.1 82.5 all-gather.2

commit v3 on v2

v3 whole, which is shorter than its diff:
```python
import math

import jax
import jax.numpy as jnp
from jax import lax
from jax.experimental import pallas as pl
from jax.experimental.pallas import tpu as pltpu
from jax.sharding import Mesh, PartitionSpec as P

D = 4608
UNITS = 18432
SEQ = 128
NZ, NC, NY, NX = 16, 2, 4, 4
NT = NY * NX
CHIP = D // NZ
OWN = CHIP // NC
HOPS = NZ // 2

LINE = ("z", "core")
PLANE = ("y", "x")
ALL = ("z", "core", "y", "x")
STEP = [(z * 2, (z + 1) % NZ * 2) for z in range(NZ)]
STEP += [(z * 2 + 1, (z - 1) % NZ * 2 + 1) for z in range(NZ)]
SWAP = [(0, 1), (1, 0)]


def spread_pairs():
    pairs = []
    for z in range(NZ):
        for c in range(NC):
            for t in range(NT):
                to_z = (z + t if c == 0 else z - t) % NZ
                to_c = c if t <= HOPS else 1 - c
                pairs.append(((z * NC + c) * NT + t, (to_z * NC + to_c) * NT + t))
    return pairs


def vmem():
    return pl.BlockSpec(memory_space=pltpu.VMEM)


def smem():
    return pl.BlockSpec(memory_space=pltpu.SMEM)


def call(kernel, outs, ins, name, flops, scratch=(), far=False, tokens=()):
    moved = sum(math.prod(a.shape) * a.dtype.itemsize for a in list(ins) + list(outs))
    if tokens:
        inner, n = kernel, len(ins)

        def kernel(*refs):
            inner(*refs[:n], *refs[n + len(tokens):])

    return pl.pallas_call(
        kernel,
        out_shape=outs,
        in_specs=[smem() if a.dtype == jnp.int32 else pl.BlockSpec(memory_space=pl.ANY) if far else vmem() for a in ins]
        + [pl.BlockSpec(memory_space=pl.ANY) for _ in tokens],
        out_specs=[vmem() for _ in outs],
        scratch_shapes=list(scratch),
        compiler_params=pltpu.CompilerParams(vmem_limit_bytes=16 * 1024 * 1024),
        cost_estimate=pl.CostEstimate(flops=flops, bytes_accessed=moved, transcendentals=0),
        name=name,
    )(*ins, *tokens)


def after(x, *others, cost=0):
    def kernel(*refs):
        del refs

    return pl.pallas_call(
        kernel,
        out_shape=jax.ShapeDtypeStruct(x.shape, x.dtype),
        in_specs=[pl.BlockSpec(memory_space=pl.ANY)] * (1 + len(others)),
        out_specs=pl.BlockSpec(memory_space=pl.ANY),
        input_output_aliases={0: 0},
        compiler_params=pltpu.CompilerParams(vmem_limit_bytes=1024 * 1024),
        cost_estimate=pl.CostEstimate(flops=cost, bytes_accessed=0, transcendentals=0),
        name="after",
    )(x, *others)


def gram_kernel(to_ref, h_hbm, g_hbm, part_ref, turned_ref, h_ref, g_ref, turned, h_sem, g_sem):
    h_copy = pltpu.make_async_copy(h_hbm, h_ref, h_sem)
    g_copy = pltpu.make_async_copy(g_hbm, g_ref, g_sem)
    h_copy.start()
    g_copy.start()
    dims = (((1,), (1,)), ((), ()))
    h_copy.wait()
    gram_h = lax.dot_general(h_ref[...], h_ref[...], dims, preferred_element_type=jnp.float32)
    g_copy.wait()
    gram_g = lax.dot_general(g_ref[...], g_ref[...], dims, preferred_element_type=jnp.float32)
    part_ref[...] = jnp.full(part_ref.shape, jnp.sum(gram_h * gram_g), jnp.float32)
    start = to_ref[0] * CHIP
    base = pl.multiple_of(start // 128 * 128, 128)
    turned[...] = g_ref[:, pl.ds(base, 384)].astype(jnp.float32).T
    turned_ref[...] = turned[pl.ds(pl.multiple_of(start - base, 32), CHIP), :]


def clip_kernel(live_ref, parts_ref, turned_ref, block_ref, norm_ref):
    total = jnp.sum(parts_ref[...], axis=0)[0:1, :]
    q = total / (float(SEQ) * float(UNITS) * float(D))
    live = live_ref[0].astype(jnp.float32)
    clip = live * jnp.minimum(1.0, 1.0 / jnp.sqrt(q + 1e-06))
    norm_ref[...] = jnp.broadcast_to(jnp.sqrt(q), norm_ref.shape)
    block_ref[...] = (turned_ref[...] * clip).astype(jnp.bfloat16)


def spread_kernel(block_ref, out_ref):
    block = block_ref[...]
    for t in range(NT):
        out_ref[t] = block


def product(s_ref, hop, p, q):
    if q is None:
        return jnp.dot(s_ref[hop], p[...], preferred_element_type=jnp.float32)
    left = jnp.concatenate([s_ref[hop], s_ref[NZ - hop]], axis=1)
    right = jnp.concatenate([p[...], q[...]], axis=0)
    return jnp.dot(left, right, preferred_element_type=jnp.float32)


def matmul(s, hops, ps, qs, acc, core=None):
    blocks = [b for hop in hops for b in (ps[hop], qs[hop]) if b is not None]
    ins = [s] + blocks + ([acc] if acc is not None else []) + ([core] if core is not None else [])
    units = blocks[0].shape[1]

    def kernel(*refs):
        s_ref, rest = refs[0], list(refs[1:])
        taken = [(hop, rest.pop(0), rest.pop(0) if qs[hop] is not None else None) for hop in hops]
        total = rest.pop(0)[...] if acc is not None else None
        for hop, p, q in taken:
            term = product(s_ref, hop, p, q)
            total = term if total is None else total + term
        if core is None:
            rest[0][...] = total
            return
        core_ref, mine_ref, theirs_ref, total_ref = rest
        total_ref[...] = total
        mine_ref[...] = total_ref[pl.ds(pl.multiple_of(core_ref[0] * OWN, 8), OWN), :]
        theirs_ref[...] = total_ref[pl.ds(pl.multiple_of((1 - core_ref[0]) * OWN, 8), OWN), :]

    whole = jax.ShapeDtypeStruct((CHIP, units), jnp.float32)
    half = jax.ShapeDtypeStruct((OWN, units), jnp.float32)
    flops = 2 * CHIP * units * SEQ * len(blocks)
    if core is None:
        return call(kernel, [whole], ins, "products", flops)
    return call(kernel, [half, half], ins, "products", flops, scratch=[pltpu.VMEM(whole.shape, whole.dtype)])


def per_device(hidden, out_grad, live):
    z, core = lax.axis_index("z"), lax.axis_index("core")
    t = lax.axis_index(PLANE)
    units = hidden.shape[1]

    ps, qs = [hidden], [None]
    own_q = lax.ppermute(hidden, "core", SWAP)

    def advance(hop):
        if hop < HOPS:
            qs.append(lax.ppermute(qs[-1] if hop > 1 else own_q, LINE, STEP))
        else:
            qs.append(None)
        ps.append(lax.ppermute(ps[-1], LINE, STEP))

    advance(1)

    to = lax.rem(z + (1 - 2 * core) * t + NZ, NZ).astype(jnp.int32).reshape(1)
    part, turned = call(
        gram_kernel,
        [jax.ShapeDtypeStruct((NT, 8, 128), jnp.float32), jax.ShapeDtypeStruct((CHIP, SEQ), jnp.float32)],
        [to, hidden, out_grad], "grams", 2 * SEQ * SEQ * (units + D),
        scratch=[pltpu.VMEM(hidden.shape, hidden.dtype), pltpu.VMEM(out_grad.shape, out_grad.dtype),
                 pltpu.VMEM((384, SEQ), jnp.float32), pltpu.SemaphoreType.DMA, pltpu.SemaphoreType.DMA],
        far=True,
    )
    def clipped(parts):
        return call(
            clip_kernel,
            [jax.ShapeDtypeStruct((CHIP, SEQ), jnp.bfloat16), jax.ShapeDtypeStruct((8, 128), jnp.float32)],
            [live, parts, turned], "clip", 10000000000,
        )

    ps[1] = after(ps[1], part)
    advance(2)
    parts = lax.all_to_all(part, PLANE, 0, 0, tiled=False)
    block, norm = clipped(parts)
    advance(3)
    block = lax.ppermute(block, ALL, spread_pairs())
    advance(4)
    advance(5)
    [spread] = call(spread_kernel, [jax.ShapeDtypeStruct((NT, CHIP, SEQ), jnp.bfloat16)], [block], "spread", 10000000000)
    s = lax.all_to_all(spread, PLANE, 0, 0, tiled=False)
    advance(6)
    ps[6] = after(ps[6], cost=1000000000)
    advance(7)
    [acc] = matmul(s, range(0, 6), ps, qs, None)

    advance(8)
    [acc] = matmul(s, range(6, 8), ps, qs, acc)
    mine, theirs = matmul(s, range(8, 9), ps, qs, acc, core.astype(jnp.int32).reshape(1))
    total = mine + lax.ppermute(theirs, "core", SWAP)
    grad = (total / math.sqrt(NZ * NC * SEQ)).T
    return grad, norm[0, 0:1]


def solution(mesh):
    grid = Mesh(mesh.devices.reshape(NZ, NC, NY, NX), ALL)
    return jax.shard_map(
        per_device,
        mesh=grid,
        in_specs=(P(LINE, PLANE), P(LINE, None), P(LINE)),
        out_specs=(P(PLANE, LINE), P(LINE)),
        check_vma=False,
    )
```

time: 119 us -> 111 us (0.933)
  the two profiles are of different devices: /device:TPU:19 before, /device:TPU:1 now
where the time goes in v3:
time: 111 us; the launch traced here: 110 us
  starting transfers between devices  86 us (77%)
  Pallas kernels  8.59 us (8%)
  waiting for transfers between devices  8.39 us (8%)
  local copies, waits for them, and re-layouts  4.42 us (4%)
  between operations  1.67 us (2%)
    ppermute x8, starting transfers between devices, advance(): ps.append(lax.ppermute(ps[-1], LINE, STEP))  32.7 us
    ppermute x7, starting transfers between devices, advance(): qs.append(lax.ppermute(qs[-1] if hop > 1 else own_q, LINE, STEP))  22.9 us
    all_to_all x1, starting transfers between devices, per_device(): s = lax.all_to_all(spread, PLANE, 0, 0, tiled=False)  14.3 us
    pallas_call x6, Pallas kernels, call(): pl.pallas_call(kernel, out_shape=outs, in_specs=[smem() if a.dtype == jnp...  8.58 us
    ppermute x1, starting transfers between devices, per_device(): total = mine + lax.ppermute(theirs, 'core', SWAP)  6.78 us
    all_to_all x1, starting transfers between devices, per_device(): parts = lax.all_to_all(part, PLANE, 0, 0, tiled=False)  6.76 us
    unnamed x14, local copies, waits for them, and re-layouts  3.9 us
    ppermute x7, waiting for transfers between devices, advance(): qs.append(lax.ppermute(qs[-1] if hop > 1 else own_q, LINE, STEP))  3.5 us
  transfers between devices with their start and end apart: 20, of which 6 were waited for; matrix products, arithmetic and copies ran while one was open for 0% of the time, Pallas kernels for 7%

profile of v3, /device:TPU:1, one launch (start us, length us, event | category | flops | bytes accessed | tf_op | source)
XLA Modules:
  0.0 110.0 jit_solution(10217693279033443661)
XLA Ops:
  0.6 12.0 %collective-permute-start.1 = (bf16[128,1152]{1,0:T(8,128)(2,1)}, bf16[128,1152]{1,0:T(8,128)(2,1)S(1)}, u32[]{:S(2)}, u32[]{:S(2)}) collective-permute-start(bf16[128,1152]{1,0:T(8,128)(2,1)} %refs_1_.1), channel_id=1, source_target_pairs={{0,32},{32,64},{64,96},{96,128},{128,160},{160,192},{192,224},{224... | collective-permute-start | bytes 884744 | tf_op jit(solution)/shard_map/ppermute | solution.py:164
  12.6 1.9 %collective-permute-start.9 = (bf16[128,1152]{1,0:T(8,128)(2,1)}, bf16[128,1152]{1,0:T(8,128)(2,1)S(1)}, u32[]{:S(2)}, u32[]{:S(2)}) collective-permute-start(bf16[128,1152]{1,0:T(8,128)(2,1)} %refs_1_.1), channel_id=1, source_target_pairs={{0,16},{16,0},{1,17},{17,1},{2,18},{18,2},{3,19},{19,3},{4,20},{20... | collective-permute-start | bytes 884744 | tf_op jit(solution)/shard_map/ppermute | solution.py:157
  14.5 0.0 copy-start
  14.5 1.0 copy-done
  15.5 1.3 %copy-done.2 = bf16[128,4608]{1,0:T(8,128)(2,1)S(1)} copy-done((bf16[128,4608]{1,0:T(8,128)(2,1)S(1)}, bf16[128,4608]{1,0:T(8,128)(2,1)}, u32[]{:S(2)}) %copy-start.2) | copy-done | bytes 1179672
  16.8 1.9 %grams.1 = (f32[16,8,128]{2,1,0:T(8,128)}, f32[288,128]{1,0:T(8,128)S(1)}) custom-call(s32[1]{0:T(128)} %bitcast.to_ref, bf16[128,1152]{1,0:T(8,128)(2,1)S(1)} %copy-done, bf16[128,4608]{1,0:T(8,128)(2,1)S(1)} %copy-done.2), custom_call_target="tpu_custom_call" | custom-call | flops 188743680 | bytes 1687556 | tf_op jit(solution)/shard_map/grams/pallas_call | solution.py:54
  18.7 0.0 collective-permute-done.1.refs_0_
  18.7 2.7 %collective-permute-start.2 = (bf16[128,1152]{1,0:T(8,128)(2,1)S(1)}, bf16[128,1152]{1,0:T(8,128)(2,1)S(1)}, u32[]{:S(2)}, u32[]{:S(2)}) collective-permute-start(bf16[128,1152]{1,0:T(8,128)(2,1)S(1)} %after.2.refs_2_), channel_id=1, source_target_pairs={{0,32},{32,64},{64,96},{96,128},{128,160},{160,192},{192,224},{224... | collective-permute-start | bytes 884744 | tf_op jit(solution)/shard_map/ppermute | solution.py:164
  21.5 0.0 collective-permute-done.9
  21.5 3.5 %collective-permute-start.10 = (bf16[128,1152]{1,0:T(8,128)(2,1)S(1)}, bf16[128,1152]{1,0:T(8,128)(2,1)S(1)}, u32[]{:S(2)}, u32[]{:S(2)}) collective-permute-start(bf16[128,1152]{1,0:T(8,128)(2,1)S(1)} %collective-permute-done.9), channel_id=1, source_target_pairs={{0,32},{32,64},{64,96},{96,128},{128,160},{160,192},{192,224},{224... | collective-permute-start | bytes 884744 | tf_op jit(solution)/shard_map/ppermute | solution.py:161
  25.0 1.5 %collective-permute-done.2.refs_4_ = bf16[128,1152]{1,0:T(8,128)(2,1)S(1)} collective-permute-done((bf16[128,1152]{1,0:T(8,128)(2,1)S(1)}, bf16[128,1152]{1,0:T(8,128)(2,1)S(1)}, u32[]{:S(2)}, u32[]{:S(2)}) %collective-permute-start.2) | collective-permute-done | bytes 294944 | tf_op jit(solution)/shard_map/ppermute | solution.py:164
  26.5 3.6 %collective-permute-start.3 = (bf16[128,1152]{1,0:T(8,128)(2,1)S(1)}, bf16[128,1152]{1,0:T(8,128)(2,1)S(1)}, u32[]{:S(2)}, u32[]{:S(2)}) collective-permute-start(bf16[128,1152]{1,0:T(8,128)(2,1)S(1)} %collective-permute-done.2.refs_4_), channel_id=1, source_target_pairs={{0,32},{32,64},{64,96},{96,128},{128,160},{160,192},{192,224},{224... | collective-permute-start | bytes 884744 | tf_op jit(solution)/shard_map/ppermute | solution.py:164
  30.1 0.0 collective-permute-done.10.refs_3_
  30.1 3.5 %collective-permute-start.11 = (bf16[128,1152]{1,0:T(8,128)(2,1)S(1)}, bf16[128,1152]{1,0:T(8,128)(2,1)S(1)}, u32[]{:S(2)}, u32[]{:S(2)}) collective-permute-start(bf16[128,1152]{1,0:T(8,128)(2,1)S(1)} %collective-permute-done.10.refs_3_), channel_id=1, source_target_pairs={{0,32},{32,64},{64,96},{96,128},{128,160},{160,192},{192,224},{224... | collective-permute-start | bytes 884744 | tf_op jit(solution)/shard_map/ppermute | solution.py:161
  33.6 6.8 %all-to-all-start = ((f32[16,8,128]{2,1,0:T(8,128)}), f32[16,8,128]{2,1,0:T(8,128)S(1)}, u32[]{:S(2)}, u32[]{:S(2)}) async-start(f32[16,8,128]{2,1,0:T(8,128)} %get-tuple-element.8.refs_1_), calls=%async_computation | async-start | bytes 131072 | tf_op jit(solution)/shard_map/all_to_all | solution.py:186
  41.1 2.2 %collective-permute-start.4 = (bf16[128,1152]{1,0:T(8,128)(2,1)S(1)}, bf16[128,1152]{1,0:T(8,128)(2,1)S(1)}, u32[]{:S(2)}, u32[]{:S(2)}) collective-permute-start(bf16[128,1152]{1,0:T(8,128)(2,1)S(1)} %collective-permute-done.3.refs_6_), channel_id=1, source_target_pairs={{0,32},{32,64},{64,96},{96,128},{128,160},{160,192},{192,224},{224... | collective-permute-start | bytes 884744 | tf_op jit(solution)/shard_map/ppermute | solution.py:164
  43.3 0.0 collective-permute-done.11.refs_5_
  43.3 2.6 %collective-permute-start.12 = (bf16[128,1152]{1,0:T(8,128)(2,1)S(1)}, bf16[128,1152]{1,0:T(8,128)(2,1)S(1)}, u32[]{:S(2)}, u32[]{:S(2)}) collective-permute-start(bf16[128,1152]{1,0:T(8,128)(2,1)S(1)} %collective-permute-done.11.refs_5_), channel_id=1, source_target_pairs={{0,32},{32,64},{64,96},{96,128},{128,160},{160,192},{192,224},{224... | collective-permute-start | bytes 884744 | tf_op jit(solution)/shard_map/ppermute | solution.py:161
  46.0 1.0 all-to-all-done.parts_ref
  47.0 0.7 collective-permute-start
  47.6 1.2 %collective-permute-done.4.refs_8_ = bf16[128,1152]{1,0:T(8,128)(2,1)S(1)} collective-permute-done((bf16[128,1152]{1,0:T(8,128)(2,1)S(1)}, bf16[128,1152]{1,0:T(8,128)(2,1)S(1)}, u32[]{:S(2)}, u32[]{:S(2)}) %collective-permute-start.4) | collective-permute-done | bytes 294944 | tf_op jit(solution)/shard_map/ppermute | solution.py:164
  48.8 3.4 %collective-permute-start.5 = (bf16[128,1152]{1,0:T(8,128)(2,1)S(1)}, bf16[128,1152]{1,0:T(8,128)(2,1)}, u32[]{:S(2)}, u32[]{:S(2)}) collective-permute-start(bf16[128,1152]{1,0:T(8,128)(2,1)S(1)} %collective-permute-done.4.refs_8_), channel_id=1, source_target_pairs={{0,32},{32,64},{64,96},{96,128},{128,160},{160,192},{192,224},{224... | collective-permute-start | bytes 884744 | tf_op jit(solution)/shard_map/ppermute | solution.py:164
  52.3 2.8 %collective-permute-start.13 = (bf16[128,1152]{1,0:T(8,128)(2,1)S(1)}, bf16[128,1152]{1,0:T(8,128)(2,1)}, u32[]{:S(2)}, u32[]{:S(2)}) collective-permute-start(bf16[128,1152]{1,0:T(8,128)(2,1)S(1)} %collective-permute-done.12.refs_7_), channel_id=1, source_target_pairs={{0,32},{32,64},{64,96},{96,128},{128,160},{160,192},{192,224},{224... | collective-permute-start | bytes 884744 | tf_op jit(solution)/shard_map/ppermute | solution.py:161
  55.1 1.2 %spread.1 = bf16[16,288,128]{2,1,0:T(8,128)(2,1)} custom-call(bf16[288,128]{1,0:T(8,128)(2,1)S(1)} %collective-permute-done.block_ref), custom_call_target="tpu_custom_call" | custom-call | flops 10000000000 | bytes 1253376 | tf_op jit(solution)/shard_map/spread/pallas_call | solution.py:54
  56.3 14.3 %all-to-all-start.1 = ((bf16[16,288,128]{2,1,0:T(8,128)(2,1)}), bf16[16,288,128]{2,1,0:T(8,128)(2,1)S(1)}, u32[]{:S(2)}, u32[]{:S(2)}) async-start(bf16[16,288,128]{2,1,0:T(8,128)(2,1)} %spread.1), calls=%async_computation.1 | async-start | bytes 2359296 | tf_op jit(solution)/shard_map/all_to_all | solution.py:193
  70.6 0.0 copy-start.1
  70.6 0.0 collective-permute-done.13.refs_9_
  70.6 2.3 %collective-permute-start.14 = (bf16[128,1152]{1,0:T(8,128)(2,1)}, bf16[128,1152]{1,0:T(8,128)(2,1)S(1)}, u32[]{:S(2)}, u32[]{:S(2)}) collective-permute-start(bf16[128,1152]{1,0:T(8,128)(2,1)} %collective-permute-done.13.refs_9_), channel_id=1, source_target_pairs={{0,32},{32,64},{64,96},{96,128},{128,160},{160,192},{192,224},{224... | collective-permute-start | bytes 884744 | tf_op jit(solution)/shard_map/ppermute | solution.py:161
  72.9 2.6 %collective-permute-start.6 = (bf16[128,1152]{1,0:T(8,128)(2,1)}, bf16[128,1152]{1,0:T(8,128)(2,1)S(1)}, u32[]{:S(2)}, u32[]{:S(2)}) collective-permute-start(bf16[128,1152]{1,0:T(8,128)(2,1)} %collective-permute-done.5.refs_10_), channel_id=1, source_target_pairs={{0,32},{32,64},{64,96},{96,128},{128,160},{160,192},{192,224},{224... | collective-permute-start | bytes 884744 | tf_op jit(solution)/shard_map/ppermute | solution.py:164
  75.5 3.2 %collective-permute-done.14.refs_11_ = bf16[128,1152]{1,0:T(8,128)(2,1)S(1)} collective-permute-done((bf16[128,1152]{1,0:T(8,128)(2,1)}, bf16[128,1152]{1,0:T(8,128)(2,1)S(1)}, u32[]{:S(2)}, u32[]{:S(2)}) %collective-permute-start.14) | collective-permute-done | bytes 294944 | tf_op jit(solution)/shard_map/ppermute | solution.py:161
  78.7 3.4 %collective-permute-start.15 = (bf16[128,1152]{1,0:T(8,128)(2,1)S(1)}, bf16[128,1152]{1,0:T(8,128)(2,1)}, u32[]{:S(2)}, u32[]{:S(2)}) collective-permute-start(bf16[128,1152]{1,0:T(8,128)(2,1)S(1)} %collective-permute-done.14.refs_11_), channel_id=1, source_target_pairs={{0,32},{32,64},{64,96},{96,128},{128,160},{160,192},{192,224},{224... | collective-permute-start | bytes 884744 | tf_op jit(solution)/shard_map/ppermute | solution.py:161
  82.1 3.1 %collective-permute-start.7 = (bf16[128,1152]{1,0:T(8,128)(2,1)S(1)}, bf16[128,1152]{1,0:T(8,128)(2,1)}, u32[]{:S(2)}, u32[]{:S(2)}) collective-permute-start(bf16[128,1152]{1,0:T(8,128)(2,1)S(1)} %after.3.refs_1_), channel_id=1, source_target_pairs={{0,32},{32,64},{64,96},{96,128},{128,160},{160,192},{192,224},{224... | collective-permute-start | bytes 884744 | tf_op jit(solution)/shard_map/ppermute | solution.py:164
  85.3 0.0 copy-start.5
  85.3 0.7 copy-done.5
  86.0 0.3 collective-permute-done.15.refs_2_
  86.3 4.8 %collective-permute-start.16 = (bf16[128,1152]{1,0:T(8,128)(2,1)}, bf16[128,1152]{1,0:T(8,128)(2,1)}, u32[]{:S(2)}, u32[]{:S(2)}) collective-permute-start(bf16[128,1152]{1,0:T(8,128)(2,1)} %collective-permute-done.15.refs_2_), channel_id=1, source_target_pairs={{0,32},{32,64},{64,96},{96,128},{128,160},{160,192},{192,224},{224... | collective-permute-start | bytes 884744 | tf_op jit(solution)/shard_map/ppermute | solution.py:161
  91.1 0.0 collective-permute-done.7.refs_3_
  91.1 3.0 %collective-permute-start.8 = (bf16[128,1152]{1,0:T(8,128)(2,1)}, bf16[128,1152]{1,0:T(8,128)(2,1)}, u32[]{:S(2)}, u32[]{:S(2)}) collective-permute-start(bf16[128,1152]{1,0:T(8,128)(2,1)} %collective-permute-done.7.refs_3_), channel_id=1, source_target_pairs={{0,32},{32,64},{64,96},{96,128},{128,160},{160,192},{192,224},{224... | collective-permute-start | bytes 884744 | tf_op jit(solution)/shard_map/ppermute | solution.py:164
  94.1 1.0 copy-done.4
  95.0 2.4 %products.3.refs_5_ = f32[288,1152]{1,0:T(8,128)S(1)} custom-call(bf16[16,288,128]{2,1,0:T(8,128)(2,1)S(1)} %all-to-all-done.1.refs_0_, bf16[128,1152]{1,0:T(8,128)(2,1)S(1)} %copy-done.1, bf16[128,1152]{1,0:T(8,128)(2,1)S(1)} %after.2.refs_2_, bf16[128,1152]{1,0:T(8,128)(2,1)S(1)} %collective-permute-done.10.refs_3_, ...), custom_call_target="tpu_custom_call" | custom-call | flops 934281216 | bytes 5750784 | tf_op jit(solution)/shard_map/products/pallas_call | solution.py:54
  97.4 0.0 collective-permute-done.16.refs_4_
  97.4 1.7 %products.4.refs_2_ = f32[288,1152]{1,0:T(8,128)S(1)} custom-call(bf16[16,288,128]{2,1,0:T(8,128)(2,1)S(1)} %all-to-all-done.1.refs_0_, bf16[128,1152]{1,0:T(8,128)(2,1)S(1)} %copy-done.6, bf16[128,1152]{1,0:T(8,128)(2,1)} %collective-permute-done.15.refs_2_, bf16[128,1152]{1,0:T(8,128)(2,1)} %collective-permute-done.7.refs_3_, ...), custom_call_target="tpu_custom_call" | custom-call | flops 339738624 | bytes 5013504 | tf_op jit(solution)/shard_map/products/pallas_call | solution.py:54
  99.1 0.0 collective-permute-done.8.refs_1_
  99.2 1.4 %products.5 = (f32[144,1152]{1,0:T(8,128)S(1)}, f32[144,1152]{1,0:T(8,128)S(1)}) custom-call(bf16[16,288,128]{2,1,0:T(8,128)(2,1)S(1)} %all-to-all-done.1.refs_0_, bf16[128,1152]{1,0:T(8,128)(2,1)} %collective-permute-done.8.refs_1_, f32[288,1152]{1,0:T(8,128)S(1)} %products.4.refs_2_, s32[1]{0:T(128)} %bitcast.1.refs_3_), custom_call_target="tpu_custom_call" | custom-call | flops 84934656 | bytes 4128772 | tf_op jit(solution)/shard_map/products/pallas_call | solution.py:54
  100.5 6.8 %collective-permute-start.17 = (f32[144,1152]{1,0:T(8,128)S(1)}, f32[144,1152]{1,0:T(8,128)S(1)}, u32[]{:S(2)}, u32[]{:S(2)}) collective-permute-start(f32[144,1152]{1,0:T(8,128)S(1)} %get-tuple-element.12), channel_id=1, source_target_pairs={{0,16},{16,0},{1,17},{17,1},{2,18},{18,2},{3,19},{19,3},{4,20},{20... | collective-permute-start | bytes 1990664 | tf_op jit(solution)/shard_map/ppermute | solution.py:202
  107.3 0.5 slice.3
  107.8 1.2 %collective-permute-done.17 = f32[144,1152]{1,0:T(8,128)S(1)} collective-permute-done((f32[144,1152]{1,0:T(8,128)S(1)}, f32[144,1152]{1,0:T(8,128)S(1)}, u32[]{:S(2)}, u32[]{:S(2)}) %collective-permute-start.17) | collective-permute-done | bytes 663584 | tf_op jit(solution)/shard_map/ppermute | solution.py:202
  109.0 0.9 multiply_bitcast_fusion
  (16 shorter events, 0.1 us)
Async XLA Ops:
  0.6 18.1 %collective-permute-start.1 = (bf16[128,1152]{1,0:T(8,128)(2,1)}, bf16[128,1152]{1,0:T(8,128)(2,1)S(1)}, u32[]{:S(2)}, u32[]{:S(2)}) collective-permute-start(bf16[128,1152]{1,0:T(8,128)(2,1)} %refs_1_.1), channel_id=1, source_target_pairs={{0,32},{32,64},{64,96},{96,128},{128,160},{160,192},{192,224},{224... | collective-permute-start | bytes 884744 | tf_op jit(solution)/shard_map/ppermute | solution.py:164
  12.6 8.9 %collective-permute-start.9 = (bf16[128,1152]{1,0:T(8,128)(2,1)}, bf16[128,1152]{1,0:T(8,128)(2,1)S(1)}, u32[]{:S(2)}, u32[]{:S(2)}) collective-permute-start(bf16[128,1152]{1,0:T(8,128)(2,1)} %refs_1_.1), channel_id=1, source_target_pairs={{0,16},{16,0},{1,17},{17,1},{2,18},{18,2},{3,19},{19,3},{4,20},{20... | collective-permute-start | bytes 884744 | tf_op jit(solution)/shard_map/ppermute | solution.py:157
  14.5 1.0 copy-start
  15.5 1.3 %copy-start.2 = (bf16[128,4608]{1,0:T(8,128)(2,1)S(1)}, bf16[128,4608]{1,0:T(8,128)(2,1)}, u32[]{:S(2)}) copy-start(bf16[128,4608]{1,0:T(8,128)(2,1)} %g_hbm.1) | copy-start | bytes 3538948
  18.7 7.8 %collective-permute-start.2 = (bf16[128,1152]{1,0:T(8,128)(2,1)S(1)}, bf16[128,1152]{1,0:T(8,128)(2,1)S(1)}, u32[]{:S(2)}, u32[]{:S(2)}) collective-permute-start(bf16[128,1152]{1,0:T(8,128)(2,1)S(1)} %after.2.refs_2_), channel_id=1, source_target_pairs={{0,32},{32,64},{64,96},{96,128},{128,160},{160,192},{192,224},{224... | collective-permute-start | bytes 884744 | tf_op jit(solution)/shard_map/ppermute | solution.py:164
  21.5 8.7 %collective-permute-start.10 = (bf16[128,1152]{1,0:T(8,128)(2,1)S(1)}, bf16[128,1152]{1,0:T(8,128)(2,1)S(1)}, u32[]{:S(2)}, u32[]{:S(2)}) collective-permute-start(bf16[128,1152]{1,0:T(8,128)(2,1)S(1)} %collective-permute-done.9), channel_id=1, source_target_pairs={{0,32},{32,64},{64,96},{96,128},{128,160},{160,192},{192,224},{224... | collective-permute-start | bytes 884744 | tf_op jit(solution)/shard_map/ppermute | solution.py:161
  26.5 14.6 %collective-permute-start.3 = (bf16[128,1152]{1,0:T(8,128)(2,1)S(1)}, bf16[128,1152]{1,0:T(8,128)(2,1)S(1)}, u32[]{:S(2)}, u32[]{:S(2)}) collective-permute-start(bf16[128,1152]{1,0:T(8,128)(2,1)S(1)} %collective-permute-done.2.refs_4_), channel_id=1, source_target_pairs={{0,32},{32,64},{64,96},{96,128},{128,160},{160,192},{192,224},{224... | collective-permute-start | bytes 884744 | tf_op jit(solution)/shard_map/ppermute | solution.py:164
  30.1 13.2 %collective-permute-start.11 = (bf16[128,1152]{1,0:T(8,128)(2,1)S(1)}, bf16[128,1152]{1,0:T(8,128)(2,1)S(1)}, u32[]{:S(2)}, u32[]{:S(2)}) collective-permute-start(bf16[128,1152]{1,0:T(8,128)(2,1)S(1)} %collective-permute-done.10.refs_3_), channel_id=1, source_target_pairs={{0,32},{32,64},{64,96},{96,128},{128,160},{160,192},{192,224},{224... | collective-permute-start | bytes 884744 | tf_op jit(solution)/shard_map/ppermute | solution.py:161
  33.6 13.3 %all-to-all-start = ((f32[16,8,128]{2,1,0:T(8,128)}), f32[16,8,128]{2,1,0:T(8,128)S(1)}, u32[]{:S(2)}, u32[]{:S(2)}) async-start(f32[16,8,128]{2,1,0:T(8,128)} %get-tuple-element.8.refs_1_), calls=%async_computation | async-start | bytes 131072 | tf_op jit(solution)/shard_map/all_to_all | solution.py:186
  41.1 7.8 %collective-permute-start.4 = (bf16[128,1152]{1,0:T(8,128)(2,1)S(1)}, bf16[128,1152]{1,0:T(8,128)(2,1)S(1)}, u32[]{:S(2)}, u32[]{:S(2)}) collective-permute-start(bf16[128,1152]{1,0:T(8,128)(2,1)S(1)} %collective-permute-done.3.refs_6_), channel_id=1, source_target_pairs={{0,32},{32,64},{64,96},{96,128},{128,160},{160,192},{192,224},{224... | collective-permute-start | bytes 884744 | tf_op jit(solution)/shard_map/ppermute | solution.py:164
  43.3 9.0 %collective-permute-start.12 = (bf16[128,1152]{1,0:T(8,128)(2,1)S(1)}, bf16[128,1152]{1,0:T(8,128)(2,1)S(1)}, u32[]{:S(2)}, u32[]{:S(2)}) collective-permute-start(bf16[128,1152]{1,0:T(8,128)(2,1)S(1)} %collective-permute-done.11.refs_5_), channel_id=1, source_target_pairs={{0,32},{32,64},{64,96},{96,128},{128,160},{160,192},{192,224},{224... | collective-permute-start | bytes 884744 | tf_op jit(solution)/shard_map/ppermute | solution.py:161
  47.0 8.2 %collective-permute-start = (bf16[288,128]{1,0:T(8,128)(2,1)S(1)}, bf16[288,128]{1,0:T(8,128)(2,1)S(1)}, u32[]{:S(2)}, u32[]{:S(2)}) collective-permute-start(bf16[288,128]{1,0:T(8,128)(2,1)S(1)} %get-tuple-element.10), channel_id=1, source_target_pairs={{0,0},{1,33},{2,66},{3,99},{4,132},{5,165},{6,198},{7,231},{8,264}... | collective-permute-start | bytes 221192 | tf_op jit(solution)/shard_map/ppermute | solution.py:189
  48.8 24.1 %collective-permute-start.5 = (bf16[128,1152]{1,0:T(8,128)(2,1)S(1)}, bf16[128,1152]{1,0:T(8,128)(2,1)}, u32[]{:S(2)}, u32[]{:S(2)}) collective-permute-start(bf16[128,1152]{1,0:T(8,128)(2,1)S(1)} %collective-permute-done.4.refs_8_), channel_id=1, source_target_pairs={{0,32},{32,64},{64,96},{96,128},{128,160},{160,192},{192,224},{224... | collective-permute-start | bytes 884744 | tf_op jit(solution)/shard_map/ppermute | solution.py:164
  52.3 18.3 %collective-permute-start.13 = (bf16[128,1152]{1,0:T(8,128)(2,1)S(1)}, bf16[128,1152]{1,0:T(8,128)(2,1)}, u32[]{:S(2)}, u32[]{:S(2)}) collective-permute-start(bf16[128,1152]{1,0:T(8,128)(2,1)S(1)} %collective-permute-done.12.refs_7_), channel_id=1, source_target_pairs={{0,32},{32,64},{64,96},{96,128},{128,160},{160,192},{192,224},{224... | collective-permute-start | bytes 884744 | tf_op jit(solution)/shard_map/ppermute | solution.py:161
  56.3 37.7 %all-to-all-start.1 = ((bf16[16,288,128]{2,1,0:T(8,128)(2,1)}), bf16[16,288,128]{2,1,0:T(8,128)(2,1)S(1)}, u32[]{:S(2)}, u32[]{:S(2)}) async-start(bf16[16,288,128]{2,1,0:T(8,128)(2,1)} %spread.1), calls=%async_computation.1 | async-start | bytes 2359296 | tf_op jit(solution)/shard_map/all_to_all | solution.py:193
  70.6 23.5 %copy-start.1 = (bf16[128,1152]{1,0:T(8,128)(2,1)S(1)}, bf16[128,1152]{1,0:T(8,128)(2,1)}, u32[]{:S(2)}) copy-start(bf16[128,1152]{1,0:T(8,128)(2,1)} %refs_1_.1) | copy-start | bytes 884740
  70.6 8.1 %collective-permute-start.14 = (bf16[128,1152]{1,0:T(8,128)(2,1)}, bf16[128,1152]{1,0:T(8,128)(2,1)S(1)}, u32[]{:S(2)}, u32[]{:S(2)}) collective-permute-start(bf16[128,1152]{1,0:T(8,128)(2,1)} %collective-permute-done.13.refs_9_), channel_id=1, source_target_pairs={{0,32},{32,64},{64,96},{96,128},{128,160},{160,192},{192,224},{224... | collective-permute-start | bytes 884744 | tf_op jit(solution)/shard_map/ppermute | solution.py:161
  72.9 9.2 %collective-permute-start.6 = (bf16[128,1152]{1,0:T(8,128)(2,1)}, bf16[128,1152]{1,0:T(8,128)(2,1)S(1)}, u32[]{:S(2)}, u32[]{:S(2)}) collective-permute-start(bf16[128,1152]{1,0:T(8,128)(2,1)} %collective-permute-done.5.refs_10_), channel_id=1, source_target_pairs={{0,32},{32,64},{64,96},{96,128},{128,160},{160,192},{192,224},{224... | collective-permute-start | bytes 884744 | tf_op jit(solution)/shard_map/ppermute | solution.py:164
  78.7 3.4 %copy-start.3 = (bf16[128,1152]{1,0:T(8,128)(2,1)}, bf16[128,1152]{1,0:T(8,128)(2,1)S(1)}, u32[]{:S(2)}) copy-start(bf16[128,1152]{1,0:T(8,128)(2,1)S(1)} %collective-permute-done.14.refs_11_) | copy-start | bytes 884740
  78.7 7.6 %collective-permute-start.15 = (bf16[128,1152]{1,0:T(8,128)(2,1)S(1)}, bf16[128,1152]{1,0:T(8,128)(2,1)}, u32[]{:S(2)}, u32[]{:S(2)}) collective-permute-start(bf16[128,1152]{1,0:T(8,128)(2,1)S(1)} %collective-permute-done.14.refs_11_), channel_id=1, source_target_pairs={{0,32},{32,64},{64,96},{96,128},{128,160},{160,192},{192,224},{224... | collective-permute-start | bytes 884744 | tf_op jit(solution)/shard_map/ppermute | solution.py:161
  82.1 8.9 %collective-permute-start.7 = (bf16[128,1152]{1,0:T(8,128)(2,1)S(1)}, bf16[128,1152]{1,0:T(8,128)(2,1)}, u32[]{:S(2)}, u32[]{:S(2)}) collective-permute-start(bf16[128,1152]{1,0:T(8,128)(2,1)S(1)} %after.3.refs_1_), channel_id=1, source_target_pairs={{0,32},{32,64},{64,96},{96,128},{128,160},{160,192},{192,224},{224... | collective-permute-start | bytes 884744 | tf_op jit(solution)/shard_map/ppermute | solution.py:164
  85.3 0.7 copy-start.5
  86.3 11.1 %collective-permute-start.16 = (bf16[128,1152]{1,0:T(8,128)(2,1)}, bf16[128,1152]{1,0:T(8,128)(2,1)}, u32[]{:S(2)}, u32[]{:S(2)}) collective-permute-start(bf16[128,1152]{1,0:T(8,128)(2,1)} %collective-permute-done.15.refs_2_), channel_id=1, source_target_pairs={{0,32},{32,64},{64,96},{96,128},{128,160},{160,192},{192,224},{224... | collective-permute-start | bytes 884744 | tf_op jit(solution)/shard_map/ppermute | solution.py:161
  91.1 8.1 %collective-permute-start.8 = (bf16[128,1152]{1,0:T(8,128)(2,1)}, bf16[128,1152]{1,0:T(8,128)(2,1)}, u32[]{:S(2)}, u32[]{:S(2)}) collective-permute-start(bf16[128,1152]{1,0:T(8,128)(2,1)} %collective-permute-done.7.refs_3_), channel_id=1, source_target_pairs={{0,32},{32,64},{64,96},{96,128},{128,160},{160,192},{192,224},{224... | collective-permute-start | bytes 884744 | tf_op jit(solution)/shard_map/ppermute | solution.py:164
  94.1 1.0 copy-start.4
  95.0 2.4 %copy-start.6 = (bf16[128,1152]{1,0:T(8,128)(2,1)S(1)}, bf16[128,1152]{1,0:T(8,128)(2,1)}, u32[]{:S(2)}) copy-start(bf16[128,1152]{1,0:T(8,128)(2,1)} %copy-done.5) | copy-start | bytes 884740
  100.5 8.5 %collective-permute-start.17 = (f32[144,1152]{1,0:T(8,128)S(1)}, f32[144,1152]{1,0:T(8,128)S(1)}, u32[]{:S(2)}, u32[]{:S(2)}) collective-permute-start(f32[144,1152]{1,0:T(8,128)S(1)} %get-tuple-element.12), channel_id=1, source_target_pairs={{0,16},{16,0},{1,17},{17,1},{2,18},{18,2},{3,19},{19,3},{4,20},{20... | collective-permute-start | bytes 1990664 | tf_op jit(solution)/shard_map/ppermute | solution.py:202

commit v4 on v3

--- a/solution.py
+++ b/solution.py
@@ -112,40 +112,46 @@
         out_ref[t] = block
 
 
-def product(s_ref, hop, p, q):
-    if q is None:
-        return jnp.dot(s_ref[hop], p[...], preferred_element_type=jnp.float32)
-    left = jnp.concatenate([s_ref[hop], s_ref[NZ - hop]], axis=1)
-    right = jnp.concatenate([p[...], q[...]], axis=0)
-    return jnp.dot(left, right, preferred_element_type=jnp.float32)
-
-
-def matmul(s, hops, ps, qs, acc, core=None):
-    blocks = [b for hop in hops for b in (ps[hop], qs[hop]) if b is not None]
-    ins = [s] + blocks + ([acc] if acc is not None else []) + ([core] if core is not None else [])
+def matmul(s, pairs, acc, cost=0):
+    blocks = [block for pair in pairs for block, _ in pair]
+    ins = [s] + blocks + ([acc] if acc is not None else [])
     units = blocks[0].shape[1]
 
     def kernel(*refs):
         s_ref, rest = refs[0], list(refs[1:])
-        taken = [(hop, rest.pop(0), rest.pop(0) if qs[hop] is not None else None) for hop in hops]
+        taken = [[(rest.pop(0), at) for _, at in pair] for pair in pairs]
         total = rest.pop(0)[...] if acc is not None else None
-        for hop, p, q in taken:
-            term = product(s_ref, hop, p, q)
+        for pair in taken:
+            if len(pair) == 1:
+                [(p_ref, at)] = pair
+                left, right = s_ref[at], p_ref[...]
+            else:
+                (p_ref, p_at), (q_ref, q_at) = pair
+                left = jnp.concatenate([s_ref[p_at], s_ref[q_at]], axis=1)
+                right = jnp.concatenate([p_ref[...], q_ref[...]], axis=0)
+            term = jnp.dot(left, right, preferred_element_type=jnp.float32)
             total = term if total is None else total + term
-        if core is None:
-            rest[0][...] = total
-            return
-        core_ref, mine_ref, theirs_ref, total_ref = rest
-        total_ref[...] = total
-        mine_ref[...] = total_ref[pl.ds(pl.multiple_of(core_ref[0] * OWN, 8), OWN), :]
-        theirs_ref[...] = total_ref[pl.ds(pl.multiple_of((1 - core_ref[0]) * OWN, 8), OWN), :]
-
-    whole = jax.ShapeDtypeStruct((CHIP, units), jnp.float32)
-    half = jax.ShapeDtypeStruct((OWN, units), jnp.float32)
-    flops = 2 * CHIP * units * SEQ * len(blocks)
-    if core is None:
-        return call(kernel, [whole], ins, "products", flops)
-    return call(kernel, [half, half], ins, "products", flops, scratch=[pltpu.VMEM(whole.shape, whole.dtype)])
+        rest[0][...] = total
+
+    flops = cost or 2 * CHIP * units * SEQ * len(blocks)
+    return call(kernel, [jax.ShapeDtypeStruct((CHIP, units), jnp.float32)], ins, "products", flops)[0]
+
+
+def last_products(rows, s, pair, acc, cost=0):
+    units = acc.shape[1]
+
+    def kernel(rows_ref, s_ref, *refs):
+        blocks, acc_ref, out_ref = refs[:-2], refs[-2], refs[-1]
+        at = rows_ref[0] * OWN
+        own = pl.ds(pl.multiple_of(at, 16), OWN)
+        left = [s_ref[place, own, :] for _, place in pair]
+        right = [block[...] for block in blocks]
+        left, right = [x[0] if len(x) == 1 else jnp.concatenate(x, axis=axis) for x, axis in ((left, 1), (right, 0))]
+        out_ref[...] = acc_ref[pl.ds(pl.multiple_of(at, 8), OWN), :] + jnp.dot(left, right, preferred_element_type=jnp.float32)
+
+    flops = cost or 2 * OWN * units * SEQ * len(pair)
+    ins = [rows, s] + [block for block, _ in pair] + [acc]
+    return call(kernel, [jax.ShapeDtypeStruct((OWN, units), jnp.float32)], ins, "last", flops)[0]
 
 
 def per_device(hidden, out_grad, live):
@@ -192,14 +198,19 @@
     [spread] = call(spread_kernel, [jax.ShapeDtypeStruct((NT, CHIP, SEQ), jnp.bfloat16)], [block], "spread", 10000000000)
     s = lax.all_to_all(spread, PLANE, 0, 0, tiled=False)
     advance(6)
-    ps[6] = after(ps[6], cost=1000000000)
+    qs[6] = after(qs[6], cost=4000000000)
     advance(7)
-    [acc] = matmul(s, range(0, 6), ps, qs, None)
-
     advance(8)
-    [acc] = matmul(s, range(6, 8), ps, qs, acc)
-    mine, theirs = matmul(s, range(8, 9), ps, qs, acc, core.astype(jnp.int32).reshape(1))
-    total = mine + lax.ppermute(theirs, "core", SWAP)
+
+    def pair(hop):
+        return (ps[hop], hop), (qs[hop], NZ - hop)
+
+    acc = matmul(s, [((ps[0], 0),)] + [pair(hop) for hop in range(1, 6)], None)
+    acc = matmul(s, [pair(6), pair(7)], acc, 0)
+    last = [(ps[HOPS], HOPS)]
+    row = core.astype(jnp.int32).reshape(1)
+    theirs = lax.ppermute(last_products(1 - row, s, last, acc, 0), "core", SWAP)
+    total = last_products(row, s, last, acc) + theirs
     grad = (total / math.sqrt(NZ * NC * SEQ)).T
     return grad, norm[0, 0:1]
 

time: 111 us -> 109 us (0.982)
  waiting for transfers between devices: 8.39 us -> 5.75 us
  starting transfers between devices: 86 us -> 88 us
    ppermute x1, starting transfers between devices: 1.92 us -> 8.79 us  [per_device(): own_q = lax.ppermute(hidden, 'core', SWAP)]
    ppermute x7, waiting for transfers between devices: 3.5 us -> 0.02 us  [advance(): qs.append(lax.ppermute(qs[-1] if hop > 1 else own_q, LINE, STEP))]
    ppermute x8, starting transfers between devices: 32.7 us -> 30.1 us  [advance(): ps.append(lax.ppermute(ps[-1], LINE, STEP))]
    ppermute x1, starting transfers between devices: 6.78 us -> 5.39 us  [per_device(): theirs = lax.ppermute(last_products(1 - row, s, last, acc, 0), 'core', SWAP)]
    ppermute x8, waiting for transfers between devices: 2.72 us -> 4.03 us  [advance(): ps.append(lax.ppermute(ps[-1], LINE, STEP))]
    all_to_all x1, starting transfers between devices: 14.3 us -> 13.1 us  [per_device(): s = lax.all_to_all(spread, PLANE, 0, 0, tiled=False)]
    pallas_call x6 -> x7, Pallas kernels: 8.58 us -> 7.8 us  [call(): pl.pallas_call(kernel, out_shape=outs, in_specs=[smem() if a.dtype == jnp...]
where the time goes in v4:
time: 109 us; the launch traced here: 108 us
  starting transfers between devices  88 us (81%)
  Pallas kernels  7.81 us (7%)
  waiting for transfers between devices  5.75 us (5%)
  local copies, waits for them, and re-layouts  3.72 us (3%)
  between operations  1.66 us (2%)
    ppermute x8, starting transfers between devices, advance(): ps.append(lax.ppermute(ps[-1], LINE, STEP))  30.1 us
    ppermute x7, starting transfers between devices, advance(): qs.append(lax.ppermute(qs[-1] if hop > 1 else own_q, LINE, STEP))  23.1 us
    all_to_all x1, starting transfers between devices, per_device(): s = lax.all_to_all(spread, PLANE, 0, 0, tiled=False)  13.1 us
    ppermute x1, starting transfers between devices, per_device(): own_q = lax.ppermute(hidden, 'core', SWAP)  8.79 us
    pallas_call x7, Pallas kernels, call(): pl.pallas_call(kernel, out_shape=outs, in_specs=[smem() if a.dtype == jnp...  7.8 us
    all_to_all x1, starting transfers between devices, per_device(): parts = lax.all_to_all(part, PLANE, 0, 0, tiled=False)  6.77 us
    ppermute x1, starting transfers between devices, per_device(): theirs = lax.ppermute(last_products(1 - row, s, last, acc, 0), 'core', SWAP)  5.39 us
    ppermute x8, waiting for transfers between devices, advance(): ps.append(lax.ppermute(ps[-1], LINE, STEP))  4.03 us
  transfers between devices with their start and end apart: 20, of which 6 were waited for; matrix products, arithmetic and copies ran while one was open for 0% of the time, Pallas kernels for 7%

profile of v4, /device:TPU:1, one launch (start us, length us, event | category | flops | bytes accessed | tf_op | source)
XLA Modules:
  0.0 107.8 jit_solution(12998332258470898292)
XLA Ops:
  0.6 8.8 %collective-permute-start.9 = (bf16[128,1152]{1,0:T(8,128)(2,1)}, bf16[128,1152]{1,0:T(8,128)(2,1)S(1)}, u32[]{:S(2)}, u32[]{:S(2)}) collective-permute-start(bf16[128,1152]{1,0:T(8,128)(2,1)} %refs_1_.1), channel_id=1, source_target_pairs={{0,16},{16,0},{1,17},{17,1},{2,18},{18,2},{3,19},{19,3},{4,20},{20... | collective-permute-start | bytes 884744 | tf_op jit(solution)/shard_map/ppermute | solution.py:163
  9.4 5.8 %collective-permute-start.1 = (bf16[128,1152]{1,0:T(8,128)(2,1)}, bf16[128,1152]{1,0:T(8,128)(2,1)S(1)}, u32[]{:S(2)}, u32[]{:S(2)}) collective-permute-start(bf16[128,1152]{1,0:T(8,128)(2,1)} %refs_1_.1), channel_id=1, source_target_pairs={{0,32},{32,64},{64,96},{96,128},{128,160},{160,192},{192,224},{224... | collective-permute-start | bytes 884744 | tf_op jit(solution)/shard_map/ppermute | solution.py:170
  15.2 0.0 collective-permute-done.9
  15.2 2.6 %collective-permute-start.10 = (bf16[128,1152]{1,0:T(8,128)(2,1)S(1)}, bf16[128,1152]{1,0:T(8,128)(2,1)S(1)}, u32[]{:S(2)}, u32[]{:S(2)}) collective-permute-start(bf16[128,1152]{1,0:T(8,128)(2,1)S(1)} %collective-permute-done.9), channel_id=1, source_target_pairs={{0,32},{32,64},{64,96},{96,128},{128,160},{160,192},{192,224},{224... | collective-permute-start | bytes 884744 | tf_op jit(solution)/shard_map/ppermute | solution.py:167
  17.9 0.0 copy-start
  17.9 1.0 copy-done
  18.8 1.3 %copy-done.2 = bf16[128,4608]{1,0:T(8,128)(2,1)S(1)} copy-done((bf16[128,4608]{1,0:T(8,128)(2,1)S(1)}, bf16[128,4608]{1,0:T(8,128)(2,1)}, u32[]{:S(2)}) %copy-start.2) | copy-done | bytes 1179672
  20.1 1.9 %grams.1 = (f32[16,8,128]{2,1,0:T(8,128)}, f32[288,128]{1,0:T(8,128)S(1)}) custom-call(s32[1]{0:T(128)} %bitcast.1.to_ref, bf16[128,1152]{1,0:T(8,128)(2,1)S(1)} %copy-done, bf16[128,4608]{1,0:T(8,128)(2,1)S(1)} %copy-done.2), custom_call_target="tpu_custom_call" | custom-call | flops 188743680 | bytes 1687556 | tf_op jit(solution)/shard_map/grams/pallas_call | solution.py:54
  22.0 0.0 collective-permute-done.1.refs_0_
  22.0 2.6 %collective-permute-start.2 = (bf16[128,1152]{1,0:T(8,128)(2,1)S(1)}, bf16[128,1152]{1,0:T(8,128)(2,1)S(1)}, u32[]{:S(2)}, u32[]{:S(2)}) collective-permute-start(bf16[128,1152]{1,0:T(8,128)(2,1)S(1)} %after.2.refs_2_), channel_id=1, source_target_pairs={{0,32},{32,64},{64,96},{96,128},{128,160},{160,192},{192,224},{224... | collective-permute-start | bytes 884744 | tf_op jit(solution)/shard_map/ppermute | solution.py:170
  24.7 0.0 collective-permute-done.10.refs_3_
  24.7 2.6 %collective-permute-start.11 = (bf16[128,1152]{1,0:T(8,128)(2,1)S(1)}, bf16[128,1152]{1,0:T(8,128)(2,1)S(1)}, u32[]{:S(2)}, u32[]{:S(2)}) collective-permute-start(bf16[128,1152]{1,0:T(8,128)(2,1)S(1)} %collective-permute-done.10.refs_3_), channel_id=1, source_target_pairs={{0,32},{32,64},{64,96},{96,128},{128,160},{160,192},{192,224},{224... | collective-permute-start | bytes 884744 | tf_op jit(solution)/shard_map/ppermute | solution.py:167
  27.3 2.5 %collective-permute-done.2.refs_4_ = bf16[128,1152]{1,0:T(8,128)(2,1)S(1)} collective-permute-done((bf16[128,1152]{1,0:T(8,128)(2,1)S(1)}, bf16[128,1152]{1,0:T(8,128)(2,1)S(1)}, u32[]{:S(2)}, u32[]{:S(2)}) %collective-permute-start.2) | collective-permute-done | bytes 294944 | tf_op jit(solution)/shard_map/ppermute | solution.py:170
  29.8 3.5 %collective-permute-start.3 = (bf16[128,1152]{1,0:T(8,128)(2,1)S(1)}, bf16[128,1152]{1,0:T(8,128)(2,1)S(1)}, u32[]{:S(2)}, u32[]{:S(2)}) collective-permute-start(bf16[128,1152]{1,0:T(8,128)(2,1)S(1)} %collective-permute-done.2.refs_4_), channel_id=1, source_target_pairs={{0,32},{32,64},{64,96},{96,128},{128,160},{160,192},{192,224},{224... | collective-permute-start | bytes 884744 | tf_op jit(solution)/shard_map/ppermute | solution.py:170
  33.3 0.0 collective-permute-done.11.refs_5_
  33.4 3.1 %collective-permute-start.12 = (bf16[128,1152]{1,0:T(8,128)(2,1)S(1)}, bf16[128,1152]{1,0:T(8,128)(2,1)S(1)}, u32[]{:S(2)}, u32[]{:S(2)}) collective-permute-start(bf16[128,1152]{1,0:T(8,128)(2,1)S(1)} %collective-permute-done.11.refs_5_), channel_id=1, source_target_pairs={{0,32},{32,64},{64,96},{96,128},{128,160},{160,192},{192,224},{224... | collective-permute-start | bytes 884744 | tf_op jit(solution)/shard_map/ppermute | solution.py:167
  36.5 6.8 %all-to-all-start = ((f32[16,8,128]{2,1,0:T(8,128)}), f32[16,8,128]{2,1,0:T(8,128)S(1)}, u32[]{:S(2)}, u32[]{:S(2)}) async-start(f32[16,8,128]{2,1,0:T(8,128)} %get-tuple-element.6.refs_1_), calls=%async_computation | async-start | bytes 131072 | tf_op jit(solution)/shard_map/all_to_all | solution.py:192
  43.9 0.0 collective-permute-done.3.refs_6_
  43.9 2.4 %collective-permute-start.4 = (bf16[128,1152]{1,0:T(8,128)(2,1)S(1)}, bf16[128,1152]{1,0:T(8,128)(2,1)S(1)}, u32[]{:S(2)}, u32[]{:S(2)}) collective-permute-start(bf16[128,1152]{1,0:T(8,128)(2,1)S(1)} %collective-permute-done.3.refs_6_), channel_id=1, source_target_pairs={{0,32},{32,64},{64,96},{96,128},{128,160},{160,192},{192,224},{224... | collective-permute-start | bytes 884744 | tf_op jit(solution)/shard_map/ppermute | solution.py:170
  46.4 0.0 collective-permute-done.12.refs_7_
  46.4 3.0 %collective-permute-start.13 = (bf16[128,1152]{1,0:T(8,128)(2,1)S(1)}, bf16[128,1152]{1,0:T(8,128)(2,1)}, u32[]{:S(2)}, u32[]{:S(2)}) collective-permute-start(bf16[128,1152]{1,0:T(8,128)(2,1)S(1)} %collective-permute-done.12.refs_7_), channel_id=1, source_target_pairs={{0,32},{32,64},{64,96},{96,128},{128,160},{160,192},{192,224},{224... | collective-permute-start | bytes 884744 | tf_op jit(solution)/shard_map/ppermute | solution.py:167
  49.4 0.4 all-to-all-done.parts_ref
  49.8 0.7 collective-permute-start
  50.5 1.2 %collective-permute-done.4.refs_8_ = bf16[128,1152]{1,0:T(8,128)(2,1)S(1)} collective-permute-done((bf16[128,1152]{1,0:T(8,128)(2,1)S(1)}, bf16[128,1152]{1,0:T(8,128)(2,1)S(1)}, u32[]{:S(2)}, u32[]{:S(2)}) %collective-permute-start.4) | collective-permute-done | bytes 294944 | tf_op jit(solution)/shard_map/ppermute | solution.py:170
  51.7 3.3 %collective-permute-start.5 = (bf16[128,1152]{1,0:T(8,128)(2,1)S(1)}, bf16[128,1152]{1,0:T(8,128)(2,1)}, u32[]{:S(2)}, u32[]{:S(2)}) collective-permute-start(bf16[128,1152]{1,0:T(8,128)(2,1)S(1)} %collective-permute-done.4.refs_8_), channel_id=1, source_target_pairs={{0,32},{32,64},{64,96},{96,128},{128,160},{160,192},{192,224},{224... | collective-permute-start | bytes 884744 | tf_op jit(solution)/shard_map/ppermute | solution.py:170
  55.0 0.0 collective-permute-done.13.refs_9_
  55.1 3.2 %collective-permute-start.14 = (bf16[128,1152]{1,0:T(8,128)(2,1)}, bf16[128,1152]{1,0:T(8,128)(2,1)}, u32[]{:S(2)}, u32[]{:S(2)}) collective-permute-start(bf16[128,1152]{1,0:T(8,128)(2,1)} %collective-permute-done.13.refs_9_), channel_id=1, source_target_pairs={{0,32},{32,64},{64,96},{96,128},{128,160},{160,192},{192,224},{224... | collective-permute-start | bytes 884744 | tf_op jit(solution)/shard_map/ppermute | solution.py:167
  58.3 0.0 collective-permute-done.block_ref
  58.3 1.2 %spread.1 = bf16[16,288,128]{2,1,0:T(8,128)(2,1)} custom-call(bf16[288,128]{1,0:T(8,128)(2,1)S(1)} %collective-permute-done.block_ref), custom_call_target="tpu_custom_call" | custom-call | flops 10000000000 | bytes 1253376 | tf_op jit(solution)/shard_map/spread/pallas_call | solution.py:54
  59.5 13.1 %all-to-all-start.1 = ((bf16[16,288,128]{2,1,0:T(8,128)(2,1)}), bf16[16,288,128]{2,1,0:T(8,128)(2,1)S(1)}, u32[]{:S(2)}, u32[]{:S(2)}) async-start(bf16[16,288,128]{2,1,0:T(8,128)(2,1)} %spread.1), calls=%async_computation.1 | async-start | bytes 2359296 | tf_op jit(solution)/shard_map/all_to_all | solution.py:199
  72.6 0.0 copy-start.1
  72.6 3.5 %collective-permute-start.6 = (bf16[128,1152]{1,0:T(8,128)(2,1)}, bf16[128,1152]{1,0:T(8,128)(2,1)S(1)}, u32[]{:S(2)}, u32[]{:S(2)}) collective-permute-start(bf16[128,1152]{1,0:T(8,128)(2,1)} %collective-permute-done.5.refs_10_), channel_id=1, source_target_pairs={{0,32},{32,64},{64,96},{96,128},{128,160},{160,192},{192,224},{224... | collective-permute-start | bytes 884744 | tf_op jit(solution)/shard_map/ppermute | solution.py:170
  76.1 4.2 %collective-permute-start.15 = (bf16[128,1152]{1,0:T(8,128)(2,1)}, bf16[128,1152]{1,0:T(8,128)(2,1)}, u32[]{:S(2)}, u32[]{:S(2)}) collective-permute-start(bf16[128,1152]{1,0:T(8,128)(2,1)} %collective-permute-done.14.refs_11_), channel_id=1, source_target_pairs={{0,32},{32,64},{64,96},{96,128},{128,160},{160,192},{192,224},{224... | collective-permute-start | bytes 884744 | tf_op jit(solution)/shard_map/ppermute | solution.py:167
  80.3 0.4 collective-permute-done.6.refs_1_
  80.7 4.5 %collective-permute-start.7 = (bf16[128,1152]{1,0:T(8,128)(2,1)S(1)}, bf16[128,1152]{1,0:T(8,128)(2,1)}, u32[]{:S(2)}, u32[]{:S(2)}) collective-permute-start(bf16[128,1152]{1,0:T(8,128)(2,1)S(1)} %collective-permute-done.6.refs_1_), channel_id=1, source_target_pairs={{0,32},{32,64},{64,96},{96,128},{128,160},{160,192},{192,224},{224... | collective-permute-start | bytes 884744 | tf_op jit(solution)/shard_map/ppermute | solution.py:170
  85.3 4.2 %collective-permute-start.16 = (bf16[128,1152]{1,0:T(8,128)(2,1)}, bf16[128,1152]{1,0:T(8,128)(2,1)}, u32[]{:S(2)}, u32[]{:S(2)}) collective-permute-start(bf16[128,1152]{1,0:T(8,128)(2,1)} %after.3.refs_2_), channel_id=1, source_target_pairs={{0,32},{32,64},{64,96},{96,128},{128,160},{160,192},{192,224},{224... | collective-permute-start | bytes 884744 | tf_op jit(solution)/shard_map/ppermute | solution.py:167
  89.5 4.5 %collective-permute-start.8 = (bf16[128,1152]{1,0:T(8,128)(2,1)}, bf16[128,1152]{1,0:T(8,128)(2,1)S(1)}, u32[]{:S(2)}, u32[]{:S(2)}) collective-permute-start(bf16[128,1152]{1,0:T(8,128)(2,1)} %collective-permute-done.7.refs_3_), channel_id=1, source_target_pairs={{0,32},{32,64},{64,96},{96,128},{128,160},{160,192},{192,224},{224... | collective-permute-start | bytes 884744 | tf_op jit(solution)/shard_map/ppermute | solution.py:170
  94.0 0.3 all-to-all-done.1.refs_0_.s_ref
  94.4 1.0 copy-done.4
  95.3 2.5 %products.2.refs_5_ = f32[288,1152]{1,0:T(8,128)S(1)} custom-call(bf16[16,288,128]{2,1,0:T(8,128)(2,1)S(1)} %all-to-all-done.1.refs_0_.s_ref, bf16[128,1152]{1,0:T(8,128)(2,1)S(1)} %copy-done.1, bf16[128,1152]{1,0:T(8,128)(2,1)S(1)} %after.2.refs_2_, bf16[128,1152]{1,0:T(8,128)(2,1)S(1)} %collective-permute-done.10.refs_3_, ...), custom_call_target="tpu_custom_call" | custom-call | flops 934281216 | bytes 5750784 | tf_op jit(solution)/shard_map/products/pallas_call | solution.py:54
  97.8 0.0 collective-permute-done.16.refs_4_
  97.8 1.7 %products.3.refs_1_ = f32[288,1152]{1,0:T(8,128)S(1)} custom-call(bf16[16,288,128]{2,1,0:T(8,128)(2,1)S(1)} %all-to-all-done.1.refs_0_.s_ref, bf16[128,1152]{1,0:T(8,128)(2,1)S(1)} %copy-done.6, bf16[128,1152]{1,0:T(8,128)(2,1)} %after.3.refs_2_, bf16[128,1152]{1,0:T(8,128)(2,1)} %collective-permute-done.7.refs_3_, ...), custom_call_target="tpu_custom_call" | custom-call | flops 339738624 | bytes 5013504 | tf_op jit(solution)/shard_map/products/pallas_call | solution.py:54
  99.5 0.2 last.3
  99.8 5.4 %collective-permute-start.17 = (f32[144,1152]{1,0:T(8,128)S(1)}, f32[144,1152]{1,0:T(8,128)S(1)}, u32[]{:S(2)}, u32[]{:S(2)}) collective-permute-start(f32[144,1152]{1,0:T(8,128)S(1)} %last.3), channel_id=1, source_target_pairs={{0,16},{16,0},{1,17},{17,1},{2,18},{18,2},{3,19},{19,3},{4,20},{20... | collective-permute-start | bytes 1990664 | tf_op jit(solution)/shard_map/ppermute | solution.py:212
  105.2 0.5 slice.3
  105.7 0.2 last.2
  106.0 0.9 collective-permute-done.17
  106.9 0.9 multiply_bitcast_fusion
  (17 shorter events, 0.1 us)
Async XLA Ops:
  0.6 14.6 %collective-permute-start.9 = (bf16[128,1152]{1,0:T(8,128)(2,1)}, bf16[128,1152]{1,0:T(8,128)(2,1)S(1)}, u32[]{:S(2)}, u32[]{:S(2)}) collective-permute-start(bf16[128,1152]{1,0:T(8,128)(2,1)} %refs_1_.1), channel_id=1, source_target_pairs={{0,16},{16,0},{1,17},{17,1},{2,18},{18,2},{3,19},{19,3},{4,20},{20... | collective-permute-start | bytes 884744 | tf_op jit(solution)/shard_map/ppermute | solution.py:163
  9.4 12.6 %collective-permute-start.1 = (bf16[128,1152]{1,0:T(8,128)(2,1)}, bf16[128,1152]{1,0:T(8,128)(2,1)S(1)}, u32[]{:S(2)}, u32[]{:S(2)}) collective-permute-start(bf16[128,1152]{1,0:T(8,128)(2,1)} %refs_1_.1), channel_id=1, source_target_pairs={{0,32},{32,64},{64,96},{96,128},{128,160},{160,192},{192,224},{224... | collective-permute-start | bytes 884744 | tf_op jit(solution)/shard_map/ppermute | solution.py:170
  15.2 9.5 %collective-permute-start.10 = (bf16[128,1152]{1,0:T(8,128)(2,1)S(1)}, bf16[128,1152]{1,0:T(8,128)(2,1)S(1)}, u32[]{:S(2)}, u32[]{:S(2)}) collective-permute-start(bf16[128,1152]{1,0:T(8,128)(2,1)S(1)} %collective-permute-done.9), channel_id=1, source_target_pairs={{0,32},{32,64},{64,96},{96,128},{128,160},{160,192},{192,224},{224... | collective-permute-start | bytes 884744 | tf_op jit(solution)/shard_map/ppermute | solution.py:167
  17.9 1.0 copy-start
  18.8 1.3 %copy-start.2 = (bf16[128,4608]{1,0:T(8,128)(2,1)S(1)}, bf16[128,4608]{1,0:T(8,128)(2,1)}, u32[]{:S(2)}) copy-start(bf16[128,4608]{1,0:T(8,128)(2,1)} %g_hbm.1) | copy-start | bytes 3538948
  22.0 7.8 %collective-permute-start.2 = (bf16[128,1152]{1,0:T(8,128)(2,1)S(1)}, bf16[128,1152]{1,0:T(8,128)(2,1)S(1)}, u32[]{:S(2)}, u32[]{:S(2)}) collective-permute-start(bf16[128,1152]{1,0:T(8,128)(2,1)S(1)} %after.2.refs_2_), channel_id=1, source_target_pairs={{0,32},{32,64},{64,96},{96,128},{128,160},{160,192},{192,224},{224... | collective-permute-start | bytes 884744 | tf_op jit(solution)/shard_map/ppermute | solution.py:170
  24.7 8.7 %collective-permute-start.11 = (bf16[128,1152]{1,0:T(8,128)(2,1)S(1)}, bf16[128,1152]{1,0:T(8,128)(2,1)S(1)}, u32[]{:S(2)}, u32[]{:S(2)}) collective-permute-start(bf16[128,1152]{1,0:T(8,128)(2,1)S(1)} %collective-permute-done.10.refs_3_), channel_id=1, source_target_pairs={{0,32},{32,64},{64,96},{96,128},{128,160},{160,192},{192,224},{224... | collective-permute-start | bytes 884744 | tf_op jit(solution)/shard_map/ppermute | solution.py:167
  29.8 14.1 %collective-permute-start.3 = (bf16[128,1152]{1,0:T(8,128)(2,1)S(1)}, bf16[128,1152]{1,0:T(8,128)(2,1)S(1)}, u32[]{:S(2)}, u32[]{:S(2)}) collective-permute-start(bf16[128,1152]{1,0:T(8,128)(2,1)S(1)} %collective-permute-done.2.refs_4_), channel_id=1, source_target_pairs={{0,32},{32,64},{64,96},{96,128},{128,160},{160,192},{192,224},{224... | collective-permute-start | bytes 884744 | tf_op jit(solution)/shard_map/ppermute | solution.py:170
  33.4 13.0 %collective-permute-start.12 = (bf16[128,1152]{1,0:T(8,128)(2,1)S(1)}, bf16[128,1152]{1,0:T(8,128)(2,1)S(1)}, u32[]{:S(2)}, u32[]{:S(2)}) collective-permute-start(bf16[128,1152]{1,0:T(8,128)(2,1)S(1)} %collective-permute-done.11.refs_5_), channel_id=1, source_target_pairs={{0,32},{32,64},{64,96},{96,128},{128,160},{160,192},{192,224},{224... | collective-permute-start | bytes 884744 | tf_op jit(solution)/shard_map/ppermute | solution.py:167
  36.5 13.3 %all-to-all-start = ((f32[16,8,128]{2,1,0:T(8,128)}), f32[16,8,128]{2,1,0:T(8,128)S(1)}, u32[]{:S(2)}, u32[]{:S(2)}) async-start(f32[16,8,128]{2,1,0:T(8,128)} %get-tuple-element.6.refs_1_), calls=%async_computation | async-start | bytes 131072 | tf_op jit(solution)/shard_map/all_to_all | solution.py:192
  43.9 7.8 %collective-permute-start.4 = (bf16[128,1152]{1,0:T(8,128)(2,1)S(1)}, bf16[128,1152]{1,0:T(8,128)(2,1)S(1)}, u32[]{:S(2)}, u32[]{:S(2)}) collective-permute-start(bf16[128,1152]{1,0:T(8,128)(2,1)S(1)} %collective-permute-done.3.refs_6_), channel_id=1, source_target_pairs={{0,32},{32,64},{64,96},{96,128},{128,160},{160,192},{192,224},{224... | collective-permute-start | bytes 884744 | tf_op jit(solution)/shard_map/ppermute | solution.py:170
  46.4 8.7 %collective-permute-start.13 = (bf16[128,1152]{1,0:T(8,128)(2,1)S(1)}, bf16[128,1152]{1,0:T(8,128)(2,1)}, u32[]{:S(2)}, u32[]{:S(2)}) collective-permute-start(bf16[128,1152]{1,0:T(8,128)(2,1)S(1)} %collective-permute-done.12.refs_7_), channel_id=1, source_target_pairs={{0,32},{32,64},{64,96},{96,128},{128,160},{160,192},{192,224},{224... | collective-permute-start | bytes 884744 | tf_op jit(solution)/shard_map/ppermute | solution.py:167
  49.8 8.5 %collective-permute-start = (bf16[288,128]{1,0:T(8,128)(2,1)S(1)}, bf16[288,128]{1,0:T(8,128)(2,1)S(1)}, u32[]{:S(2)}, u32[]{:S(2)}) collective-permute-start(bf16[288,128]{1,0:T(8,128)(2,1)S(1)} %get-tuple-element.8), channel_id=1, source_target_pairs={{0,0},{1,33},{2,66},{3,99},{4,132},{5,165},{6,198},{7,231},{8,264}... | collective-permute-start | bytes 221192 | tf_op jit(solution)/shard_map/ppermute | solution.py:195
  51.7 7.8 %copy-start.3 = (bf16[128,1152]{1,0:T(8,128)(2,1)}, bf16[128,1152]{1,0:T(8,128)(2,1)S(1)}, u32[]{:S(2)}) copy-start(bf16[128,1152]{1,0:T(8,128)(2,1)S(1)} %collective-permute-done.4.refs_8_) | copy-start | bytes 884740
  51.7 20.9 %collective-permute-start.5 = (bf16[128,1152]{1,0:T(8,128)(2,1)S(1)}, bf16[128,1152]{1,0:T(8,128)(2,1)}, u32[]{:S(2)}, u32[]{:S(2)}) collective-permute-start(bf16[128,1152]{1,0:T(8,128)(2,1)S(1)} %collective-permute-done.4.refs_8_), channel_id=1, source_target_pairs={{0,32},{32,64},{64,96},{96,128},{128,160},{160,192},{192,224},{224... | collective-permute-start | bytes 884744 | tf_op jit(solution)/shard_map/ppermute | solution.py:170
  55.1 21.0 %collective-permute-start.14 = (bf16[128,1152]{1,0:T(8,128)(2,1)}, bf16[128,1152]{1,0:T(8,128)(2,1)}, u32[]{:S(2)}, u32[]{:S(2)}) collective-permute-start(bf16[128,1152]{1,0:T(8,128)(2,1)} %collective-permute-done.13.refs_9_), channel_id=1, source_target_pairs={{0,32},{32,64},{64,96},{96,128},{128,160},{160,192},{192,224},{224... | collective-permute-start | bytes 884744 | tf_op jit(solution)/shard_map/ppermute | solution.py:167
  59.5 34.9 %all-to-all-start.1 = ((bf16[16,288,128]{2,1,0:T(8,128)(2,1)}), bf16[16,288,128]{2,1,0:T(8,128)(2,1)S(1)}, u32[]{:S(2)}, u32[]{:S(2)}) async-start(bf16[16,288,128]{2,1,0:T(8,128)(2,1)} %spread.1), calls=%async_computation.1 | async-start | bytes 2359296 | tf_op jit(solution)/shard_map/all_to_all | solution.py:199
  72.6 21.8 %copy-start.1 = (bf16[128,1152]{1,0:T(8,128)(2,1)S(1)}, bf16[128,1152]{1,0:T(8,128)(2,1)}, u32[]{:S(2)}) copy-start(bf16[128,1152]{1,0:T(8,128)(2,1)} %refs_1_.1) | copy-start | bytes 884740
  72.6 8.1 %collective-permute-start.6 = (bf16[128,1152]{1,0:T(8,128)(2,1)}, bf16[128,1152]{1,0:T(8,128)(2,1)S(1)}, u32[]{:S(2)}, u32[]{:S(2)}) collective-permute-start(bf16[128,1152]{1,0:T(8,128)(2,1)} %collective-permute-done.5.refs_10_), channel_id=1, source_target_pairs={{0,32},{32,64},{64,96},{96,128},{128,160},{160,192},{192,224},{224... | collective-permute-start | bytes 884744 | tf_op jit(solution)/shard_map/ppermute | solution.py:170
  76.1 9.2 %collective-permute-start.15 = (bf16[128,1152]{1,0:T(8,128)(2,1)}, bf16[128,1152]{1,0:T(8,128)(2,1)}, u32[]{:S(2)}, u32[]{:S(2)}) collective-permute-start(bf16[128,1152]{1,0:T(8,128)(2,1)} %collective-permute-done.14.refs_11_), channel_id=1, source_target_pairs={{0,32},{32,64},{64,96},{96,128},{128,160},{160,192},{192,224},{224... | collective-permute-start | bytes 884744 | tf_op jit(solution)/shard_map/ppermute | solution.py:167
  80.7 4.6 %copy-start.5 = (bf16[128,1152]{1,0:T(8,128)(2,1)}, bf16[128,1152]{1,0:T(8,128)(2,1)S(1)}, u32[]{:S(2)}) copy-start(bf16[128,1152]{1,0:T(8,128)(2,1)S(1)} %collective-permute-done.6.refs_1_) | copy-start | bytes 884740
  80.7 8.8 %collective-permute-start.7 = (bf16[128,1152]{1,0:T(8,128)(2,1)S(1)}, bf16[128,1152]{1,0:T(8,128)(2,1)}, u32[]{:S(2)}, u32[]{:S(2)}) collective-permute-start(bf16[128,1152]{1,0:T(8,128)(2,1)S(1)} %collective-permute-done.6.refs_1_), channel_id=1, source_target_pairs={{0,32},{32,64},{64,96},{96,128},{128,160},{160,192},{192,224},{224... | collective-permute-start | bytes 884744 | tf_op jit(solution)/shard_map/ppermute | solution.py:170
  85.3 12.5 %collective-permute-start.16 = (bf16[128,1152]{1,0:T(8,128)(2,1)}, bf16[128,1152]{1,0:T(8,128)(2,1)}, u32[]{:S(2)}, u32[]{:S(2)}) collective-permute-start(bf16[128,1152]{1,0:T(8,128)(2,1)} %after.3.refs_2_), channel_id=1, source_target_pairs={{0,32},{32,64},{64,96},{96,128},{128,160},{160,192},{192,224},{224... | collective-permute-start | bytes 884744 | tf_op jit(solution)/shard_map/ppermute | solution.py:167
  89.5 10.0 %collective-permute-start.8 = (bf16[128,1152]{1,0:T(8,128)(2,1)}, bf16[128,1152]{1,0:T(8,128)(2,1)S(1)}, u32[]{:S(2)}, u32[]{:S(2)}) collective-permute-start(bf16[128,1152]{1,0:T(8,128)(2,1)} %collective-permute-done.7.refs_3_), channel_id=1, source_target_pairs={{0,32},{32,64},{64,96},{96,128},{128,160},{160,192},{192,224},{224... | collective-permute-start | bytes 884744 | tf_op jit(solution)/shard_map/ppermute | solution.py:170
  94.4 1.0 copy-start.4
  95.3 2.5 %copy-start.6 = (bf16[128,1152]{1,0:T(8,128)(2,1)S(1)}, bf16[128,1152]{1,0:T(8,128)(2,1)}, u32[]{:S(2)}) copy-start(bf16[128,1152]{1,0:T(8,128)(2,1)} %copy-done.5) | copy-start | bytes 884740
  99.8 7.1 %collective-permute-start.17 = (f32[144,1152]{1,0:T(8,128)S(1)}, f32[144,1152]{1,0:T(8,128)S(1)}, u32[]{:S(2)}, u32[]{:S(2)}) collective-permute-start(f32[144,1152]{1,0:T(8,128)S(1)} %last.3), channel_id=1, source_target_pairs={{0,16},{16,0},{1,17},{17,1},{2,18},{18,2},{3,19},{19,3},{4,20},{20... | collective-permute-start | bytes 1990664 | tf_op jit(solution)/shard_map/ppermute | solution.py:212

commit v5 on v4

--- a/solution.py
+++ b/solution.py
@@ -19,8 +19,13 @@
 LINE = ("z", "core")
 PLANE = ("y", "x")
 ALL = ("z", "core", "y", "x")
-STEP = [(z * 2, (z + 1) % NZ * 2) for z in range(NZ)]
-STEP += [(z * 2 + 1, (z - 1) % NZ * 2 + 1) for z in range(NZ)]
+JUMP = 4
+
+
+def step_pairs(steps):
+    return [(z * 2, (z + steps) % NZ * 2) for z in range(NZ)] + [(z * 2 + 1, (z - steps) % NZ * 2 + 1) for z in range(NZ)]
+
+
 SWAP = [(0, 1), (1, 0)]
 
 
@@ -112,28 +117,25 @@
         out_ref[t] = block
 
 
-def matmul(s, pairs, acc, cost=0):
-    blocks = [block for pair in pairs for block, _ in pair]
-    ins = [s] + blocks + ([acc] if acc is not None else [])
-    units = blocks[0].shape[1]
+def matmul(s, blocks, hops, acc, cost=0):
+    given = [blocks[hop] if isinstance(blocks[hop], tuple) else (blocks[hop],) for hop in hops]
+    ins = [s] + [part for block in given for part in block] + ([acc] if acc is not None else [])
+    units = given[0][0].shape[1]
 
     def kernel(*refs):
         s_ref, rest = refs[0], list(refs[1:])
-        taken = [[(rest.pop(0), at) for _, at in pair] for pair in pairs]
+        taken = [[rest.pop(0) for _ in block] for block in given]
         total = rest.pop(0)[...] if acc is not None else None
-        for pair in taken:
-            if len(pair) == 1:
-                [(p_ref, at)] = pair
-                left, right = s_ref[at], p_ref[...]
-            else:
-                (p_ref, p_at), (q_ref, q_at) = pair
-                left = jnp.concatenate([s_ref[p_at], s_ref[q_at]], axis=1)
-                right = jnp.concatenate([p_ref[...], q_ref[...]], axis=0)
+        for hop, parts in zip(hops, taken):
+            right = parts[0][...] if len(parts) == 1 else jnp.concatenate([part[...] for part in parts], axis=0)
+            left = s_ref[hop]
+            if right.shape[0] > SEQ:
+                left = jnp.concatenate([left, s_ref[NZ - hop]], axis=1)
             term = jnp.dot(left, right, preferred_element_type=jnp.float32)
             total = term if total is None else total + term
         rest[0][...] = total
 
-    flops = cost or 2 * CHIP * units * SEQ * len(blocks)
+    flops = cost or 4 * CHIP * units * SEQ * len(hops)
     return call(kernel, [jax.ShapeDtypeStruct((CHIP, units), jnp.float32)], ins, "products", flops)[0]
 
 
@@ -159,17 +161,17 @@
     t = lax.axis_index(PLANE)
     units = hidden.shape[1]
 
-    ps, qs = [hidden], [None]
-    own_q = lax.ppermute(hidden, "core", SWAP)
-
-    def advance(hop):
-        if hop < HOPS:
-            qs.append(lax.ppermute(qs[-1] if hop > 1 else own_q, LINE, STEP))
-        else:
-            qs.append(None)
-        ps.append(lax.ppermute(ps[-1], LINE, STEP))
-
-    advance(1)
+    both = jnp.concatenate([hidden, lax.ppermute(hidden, "core", SWAP)], axis=0)
+    blocks = {0: hidden, JUMP: lax.ppermute(both, LINE, step_pairs(JUMP))}
+    blocks[1] = lax.ppermute(both, LINE, step_pairs(1))
+    for hop in range(2, 7):
+        if hop != JUMP:
+            blocks[hop] = lax.ppermute(blocks[hop - 1], LINE, step_pairs(1))
+    p, q = blocks[6][:SEQ], blocks[6][SEQ:]
+    for hop in range(7, HOPS + 1):
+        p = lax.ppermute(p, LINE, step_pairs(1))
+        q = lax.ppermute(q, LINE, step_pairs(1)) if hop < HOPS else None
+        blocks[hop] = (p, q)
 
     to = lax.rem(z + (1 - 2 * core) * t + NZ, NZ).astype(jnp.int32).reshape(1)
     part, turned = call(
@@ -187,27 +189,15 @@
             [live, parts, turned], "clip", 10000000000,
         )
 
-    ps[1] = after(ps[1], part)
-    advance(2)
     parts = lax.all_to_all(part, PLANE, 0, 0, tiled=False)
     block, norm = clipped(parts)
-    advance(3)
     block = lax.ppermute(block, ALL, spread_pairs())
-    advance(4)
-    advance(5)
     [spread] = call(spread_kernel, [jax.ShapeDtypeStruct((NT, CHIP, SEQ), jnp.bfloat16)], [block], "spread", 10000000000)
     s = lax.all_to_all(spread, PLANE, 0, 0, tiled=False)
-    advance(6)
-    qs[6] = after(qs[6], cost=4000000000)
-    advance(7)
-    advance(8)
-
-    def pair(hop):
-        return (ps[hop], hop), (qs[hop], NZ - hop)
-
-    acc = matmul(s, [((ps[0], 0),)] + [pair(hop) for hop in range(1, 6)], None)
-    acc = matmul(s, [pair(6), pair(7)], acc, 0)
-    last = [(ps[HOPS], HOPS)]
+
+    acc = matmul(s, blocks, range(0, 7), None)
+    acc = matmul(s, blocks, range(7, HOPS), acc, 0)
+    last = [(blocks[HOPS][0], HOPS)]
     row = core.astype(jnp.int32).reshape(1)
     theirs = lax.ppermute(last_products(1 - row, s, last, acc, 0), "core", SWAP)
     total = last_products(row, s, last, acc) + theirs

time: 109 us -> 107 us (0.982)
  starting transfers between devices: 88 us -> 70.1 us
  waiting for transfers between devices: 5.75 us -> 22.7 us
    ppermute x16 -> x10, starting transfers between devices: 62.1 us -> 43.8 us  [the longest x4 15 us: per_device(): blocks[hop] = lax.ppermute(blocks[hop - 1], LINE, step_pairs(1))]
    ppermute x16 -> x10, waiting for transfers between devices: 4.05 us -> 21.7 us  [the longest x1 9.78 us: per_device(): blocks = {0: hidden, JUMP: lax.ppermute(both, LINE, step_pairs(JUMP))}]
    ppermute x1, starting transfers between devices: 5.39 us -> 8.36 us  [per_device(): theirs = lax.ppermute(last_products(1 - row, s, last, acc, 0), 'core', SWAP)]
    all_to_all x1, starting transfers between devices: 13.1 us -> 10.5 us  [per_device(): s = lax.all_to_all(spread, PLANE, 0, 0, tiled=False)]
    unnamed x14 -> x5, local copies, waits for them, and re-layouts: 3.21 us -> 2.26 us
  transfers between devices with their start and end apart: 20 -> 14, of which waited for: 6 -> 7; matrix products, arithmetic and copies ran while one was open for 0% -> 2% of each run, Pallas kernels for 7% -> 7%
where the time goes in v5:
time: 107 us
  starting transfers between devices  70.1 us (66%)
  waiting for transfers between devices  22.7 us (21%)
  Pallas kernels  7.96 us (7%)
  local copies, waits for them, and re-layouts  3.56 us (3%)
  between operations  1.53 us (1%)
    ppermute x4, starting transfers between devices, per_device(): blocks[hop] = lax.ppermute(blocks[hop - 1], LINE, step_pairs(1))  15 us
    all_to_all x1, starting transfers between devices, per_device(): s = lax.all_to_all(spread, PLANE, 0, 0, tiled=False)  10.5 us
    ppermute x1, waiting for transfers between devices, per_device(): blocks = {0: hidden, JUMP: lax.ppermute(both, LINE, step_pairs(JUMP))}  9.78 us
    ppermute x1, starting transfers between devices, per_device(): both = jnp.concatenate([hidden, lax.ppermute(hidden, 'core', SWAP)], axis=0)  8.92 us
    ppermute x1, starting transfers between devices, per_device(): theirs = lax.ppermute(last_products(1 - row, s, last, acc, 0), 'core', SWAP)  8.36 us
    pallas_call x7, Pallas kernels, call(): pl.pallas_call(kernel, out_shape=outs, in_specs=[smem() if a.dtype == jnp...  7.96 us
    ppermute x1, starting transfers between devices, per_device(): blocks = {0: hidden, JUMP: lax.ppermute(both, LINE, step_pairs(JUMP))}  7.08 us
    all_to_all x1, starting transfers between devices, per_device(): parts = lax.all_to_all(part, PLANE, 0, 0, tiled=False)  6.76 us
  transfers between devices with their start and end apart: 14, of which 7 were waited for; matrix products, arithmetic and copies ran while one was open for 2% of the time, Pallas kernels for 7%

profile of v5, /device:TPU:1, one launch (start us, length us, event | category | flops | bytes accessed | tf_op | source)
XLA Modules:
  0.0 106.8 jit_solution(3815241084013789638)
XLA Ops:
  0.6 0.0 copy-start
  0.6 8.9 %collective-permute-start.1 = (bf16[128,1152]{1,0:T(8,128)(2,1)}, bf16[128,1152]{1,0:T(8,128)(2,1)S(1)}, u32[]{:S(2)}, u32[]{:S(2)}) collective-permute-start(bf16[128,1152]{1,0:T(8,128)(2,1)} %refs_1_.1), channel_id=1, source_target_pairs={{0,16},{16,0},{1,17},{17,1},{2,18},{18,2},{3,19},{19,3},{4,20},{20... | collective-permute-start | bytes 884744 | tf_op jit(solution)/shard_map/ppermute | solution.py:164
  9.6 1.0 constant_dynamic-update-slice_fusion.1
  10.6 0.4 collective-permute-done.1
  11.0 7.1 %collective-permute-start.2 = (bf16[256,1152]{1,0:T(8,128)(2,1)S(1)}, bf16[256,1152]{1,0:T(8,128)(2,1)S(1)}, u32[]{:S(2)}, u32[]{:S(2)}) collective-permute-start(bf16[256,1152]{1,0:T(8,128)(2,1)S(1)} %constant_dynamic-update-slice_fusion), channel_id=1, source_target_pairs={{0,128},{32,160},{64,192},{96,224},{128,256},{160,288},{192,320},{... | collective-permute-start | bytes 1769480 | tf_op jit(solution)/shard_map/ppermute | solution.py:165
  18.1 0.0 copy-done
  18.1 0.0 copy-start.1
  18.1 1.3 %copy-done.1 = bf16[128,4608]{1,0:T(8,128)(2,1)S(1)} copy-done((bf16[128,4608]{1,0:T(8,128)(2,1)S(1)}, bf16[128,4608]{1,0:T(8,128)(2,1)}, u32[]{:S(2)}) %copy-start.1) | copy-done | bytes 1179672
  19.4 1.9 %grams.1 = (f32[16,8,128]{2,1,0:T(8,128)}, f32[288,128]{1,0:T(8,128)S(1)}) custom-call(s32[1]{0:T(128)} %bitcast.1.to_ref, bf16[128,1152]{1,0:T(8,128)(2,1)S(1)} %copy-done, bf16[128,4608]{1,0:T(8,128)(2,1)S(1)} %copy-done.1), custom_call_target="tpu_custom_call" | custom-call | flops 188743680 | bytes 1687556 | tf_op jit(solution)/shard_map/grams/pallas_call | solution.py:59
  21.3 6.8 %all-to-all-start = ((f32[16,8,128]{2,1,0:T(8,128)}), f32[16,8,128]{2,1,0:T(8,128)S(1)}, u32[]{:S(2)}, u32[]{:S(2)}) async-start(f32[16,8,128]{2,1,0:T(8,128)} %get-tuple-element.6), calls=%async_computation | async-start | bytes 131072 | tf_op jit(solution)/shard_map/all_to_all | solution.py:192
  28.7 3.8 %collective-permute-start.8 = (bf16[256,1152]{1,0:T(8,128)(2,1)S(1)}, bf16[256,1152]{1,0:T(8,128)(2,1)S(1)}, u32[]{:S(2)}, u32[]{:S(2)}) collective-permute-start(bf16[256,1152]{1,0:T(8,128)(2,1)S(1)} %constant_dynamic-update-slice_fusion), channel_id=1, source_target_pairs={{0,32},{32,64},{64,96},{96,128},{128,160},{160,192},{192,224},{224... | collective-permute-start | bytes 1769480 | tf_op jit(solution)/shard_map/ppermute | solution.py:166
  32.6 9.8 %collective-permute-done.2.refs_5_ = bf16[256,1152]{1,0:T(8,128)(2,1)S(1)} collective-permute-done((bf16[256,1152]{1,0:T(8,128)(2,1)S(1)}, bf16[256,1152]{1,0:T(8,128)(2,1)S(1)}, u32[]{:S(2)}, u32[]{:S(2)}) %collective-permute-start.2) | collective-permute-done | bytes 589856 | tf_op jit(solution)/shard_map/ppermute | solution.py:165
  42.4 5.5 %collective-permute-start.3 = (bf16[256,1152]{1,0:T(8,128)(2,1)S(1)}, bf16[256,1152]{1,0:T(8,128)(2,1)}, u32[]{:S(2)}, u32[]{:S(2)}) collective-permute-start(bf16[256,1152]{1,0:T(8,128)(2,1)S(1)} %collective-permute-done.2.refs_5_), channel_id=1, source_target_pairs={{0,32},{32,64},{64,96},{96,128},{128,160},{160,192},{192,224},{224... | collective-permute-start | bytes 1769480 | tf_op jit(solution)/shard_map/ppermute | solution.py:169
  47.8 0.0 all-to-all-done.parts_ref
  47.9 0.7 collective-permute-start
  48.6 2.8 %collective-permute-done.8.refs_2_ = bf16[256,1152]{1,0:T(8,128)(2,1)S(1)} collective-permute-done((bf16[256,1152]{1,0:T(8,128)(2,1)S(1)}, bf16[256,1152]{1,0:T(8,128)(2,1)S(1)}, u32[]{:S(2)}, u32[]{:S(2)}) %collective-permute-start.8) | collective-permute-done | bytes 589856 | tf_op jit(solution)/shard_map/ppermute | solution.py:166
  51.3 3.9 %collective-permute-start.9 = (bf16[256,1152]{1,0:T(8,128)(2,1)S(1)}, bf16[256,1152]{1,0:T(8,128)(2,1)}, u32[]{:S(2)}, u32[]{:S(2)}) collective-permute-start(bf16[256,1152]{1,0:T(8,128)(2,1)S(1)} %collective-permute-done.8.refs_2_), channel_id=1, source_target_pairs={{0,32},{32,64},{64,96},{96,128},{128,160},{160,192},{192,224},{224... | collective-permute-start | bytes 1769480 | tf_op jit(solution)/shard_map/ppermute | solution.py:169
  55.3 2.8 %collective-permute-done.3.refs_6_ = bf16[256,1152]{1,0:T(8,128)(2,1)} collective-permute-done((bf16[256,1152]{1,0:T(8,128)(2,1)S(1)}, bf16[256,1152]{1,0:T(8,128)(2,1)}, u32[]{:S(2)}, u32[]{:S(2)}) %collective-permute-start.3) | collective-permute-done | bytes 589856 | tf_op jit(solution)/shard_map/ppermute | solution.py:169
  58.1 3.6 %collective-permute-start.4 = (bf16[256,1152]{1,0:T(8,128)(2,1)}, bf16[256,1152]{1,0:T(8,128)(2,1)S(1)}, u32[]{:S(2)}, u32[]{:S(2)}) collective-permute-start(bf16[256,1152]{1,0:T(8,128)(2,1)} %collective-permute-done.3.refs_6_), channel_id=1, source_target_pairs={{0,32},{32,64},{64,96},{96,128},{128,160},{160,192},{192,224},{224... | collective-permute-start | bytes 1769480 | tf_op jit(solution)/shard_map/ppermute | solution.py:169
  61.7 0.0 collective-permute-done.block_ref
  61.7 1.2 %spread.1 = bf16[16,288,128]{2,1,0:T(8,128)(2,1)} custom-call(bf16[288,128]{1,0:T(8,128)(2,1)S(1)} %collective-permute-done.block_ref), custom_call_target="tpu_custom_call" | custom-call | flops 10000000000 | bytes 1253376 | tf_op jit(solution)/shard_map/spread/pallas_call | solution.py:59
  62.9 10.5 %all-to-all-start.1 = ((bf16[16,288,128]{2,1,0:T(8,128)(2,1)}), bf16[16,288,128]{2,1,0:T(8,128)(2,1)S(1)}, u32[]{:S(2)}, u32[]{:S(2)}) async-start(bf16[16,288,128]{2,1,0:T(8,128)(2,1)} %spread.1), calls=%async_computation.1 | async-start | bytes 2359296 | tf_op jit(solution)/shard_map/all_to_all | solution.py:196
  73.4 0.0 collective-permute-done.9.refs_3_
  73.4 1.9 %collective-permute-start.10 = (bf16[256,1152]{1,0:T(8,128)(2,1)}, bf16[256,1152]{1,0:T(8,128)(2,1)}, u32[]{:S(2)}, u32[]{:S(2)}) collective-permute-start(bf16[256,1152]{1,0:T(8,128)(2,1)} %collective-permute-done.9.refs_3_), channel_id=1, source_target_pairs={{0,32},{32,64},{64,96},{96,128},{128,160},{160,192},{192,224},{224... | collective-permute-start | bytes 1769480 | tf_op jit(solution)/shard_map/ppermute | solution.py:169
  75.4 0.0 collective-permute-done.4.refs_7_
  75.4 0.8 fusion
  76.1 3.2 %collective-permute-start.5 = (bf16[128,1152]{1,0:T(8,128)(2,1)S(1)}, bf16[128,1152]{1,0:T(8,128)(2,1)}, u32[]{:S(2)}, u32[]{:S(2)}) collective-permute-start(bf16[128,1152]{1,0:T(8,128)(2,1)S(1)} %get-tuple-element.11), channel_id=1, source_target_pairs={{0,32},{32,64},{64,96},{96,128},{128,160},{160,192},{192,224},{224... | collective-permute-start | bytes 884744 | tf_op jit(solution)/shard_map/ppermute | solution.py:172
  79.4 2.8 %collective-permute-start.7 = (bf16[128,1152]{1,0:T(8,128)(2,1)}, bf16[128,1152]{1,0:T(8,128)(2,1)}, u32[]{:S(2)}, u32[]{:S(2)}) collective-permute-start(bf16[128,1152]{1,0:T(8,128)(2,1)} %get-tuple-element.10), channel_id=1, source_target_pairs={{0,32},{32,64},{64,96},{96,128},{128,160},{160,192},{192,224},{224... | collective-permute-start | bytes 884744 | tf_op jit(solution)/shard_map/ppermute | solution.py:173
  82.2 5.7 %collective-permute-done.5.refs_1_ = bf16[128,1152]{1,0:T(8,128)(2,1)} collective-permute-done((bf16[128,1152]{1,0:T(8,128)(2,1)S(1)}, bf16[128,1152]{1,0:T(8,128)(2,1)}, u32[]{:S(2)}, u32[]{:S(2)}) %collective-permute-start.5) | collective-permute-done | bytes 294944 | tf_op jit(solution)/shard_map/ppermute | solution.py:172
  87.8 3.0 %collective-permute-start.6 = (bf16[128,1152]{1,0:T(8,128)(2,1)}, bf16[128,1152]{1,0:T(8,128)(2,1)S(1)}, u32[]{:S(2)}, u32[]{:S(2)}) collective-permute-start(bf16[128,1152]{1,0:T(8,128)(2,1)} %collective-permute-done.5.refs_1_), channel_id=1, source_target_pairs={{0,32},{32,64},{64,96},{96,128},{128,160},{160,192},{192,224},{224... | collective-permute-start | bytes 884744 | tf_op jit(solution)/shard_map/ppermute | solution.py:172
  90.9 0.0 all-to-all-done.1.refs_0_.s_ref
  90.9 0.0 collective-permute-done.10.refs_4_
  90.9 2.9 %products.2.refs_3_ = f32[288,1152]{1,0:T(8,128)S(1)} custom-call(bf16[16,288,128]{2,1,0:T(8,128)(2,1)S(1)} %all-to-all-done.1.refs_0_.s_ref, bf16[128,1152]{1,0:T(8,128)(2,1)S(1)} %copy-done, bf16[256,1152]{1,0:T(8,128)(2,1)S(1)} %collective-permute-done.8.refs_2_, bf16[256,1152]{1,0:T(8,128)(2,1)} %collective-permute-done.9.refs_3_, ...), custom_call_target="tpu_custom_call" | custom-call | flops 1189085184 | bytes 6340608 | tf_op jit(solution)/shard_map/products/pallas_call | solution.py:59
  93.8 0.0 collective-permute-done.7.refs_2_
  93.8 1.4 %products.3.refs_1_ = f32[288,1152]{1,0:T(8,128)S(1)} custom-call(bf16[16,288,128]{2,1,0:T(8,128)(2,1)S(1)} %all-to-all-done.1.refs_0_.s_ref, bf16[128,1152]{1,0:T(8,128)(2,1)} %collective-permute-done.5.refs_1_, bf16[128,1152]{1,0:T(8,128)(2,1)} %collective-permute-done.7.refs_2_, f32[288,1152]{1,0:T(8,128)S(1)} %products.2.refs_3_), custom_call_target="tpu_custom_call" | custom-call | flops 169869312 | bytes 4423680 | tf_op jit(solution)/shard_map/products/pallas_call | solution.py:59
  95.2 0.3 collective-permute-done.6.refs_0_
  95.5 0.2 last.3
  95.8 8.4 %collective-permute-start.11 = (f32[144,1152]{1,0:T(8,128)S(1)}, f32[144,1152]{1,0:T(8,128)S(1)}, u32[]{:S(2)}, u32[]{:S(2)}) collective-permute-start(f32[144,1152]{1,0:T(8,128)S(1)} %last.3), channel_id=1, source_target_pairs={{0,16},{16,0},{1,17},{17,1},{2,18},{18,2},{3,19},{19,3},{4,20},{20... | collective-permute-start | bytes 1990664 | tf_op jit(solution)/shard_map/ppermute | solution.py:202
  104.1 0.5 slice.11
  104.6 0.2 last.2
  104.9 0.9 collective-permute-done.11
  105.8 0.9 multiply_bitcast_fusion
  (2 shorter events, 0.1 us)
Async XLA Ops:
  0.6 17.5 %copy-start = (bf16[128,1152]{1,0:T(8,128)(2,1)S(1)}, bf16[128,1152]{1,0:T(8,128)(2,1)}, u32[]{:S(2)}) copy-start(bf16[128,1152]{1,0:T(8,128)(2,1)} %refs_1_.1) | copy-start | bytes 884740
  0.6 10.3 %collective-permute-start.1 = (bf16[128,1152]{1,0:T(8,128)(2,1)}, bf16[128,1152]{1,0:T(8,128)(2,1)S(1)}, u32[]{:S(2)}, u32[]{:S(2)}) collective-permute-start(bf16[128,1152]{1,0:T(8,128)(2,1)} %refs_1_.1), channel_id=1, source_target_pairs={{0,16},{16,0},{1,17},{17,1},{2,18},{18,2},{3,19},{19,3},{4,20},{20... | collective-permute-start | bytes 884744 | tf_op jit(solution)/shard_map/ppermute | solution.py:164
  11.0 31.4 %collective-permute-start.2 = (bf16[256,1152]{1,0:T(8,128)(2,1)S(1)}, bf16[256,1152]{1,0:T(8,128)(2,1)S(1)}, u32[]{:S(2)}, u32[]{:S(2)}) collective-permute-start(bf16[256,1152]{1,0:T(8,128)(2,1)S(1)} %constant_dynamic-update-slice_fusion), channel_id=1, source_target_pairs={{0,128},{32,160},{64,192},{96,224},{128,256},{160,288},{192,320},{... | collective-permute-start | bytes 1769480 | tf_op jit(solution)/shard_map/ppermute | solution.py:165
  18.1 1.3 %copy-start.1 = (bf16[128,4608]{1,0:T(8,128)(2,1)S(1)}, bf16[128,4608]{1,0:T(8,128)(2,1)}, u32[]{:S(2)}) copy-start(bf16[128,4608]{1,0:T(8,128)(2,1)} %g_hbm.1) | copy-start | bytes 3538948
  21.3 26.5 %all-to-all-start = ((f32[16,8,128]{2,1,0:T(8,128)}), f32[16,8,128]{2,1,0:T(8,128)S(1)}, u32[]{:S(2)}, u32[]{:S(2)}) async-start(f32[16,8,128]{2,1,0:T(8,128)} %get-tuple-element.6), calls=%async_computation | async-start | bytes 131072 | tf_op jit(solution)/shard_map/all_to_all | solution.py:192
  28.7 22.6 %collective-permute-start.8 = (bf16[256,1152]{1,0:T(8,128)(2,1)S(1)}, bf16[256,1152]{1,0:T(8,128)(2,1)S(1)}, u32[]{:S(2)}, u32[]{:S(2)}) collective-permute-start(bf16[256,1152]{1,0:T(8,128)(2,1)S(1)} %constant_dynamic-update-slice_fusion), channel_id=1, source_target_pairs={{0,32},{32,64},{64,96},{96,128},{128,160},{160,192},{192,224},{224... | collective-permute-start | bytes 1769480 | tf_op jit(solution)/shard_map/ppermute | solution.py:166
  42.4 15.7 %collective-permute-start.3 = (bf16[256,1152]{1,0:T(8,128)(2,1)S(1)}, bf16[256,1152]{1,0:T(8,128)(2,1)}, u32[]{:S(2)}, u32[]{:S(2)}) collective-permute-start(bf16[256,1152]{1,0:T(8,128)(2,1)S(1)} %collective-permute-done.2.refs_5_), channel_id=1, source_target_pairs={{0,32},{32,64},{64,96},{96,128},{128,160},{160,192},{192,224},{224... | collective-permute-start | bytes 1769480 | tf_op jit(solution)/shard_map/ppermute | solution.py:169
  47.9 13.8 %collective-permute-start = (bf16[288,128]{1,0:T(8,128)(2,1)S(1)}, bf16[288,128]{1,0:T(8,128)(2,1)S(1)}, u32[]{:S(2)}, u32[]{:S(2)}) collective-permute-start(bf16[288,128]{1,0:T(8,128)(2,1)S(1)} %get-tuple-element.8), channel_id=1, source_target_pairs={{0,0},{1,33},{2,66},{3,99},{4,132},{5,165},{6,198},{7,231},{8,264}... | collective-permute-start | bytes 221192 | tf_op jit(solution)/shard_map/ppermute | solution.py:194
  51.3 22.1 %collective-permute-start.9 = (bf16[256,1152]{1,0:T(8,128)(2,1)S(1)}, bf16[256,1152]{1,0:T(8,128)(2,1)}, u32[]{:S(2)}, u32[]{:S(2)}) collective-permute-start(bf16[256,1152]{1,0:T(8,128)(2,1)S(1)} %collective-permute-done.8.refs_2_), channel_id=1, source_target_pairs={{0,32},{32,64},{64,96},{96,128},{128,160},{160,192},{192,224},{224... | collective-permute-start | bytes 1769480 | tf_op jit(solution)/shard_map/ppermute | solution.py:169
  58.1 17.3 %collective-permute-start.4 = (bf16[256,1152]{1,0:T(8,128)(2,1)}, bf16[256,1152]{1,0:T(8,128)(2,1)S(1)}, u32[]{:S(2)}, u32[]{:S(2)}) collective-permute-start(bf16[256,1152]{1,0:T(8,128)(2,1)} %collective-permute-done.3.refs_6_), channel_id=1, source_target_pairs={{0,32},{32,64},{64,96},{96,128},{128,160},{160,192},{192,224},{224... | collective-permute-start | bytes 1769480 | tf_op jit(solution)/shard_map/ppermute | solution.py:169
  62.9 27.9 %all-to-all-start.1 = ((bf16[16,288,128]{2,1,0:T(8,128)(2,1)}), bf16[16,288,128]{2,1,0:T(8,128)(2,1)S(1)}, u32[]{:S(2)}, u32[]{:S(2)}) async-start(bf16[16,288,128]{2,1,0:T(8,128)(2,1)} %spread.1), calls=%async_computation.1 | async-start | bytes 2359296 | tf_op jit(solution)/shard_map/all_to_all | solution.py:196
  73.4 17.4 %collective-permute-start.10 = (bf16[256,1152]{1,0:T(8,128)(2,1)}, bf16[256,1152]{1,0:T(8,128)(2,1)}, u32[]{:S(2)}, u32[]{:S(2)}) collective-permute-start(bf16[256,1152]{1,0:T(8,128)(2,1)} %collective-permute-done.9.refs_3_), channel_id=1, source_target_pairs={{0,32},{32,64},{64,96},{96,128},{128,160},{160,192},{192,224},{224... | collective-permute-start | bytes 1769480 | tf_op jit(solution)/shard_map/ppermute | solution.py:169
  76.1 11.7 %collective-permute-start.5 = (bf16[128,1152]{1,0:T(8,128)(2,1)S(1)}, bf16[128,1152]{1,0:T(8,128)(2,1)}, u32[]{:S(2)}, u32[]{:S(2)}) collective-permute-start(bf16[128,1152]{1,0:T(8,128)(2,1)S(1)} %get-tuple-element.11), channel_id=1, source_target_pairs={{0,32},{32,64},{64,96},{96,128},{128,160},{160,192},{192,224},{224... | collective-permute-start | bytes 884744 | tf_op jit(solution)/shard_map/ppermute | solution.py:172
  79.4 14.4 %collective-permute-start.7 = (bf16[128,1152]{1,0:T(8,128)(2,1)}, bf16[128,1152]{1,0:T(8,128)(2,1)}, u32[]{:S(2)}, u32[]{:S(2)}) collective-permute-start(bf16[128,1152]{1,0:T(8,128)(2,1)} %get-tuple-element.10), channel_id=1, source_target_pairs={{0,32},{32,64},{64,96},{96,128},{128,160},{160,192},{192,224},{224... | collective-permute-start | bytes 884744 | tf_op jit(solution)/shard_map/ppermute | solution.py:173
  87.8 7.7 %collective-permute-start.6 = (bf16[128,1152]{1,0:T(8,128)(2,1)}, bf16[128,1152]{1,0:T(8,128)(2,1)S(1)}, u32[]{:S(2)}, u32[]{:S(2)}) collective-permute-start(bf16[128,1152]{1,0:T(8,128)(2,1)} %collective-permute-done.5.refs_1_), channel_id=1, source_target_pairs={{0,32},{32,64},{64,96},{96,128},{128,160},{160,192},{192,224},{224... | collective-permute-start | bytes 884744 | tf_op jit(solution)/shard_map/ppermute | solution.py:172
  95.8 10.1 %collective-permute-start.11 = (f32[144,1152]{1,0:T(8,128)S(1)}, f32[144,1152]{1,0:T(8,128)S(1)}, u32[]{:S(2)}, u32[]{:S(2)}) collective-permute-start(f32[144,1152]{1,0:T(8,128)S(1)} %last.3), channel_id=1, source_target_pairs={{0,16},{16,0},{1,17},{17,1},{2,18},{18,2},{3,19},{19,3},{4,20},{20... | collective-permute-start | bytes 1990664 | tf_op jit(solution)/shard_map/ppermute | solution.py:202

commit v6 on v5

--- a/solution.py
+++ b/solution.py
@@ -19,7 +19,7 @@
 LINE = ("z", "core")
 PLANE = ("y", "x")
 ALL = ("z", "core", "y", "x")
-JUMP = 4
+JUMP = 3
 
 
 def step_pairs(steps):
@@ -161,16 +161,21 @@
     t = lax.axis_index(PLANE)
     units = hidden.shape[1]
 
-    both = jnp.concatenate([hidden, lax.ppermute(hidden, "core", SWAP)], axis=0)
-    blocks = {0: hidden, JUMP: lax.ppermute(both, LINE, step_pairs(JUMP))}
-    blocks[1] = lax.ppermute(both, LINE, step_pairs(1))
-    for hop in range(2, 7):
-        if hop != JUMP:
-            blocks[hop] = lax.ppermute(blocks[hop - 1], LINE, step_pairs(1))
-    p, q = blocks[6][:SEQ], blocks[6][SEQ:]
-    for hop in range(7, HOPS + 1):
+    other = lax.ppermute(hidden, "core", SWAP)
+    both = jnp.concatenate([hidden, other], axis=0)
+    blocks = {0: hidden}
+    for hop in range(1, JUMP):
+        blocks[hop] = lax.ppermute(blocks[hop - 1] if hop > 1 else both, LINE, step_pairs(1))
+
+    p, q = lax.ppermute(hidden, LINE, step_pairs(JUMP)), lax.ppermute(other, LINE, step_pairs(JUMP))
+    blocks[JUMP] = (p, q)
+    for hop in range(JUMP + 1, HOPS + 1):
         p = lax.ppermute(p, LINE, step_pairs(1))
         q = lax.ppermute(q, LINE, step_pairs(1)) if hop < HOPS else None
+        if hop == 6:
+            p = after(p, cost=2000000000)
+        if hop == 6:
+            q = after(q, cost=4000000000)
         blocks[hop] = (p, q)
 
     to = lax.rem(z + (1 - 2 * core) * t + NZ, NZ).astype(jnp.int32).reshape(1)
@@ -195,8 +200,8 @@
     [spread] = call(spread_kernel, [jax.ShapeDtypeStruct((NT, CHIP, SEQ), jnp.bfloat16)], [block], "spread", 10000000000)
     s = lax.all_to_all(spread, PLANE, 0, 0, tiled=False)
 
-    acc = matmul(s, blocks, range(0, 7), None)
-    acc = matmul(s, blocks, range(7, HOPS), acc, 0)
+    acc = matmul(s, blocks, range(0, 4), None)
+    acc = matmul(s, blocks, range(4, HOPS), acc, 0)
     last = [(blocks[HOPS][0], HOPS)]
     row = core.astype(jnp.int32).reshape(1)
     theirs = lax.ppermute(last_products(1 - row, s, last, acc, 0), "core", SWAP)

time: 107 us -> 105 us (0.981)
  waiting for transfers between devices: 22.7 us -> 7.1 us
  starting transfers between devices: 70.1 us -> 83.5 us
  Pallas kernels: 7.96 us -> 6.79 us
    ppermute x7 -> x5, waiting for transfers between devices: 15.8 us -> 0.66 us  [the longest x1 0.65 us: per_device(): lax.ppermute(other, LINE, step_pairs(JUMP))]
    ppermute x2 -> x5, starting transfers between devices: 6.25 us -> 17.2 us  [per_device(): p = lax.ppermute(p, LINE, step_pairs(1))]
    ppermute x1 -> x4, starting transfers between devices: 2.78 us -> 12.1 us  [per_device(): q = lax.ppermute(q, LINE, step_pairs(1)) if hop < HOPS else None]
    ppermute x7 -> x5, starting transfers between devices: 34.8 us -> 27.2 us  [the longest x1 8.79 us: per_device(): other = lax.ppermute(hidden, 'core', SWAP)]
    pallas_call x7, Pallas kernels: 7.96 us -> 6.79 us  [call(): pl.pallas_call(kernel, out_shape=outs, in_specs=[smem() if a.dtype == jnp...]
    ppermute x2 -> x5, waiting for transfers between devices: 5.96 us -> 5.48 us  [per_device(): p = lax.ppermute(p, LINE, step_pairs(1))]
    unnamed x5 -> x18, local copies, waits for them, and re-layouts: 2.26 us -> 2.52 us
  transfers between devices with their start and end apart: 14 -> 18, of which waited for: 7 -> 4; matrix products, arithmetic and copies ran while one was open for 2% -> 1% of each run, Pallas kernels for 7% -> 6%
where the time goes in v6:
time: 105 us; the launch traced here: 104 us
  starting transfers between devices  83.5 us (80%)
  waiting for transfers between devices  7.1 us (7%)
  Pallas kernels  6.79 us (6%)
  local copies, waits for them, and re-layouts  3.03 us (3%)
  other arithmetic  1.77 us (2%)
  between operations  1.69 us (2%)
    ppermute x5, starting transfers between devices, per_device(): p = lax.ppermute(p, LINE, step_pairs(1))  17.2 us
    ppermute x4, starting transfers between devices, per_device(): q = lax.ppermute(q, LINE, step_pairs(1)) if hop < HOPS else None  12.1 us
    all_to_all x1, starting transfers between devices, per_device(): s = lax.all_to_all(spread, PLANE, 0, 0, tiled=False)  10.5 us
    ppermute x1, starting transfers between devices, per_device(): theirs = lax.ppermute(last_products(1 - row, s, last, acc, 0), 'core', SWAP)  8.97 us
    ppermute x1, starting transfers between devices, per_device(): other = lax.ppermute(hidden, 'core', SWAP)  8.79 us
    ppermute x2, starting transfers between devices, per_device(): lax.ppermute(blocks[hop - 1] if hop > 1 else both, LINE, step_pairs(1))  7 us
    pallas_call x7, Pallas kernels, call(): pl.pallas_call(kernel, out_shape=outs, in_specs=[smem() if a.dtype == jnp...  6.79 us
    all_to_all x1, starting transfers between devices, per_device(): parts = lax.all_to_all(part, PLANE, 0, 0, tiled=False)  6.77 us
  transfers between devices with their start and end apart: 18, of which 4 were waited for; matrix products, arithmetic and copies ran while one was open for 1% of the time, Pallas kernels for 6%

profile of v6, /device:TPU:1, one launch (start us, length us, event | category | flops | bytes accessed | tf_op | source)
XLA Modules:
  0.0 103.8 jit_solution(17827196143249942962)
XLA Ops:
  0.6 8.8 %collective-permute-start.7 = (bf16[128,1152]{1,0:T(8,128)(2,1)}, bf16[128,1152]{1,0:T(8,128)(2,1)S(1)}, u32[]{:S(2)}, u32[]{:S(2)}) collective-permute-start(bf16[128,1152]{1,0:T(8,128)(2,1)} %refs_1_.1), channel_id=1, source_target_pairs={{0,16},{16,0},{1,17},{17,1},{2,18},{18,2},{3,19},{19,3},{4,20},{20... | collective-permute-start | bytes 884744 | tf_op jit(solution)/shard_map/ppermute | solution.py:164
  9.4 6.6 %collective-permute-start.1 = (bf16[128,1152]{1,0:T(8,128)(2,1)}, bf16[128,1152]{1,0:T(8,128)(2,1)S(1)}, u32[]{:S(2)}, u32[]{:S(2)}) collective-permute-start(bf16[128,1152]{1,0:T(8,128)(2,1)} %refs_1_.1), channel_id=1, source_target_pairs={{0,96},{32,128},{64,160},{96,192},{128,224},{160,256},{192,288},{2... | collective-permute-start | bytes 884744 | tf_op jit(solution)/shard_map/ppermute | solution.py:170
  16.1 0.0 collective-permute-done.7
  16.1 4.7 %collective-permute-start.8 = (bf16[128,1152]{1,0:T(8,128)(2,1)S(1)}, bf16[128,1152]{1,0:T(8,128)(2,1)S(1)}, u32[]{:S(2)}, u32[]{:S(2)}) collective-permute-start(bf16[128,1152]{1,0:T(8,128)(2,1)S(1)} %collective-permute-done.7), channel_id=1, source_target_pairs={{0,96},{32,128},{64,160},{96,192},{128,224},{160,256},{192,288},{2... | collective-permute-start | bytes 884744 | tf_op jit(solution)/shard_map/ppermute | solution.py:170
  20.8 0.0 copy-start
  20.9 1.0 copy-done
  21.8 1.3 %copy-done.2 = bf16[128,4608]{1,0:T(8,128)(2,1)S(1)} copy-done((bf16[128,4608]{1,0:T(8,128)(2,1)S(1)}, bf16[128,4608]{1,0:T(8,128)(2,1)}, u32[]{:S(2)}) %copy-start.2) | copy-done | bytes 1179672
  23.1 1.9 %grams.1 = (f32[16,8,128]{2,1,0:T(8,128)}, f32[288,128]{1,0:T(8,128)S(1)}) custom-call(s32[1]{0:T(128)} %bitcast.1.to_ref, bf16[128,1152]{1,0:T(8,128)(2,1)S(1)} %copy-done, bf16[128,4608]{1,0:T(8,128)(2,1)S(1)} %copy-done.2), custom_call_target="tpu_custom_call" | custom-call | flops 188743680 | bytes 1687556 | tf_op jit(solution)/shard_map/grams/pallas_call | solution.py:59
  25.0 6.8 %all-to-all-start = ((f32[16,8,128]{2,1,0:T(8,128)}), f32[16,8,128]{2,1,0:T(8,128)S(1)}, u32[]{:S(2)}, u32[]{:S(2)}) async-start(f32[16,8,128]{2,1,0:T(8,128)} %get-tuple-element.6), calls=%async_computation | async-start | bytes 131072 | tf_op jit(solution)/shard_map/all_to_all | solution.py:197
  32.4 0.0 collective-permute-done.1.refs_4_
  32.4 2.6 %collective-permute-start.2 = (bf16[128,1152]{1,0:T(8,128)(2,1)S(1)}, bf16[128,1152]{1,0:T(8,128)(2,1)S(1)}, u32[]{:S(2)}, u32[]{:S(2)}) collective-permute-start(bf16[128,1152]{1,0:T(8,128)(2,1)S(1)} %collective-permute-done.1.refs_4_), channel_id=1, source_target_pairs={{0,32},{32,64},{64,96},{96,128},{128,160},{160,192},{192,224},{224... | collective-permute-start | bytes 884744 | tf_op jit(solution)/shard_map/ppermute | solution.py:173
  35.1 0.7 collective-permute-done.8.refs_5_
  35.7 2.9 %collective-permute-start.9 = (bf16[128,1152]{1,0:T(8,128)(2,1)S(1)}, bf16[128,1152]{1,0:T(8,128)(2,1)S(1)}, u32[]{:S(2)}, u32[]{:S(2)}) collective-permute-start(bf16[128,1152]{1,0:T(8,128)(2,1)S(1)} %collective-permute-done.8.refs_5_), channel_id=1, source_target_pairs={{0,32},{32,64},{64,96},{96,128},{128,160},{160,192},{192,224},{224... | collective-permute-start | bytes 884744 | tf_op jit(solution)/shard_map/ppermute | solution.py:174
  38.7 0.0 all-to-all-done.parts_ref
  38.7 0.0 copy-start.1
  38.7 0.8 collective-permute-start
  39.5 0.1 copy-done.1
  39.6 0.9 pad_maximum_fusion
  40.5 4.8 %collective-permute-start.13 = (bf16[256,1152]{1,0:T(8,128)(2,1)}, bf16[256,1152]{1,0:T(8,128)(2,1)S(1)}, u32[]{:S(2)}, u32[]{:S(2)}) collective-permute-start(bf16[256,1152]{1,0:T(8,128)(2,1)} %pad_maximum_fusion), channel_id=1, source_target_pairs={{0,32},{32,64},{64,96},{96,128},{128,160},{160,192},{192,224},{224... | collective-permute-start | bytes 1769480 | tf_op jit(solution)/shard_map/ppermute | solution.py:168
  45.3 0.0 collective-permute-done.2.refs_1_
  45.3 3.6 %collective-permute-start.3 = (bf16[128,1152]{1,0:T(8,128)(2,1)S(1)}, bf16[128,1152]{1,0:T(8,128)(2,1)}, u32[]{:S(2)}, u32[]{:S(2)}) collective-permute-start(bf16[128,1152]{1,0:T(8,128)(2,1)S(1)} %collective-permute-done.2.refs_1_), channel_id=1, source_target_pairs={{0,32},{32,64},{64,96},{96,128},{128,160},{160,192},{192,224},{224... | collective-permute-start | bytes 884744 | tf_op jit(solution)/shard_map/ppermute | solution.py:173
  49.0 2.0 %collective-permute-start.10 = (bf16[128,1152]{1,0:T(8,128)(2,1)S(1)}, bf16[128,1152]{1,0:T(8,128)(2,1)}, u32[]{:S(2)}, u32[]{:S(2)}) collective-permute-start(bf16[128,1152]{1,0:T(8,128)(2,1)S(1)} %collective-permute-done.9.refs_2_), channel_id=1, source_target_pairs={{0,32},{32,64},{64,96},{96,128},{128,160},{160,192},{192,224},{224... | collective-permute-start | bytes 884744 | tf_op jit(solution)/shard_map/ppermute | solution.py:174
  51.0 1.2 %spread.1 = bf16[16,288,128]{2,1,0:T(8,128)(2,1)} custom-call(bf16[288,128]{1,0:T(8,128)(2,1)S(1)} %collective-permute-done.block_ref), custom_call_target="tpu_custom_call" | custom-call | flops 10000000000 | bytes 1253376 | tf_op jit(solution)/shard_map/spread/pallas_call | solution.py:59
  52.2 10.5 %all-to-all-start.1 = ((bf16[16,288,128]{2,1,0:T(8,128)(2,1)}), bf16[16,288,128]{2,1,0:T(8,128)(2,1)S(1)}, u32[]{:S(2)}, u32[]{:S(2)}) async-start(bf16[16,288,128]{2,1,0:T(8,128)(2,1)} %spread.1), calls=%async_computation.1 | async-start | bytes 2359296 | tf_op jit(solution)/shard_map/all_to_all | solution.py:201
  62.7 3.2 %collective-permute-start.4 = (bf16[128,1152]{1,0:T(8,128)(2,1)}, bf16[128,1152]{1,0:T(8,128)(2,1)S(1)}, u32[]{:S(2)}, u32[]{:S(2)}) collective-permute-start(bf16[128,1152]{1,0:T(8,128)(2,1)} %collective-permute-done.3.refs_3_), channel_id=1, source_target_pairs={{0,32},{32,64},{64,96},{96,128},{128,160},{160,192},{192,224},{224... | collective-permute-start | bytes 884744 | tf_op jit(solution)/shard_map/ppermute | solution.py:173
  66.0 0.0 collective-permute-done.10.refs_4_
  66.0 3.6 %collective-permute-start.11 = (bf16[128,1152]{1,0:T(8,128)(2,1)}, bf16[128,1152]{1,0:T(8,128)(2,1)}, u32[]{:S(2)}, u32[]{:S(2)}) collective-permute-start(bf16[128,1152]{1,0:T(8,128)(2,1)} %collective-permute-done.10.refs_4_), channel_id=1, source_target_pairs={{0,32},{32,64},{64,96},{96,128},{128,160},{160,192},{192,224},{224... | collective-permute-start | bytes 884744 | tf_op jit(solution)/shard_map/ppermute | solution.py:174
  69.6 0.0 collective-permute-done.13.refs_2_
  69.6 2.2 %collective-permute-start.14 = (bf16[256,1152]{1,0:T(8,128)(2,1)S(1)}, bf16[256,1152]{1,0:T(8,128)(2,1)S(1)}, u32[]{:S(2)}, u32[]{:S(2)}) collective-permute-start(bf16[256,1152]{1,0:T(8,128)(2,1)S(1)} %collective-permute-done.13.refs_2_), channel_id=1, source_target_pairs={{0,32},{32,64},{64,96},{96,128},{128,160},{160,192},{192,224},{224... | collective-permute-start | bytes 1769480 | tf_op jit(solution)/shard_map/ppermute | solution.py:168
  71.8 0.0 copy-start.7
  71.8 3.3 %collective-permute-start.5 = (bf16[128,1152]{1,0:T(8,128)(2,1)S(1)}, bf16[128,1152]{1,0:T(8,128)(2,1)}, u32[]{:S(2)}, u32[]{:S(2)}) collective-permute-start(bf16[128,1152]{1,0:T(8,128)(2,1)S(1)} %after.2.refs_5_), channel_id=1, source_target_pairs={{0,32},{32,64},{64,96},{96,128},{128,160},{160,192},{192,224},{224... | collective-permute-start | bytes 884744 | tf_op jit(solution)/shard_map/ppermute | solution.py:173
  75.2 3.6 %collective-permute-start.12 = (bf16[128,1152]{1,0:T(8,128)(2,1)}, bf16[128,1152]{1,0:T(8,128)(2,1)}, u32[]{:S(2)}, u32[]{:S(2)}) collective-permute-start(bf16[128,1152]{1,0:T(8,128)(2,1)} %after.3.refs_6_), channel_id=1, source_target_pairs={{0,32},{32,64},{64,96},{96,128},{128,160},{160,192},{192,224},{224... | collective-permute-start | bytes 884744 | tf_op jit(solution)/shard_map/ppermute | solution.py:174
  78.7 4.9 %collective-permute-done.5.refs_7_ = bf16[128,1152]{1,0:T(8,128)(2,1)} collective-permute-done((bf16[128,1152]{1,0:T(8,128)(2,1)S(1)}, bf16[128,1152]{1,0:T(8,128)(2,1)}, u32[]{:S(2)}, u32[]{:S(2)}) %collective-permute-start.5) | collective-permute-done | bytes 294944 | tf_op jit(solution)/shard_map/ppermute | solution.py:173
  83.7 4.4 %collective-permute-start.6 = (bf16[128,1152]{1,0:T(8,128)(2,1)}, bf16[128,1152]{1,0:T(8,128)(2,1)S(1)}, u32[]{:S(2)}, u32[]{:S(2)}) collective-permute-start(bf16[128,1152]{1,0:T(8,128)(2,1)} %collective-permute-done.5.refs_7_), channel_id=1, source_target_pairs={{0,32},{32,64},{64,96},{96,128},{128,160},{160,192},{192,224},{224... | collective-permute-start | bytes 884744 | tf_op jit(solution)/shard_map/ppermute | solution.py:173
  88.1 0.0 copy-start.8
  88.1 0.0 collective-permute-done.14.refs_3_
  88.1 0.9 products.2.refs_9_
  89.0 0.0 collective-permute-done.12.refs_8_
  89.0 0.1 copy-done.6
  89.1 0.1 copy-done.8
  89.2 2.2 %products.3.refs_1_ = f32[288,1152]{1,0:T(8,128)S(1)} custom-call(bf16[16,288,128]{2,1,0:T(8,128)(2,1)S(1)} %all-to-all-done.1.refs_0_.s_ref, bf16[128,1152]{1,0:T(8,128)(2,1)S(1)} %copy-done.4, bf16[128,1152]{1,0:T(8,128)(2,1)S(1)} %copy-done.6, bf16[128,1152]{1,0:T(8,128)(2,1)} %collective-permute-done.3.refs_3_, ...), custom_call_target="tpu_custom_call" | custom-call | flops 679477248 | bytes 6193152 | tf_op jit(solution)/shard_map/products/pallas_call | solution.py:59
  91.4 0.6 collective-permute-done.6.refs_0_
  92.0 0.2 last.3
  92.2 9.0 %collective-permute-start.15 = (f32[144,1152]{1,0:T(8,128)S(1)}, f32[144,1152]{1,0:T(8,128)S(1)}, u32[]{:S(2)}, u32[]{:S(2)}) collective-permute-start(f32[144,1152]{1,0:T(8,128)S(1)} %last.3), channel_id=1, source_target_pairs={{0,16},{16,0},{1,17},{17,1},{2,18},{18,2},{3,19},{19,3},{4,20},{20... | collective-permute-start | bytes 1990664 | tf_op jit(solution)/shard_map/ppermute | solution.py:207
  101.2 0.5 slice.3
  101.7 0.2 last.2
  102.0 0.9 collective-permute-done.15
  102.9 0.9 multiply_bitcast_fusion
  (18 shorter events, 0.1 us)
Async XLA Ops:
  0.6 15.4 %collective-permute-start.7 = (bf16[128,1152]{1,0:T(8,128)(2,1)}, bf16[128,1152]{1,0:T(8,128)(2,1)S(1)}, u32[]{:S(2)}, u32[]{:S(2)}) collective-permute-start(bf16[128,1152]{1,0:T(8,128)(2,1)} %refs_1_.1), channel_id=1, source_target_pairs={{0,16},{16,0},{1,17},{17,1},{2,18},{18,2},{3,19},{19,3},{4,20},{20... | collective-permute-start | bytes 884744 | tf_op jit(solution)/shard_map/ppermute | solution.py:164
  9.4 23.0 %collective-permute-start.1 = (bf16[128,1152]{1,0:T(8,128)(2,1)}, bf16[128,1152]{1,0:T(8,128)(2,1)S(1)}, u32[]{:S(2)}, u32[]{:S(2)}) collective-permute-start(bf16[128,1152]{1,0:T(8,128)(2,1)} %refs_1_.1), channel_id=1, source_target_pairs={{0,96},{32,128},{64,160},{96,192},{128,224},{160,256},{192,288},{2... | collective-permute-start | bytes 884744 | tf_op jit(solution)/shard_map/ppermute | solution.py:170
  16.1 19.6 %collective-permute-start.8 = (bf16[128,1152]{1,0:T(8,128)(2,1)S(1)}, bf16[128,1152]{1,0:T(8,128)(2,1)S(1)}, u32[]{:S(2)}, u32[]{:S(2)}) collective-permute-start(bf16[128,1152]{1,0:T(8,128)(2,1)S(1)} %collective-permute-done.7), channel_id=1, source_target_pairs={{0,96},{32,128},{64,160},{96,192},{128,224},{160,256},{192,288},{2... | collective-permute-start | bytes 884744 | tf_op jit(solution)/shard_map/ppermute | solution.py:170
  20.8 1.0 copy-start
  21.8 1.3 %copy-start.2 = (bf16[128,4608]{1,0:T(8,128)(2,1)S(1)}, bf16[128,4608]{1,0:T(8,128)(2,1)}, u32[]{:S(2)}) copy-start(bf16[128,4608]{1,0:T(8,128)(2,1)} %g_hbm.1) | copy-start | bytes 3538948
  25.0 13.6 %all-to-all-start = ((f32[16,8,128]{2,1,0:T(8,128)}), f32[16,8,128]{2,1,0:T(8,128)S(1)}, u32[]{:S(2)}, u32[]{:S(2)}) async-start(f32[16,8,128]{2,1,0:T(8,128)} %get-tuple-element.6), calls=%async_computation | async-start | bytes 131072 | tf_op jit(solution)/shard_map/all_to_all | solution.py:197
  32.4 12.9 %collective-permute-start.2 = (bf16[128,1152]{1,0:T(8,128)(2,1)S(1)}, bf16[128,1152]{1,0:T(8,128)(2,1)S(1)}, u32[]{:S(2)}, u32[]{:S(2)}) collective-permute-start(bf16[128,1152]{1,0:T(8,128)(2,1)S(1)} %collective-permute-done.1.refs_4_), channel_id=1, source_target_pairs={{0,32},{32,64},{64,96},{96,128},{128,160},{160,192},{192,224},{224... | collective-permute-start | bytes 884744 | tf_op jit(solution)/shard_map/ppermute | solution.py:173
  35.7 13.2 %collective-permute-start.9 = (bf16[128,1152]{1,0:T(8,128)(2,1)S(1)}, bf16[128,1152]{1,0:T(8,128)(2,1)S(1)}, u32[]{:S(2)}, u32[]{:S(2)}) collective-permute-start(bf16[128,1152]{1,0:T(8,128)(2,1)S(1)} %collective-permute-done.8.refs_5_), channel_id=1, source_target_pairs={{0,32},{32,64},{64,96},{96,128},{128,160},{160,192},{192,224},{224... | collective-permute-start | bytes 884744 | tf_op jit(solution)/shard_map/ppermute | solution.py:174
  38.7 1.0 copy-start.1
  38.7 12.3 %collective-permute-start = (bf16[288,128]{1,0:T(8,128)(2,1)S(1)}, bf16[288,128]{1,0:T(8,128)(2,1)S(1)}, u32[]{:S(2)}, u32[]{:S(2)}) collective-permute-start(bf16[288,128]{1,0:T(8,128)(2,1)S(1)} %get-tuple-element.8), channel_id=1, source_target_pairs={{0,0},{1,33},{2,66},{3,99},{4,132},{5,165},{6,198},{7,231},{8,264}... | collective-permute-start | bytes 221192 | tf_op jit(solution)/shard_map/ppermute | solution.py:199
  40.5 29.1 %collective-permute-start.13 = (bf16[256,1152]{1,0:T(8,128)(2,1)}, bf16[256,1152]{1,0:T(8,128)(2,1)S(1)}, u32[]{:S(2)}, u32[]{:S(2)}) collective-permute-start(bf16[256,1152]{1,0:T(8,128)(2,1)} %pad_maximum_fusion), channel_id=1, source_target_pairs={{0,32},{32,64},{64,96},{96,128},{128,160},{160,192},{192,224},{224... | collective-permute-start | bytes 1769480 | tf_op jit(solution)/shard_map/ppermute | solution.py:168
  45.3 6.9 %copy-start.3 = (bf16[128,1152]{1,0:T(8,128)(2,1)}, bf16[128,1152]{1,0:T(8,128)(2,1)S(1)}, u32[]{:S(2)}) copy-start(bf16[128,1152]{1,0:T(8,128)(2,1)S(1)} %collective-permute-done.2.refs_1_) | copy-start | bytes 884740
  45.3 17.4 %collective-permute-start.3 = (bf16[128,1152]{1,0:T(8,128)(2,1)S(1)}, bf16[128,1152]{1,0:T(8,128)(2,1)}, u32[]{:S(2)}, u32[]{:S(2)}) collective-permute-start(bf16[128,1152]{1,0:T(8,128)(2,1)S(1)} %collective-permute-done.2.refs_1_), channel_id=1, source_target_pairs={{0,32},{32,64},{64,96},{96,128},{128,160},{160,192},{192,224},{224... | collective-permute-start | bytes 884744 | tf_op jit(solution)/shard_map/ppermute | solution.py:173
  49.0 3.3 %copy-start.5 = (bf16[128,1152]{1,0:T(8,128)(2,1)}, bf16[128,1152]{1,0:T(8,128)(2,1)S(1)}, u32[]{:S(2)}) copy-start(bf16[128,1152]{1,0:T(8,128)(2,1)S(1)} %collective-permute-done.9.refs_2_) | copy-start | bytes 884740
  49.0 17.0 %collective-permute-start.10 = (bf16[128,1152]{1,0:T(8,128)(2,1)S(1)}, bf16[128,1152]{1,0:T(8,128)(2,1)}, u32[]{:S(2)}, u32[]{:S(2)}) collective-permute-start(bf16[128,1152]{1,0:T(8,128)(2,1)S(1)} %collective-permute-done.9.refs_2_), channel_id=1, source_target_pairs={{0,32},{32,64},{64,96},{96,128},{128,160},{160,192},{192,224},{224... | collective-permute-start | bytes 884744 | tf_op jit(solution)/shard_map/ppermute | solution.py:174
  52.2 35.8 %all-to-all-start.1 = ((bf16[16,288,128]{2,1,0:T(8,128)(2,1)}), bf16[16,288,128]{2,1,0:T(8,128)(2,1)S(1)}, u32[]{:S(2)}, u32[]{:S(2)}) async-start(bf16[16,288,128]{2,1,0:T(8,128)(2,1)} %spread.1), calls=%async_computation.1 | async-start | bytes 2359296 | tf_op jit(solution)/shard_map/all_to_all | solution.py:201
  62.7 9.1 %collective-permute-start.4 = (bf16[128,1152]{1,0:T(8,128)(2,1)}, bf16[128,1152]{1,0:T(8,128)(2,1)S(1)}, u32[]{:S(2)}, u32[]{:S(2)}) collective-permute-start(bf16[128,1152]{1,0:T(8,128)(2,1)} %collective-permute-done.3.refs_3_), channel_id=1, source_target_pairs={{0,32},{32,64},{64,96},{96,128},{128,160},{160,192},{192,224},{224... | collective-permute-start | bytes 884744 | tf_op jit(solution)/shard_map/ppermute | solution.py:173
  66.0 9.2 %collective-permute-start.11 = (bf16[128,1152]{1,0:T(8,128)(2,1)}, bf16[128,1152]{1,0:T(8,128)(2,1)}, u32[]{:S(2)}, u32[]{:S(2)}) collective-permute-start(bf16[128,1152]{1,0:T(8,128)(2,1)} %collective-permute-done.10.refs_4_), channel_id=1, source_target_pairs={{0,32},{32,64},{64,96},{96,128},{128,160},{160,192},{192,224},{224... | collective-permute-start | bytes 884744 | tf_op jit(solution)/shard_map/ppermute | solution.py:174
  69.6 18.5 %collective-permute-start.14 = (bf16[256,1152]{1,0:T(8,128)(2,1)S(1)}, bf16[256,1152]{1,0:T(8,128)(2,1)S(1)}, u32[]{:S(2)}, u32[]{:S(2)}) collective-permute-start(bf16[256,1152]{1,0:T(8,128)(2,1)S(1)} %collective-permute-done.13.refs_2_), channel_id=1, source_target_pairs={{0,32},{32,64},{64,96},{96,128},{128,160},{160,192},{192,224},{224... | collective-permute-start | bytes 1769480 | tf_op jit(solution)/shard_map/ppermute | solution.py:168
  71.8 3.4 %copy-start.7 = (bf16[128,1152]{1,0:T(8,128)(2,1)}, bf16[128,1152]{1,0:T(8,128)(2,1)S(1)}, u32[]{:S(2)}) copy-start(bf16[128,1152]{1,0:T(8,128)(2,1)S(1)} %after.2.refs_5_) | copy-start | bytes 884740
  71.8 11.9 %collective-permute-start.5 = (bf16[128,1152]{1,0:T(8,128)(2,1)S(1)}, bf16[128,1152]{1,0:T(8,128)(2,1)}, u32[]{:S(2)}, u32[]{:S(2)}) collective-permute-start(bf16[128,1152]{1,0:T(8,128)(2,1)S(1)} %after.2.refs_5_), channel_id=1, source_target_pairs={{0,32},{32,64},{64,96},{96,128},{128,160},{160,192},{192,224},{224... | collective-permute-start | bytes 884744 | tf_op jit(solution)/shard_map/ppermute | solution.py:173
  75.2 13.8 %collective-permute-start.12 = (bf16[128,1152]{1,0:T(8,128)(2,1)}, bf16[128,1152]{1,0:T(8,128)(2,1)}, u32[]{:S(2)}, u32[]{:S(2)}) collective-permute-start(bf16[128,1152]{1,0:T(8,128)(2,1)} %after.3.refs_6_), channel_id=1, source_target_pairs={{0,32},{32,64},{64,96},{96,128},{128,160},{160,192},{192,224},{224... | collective-permute-start | bytes 884744 | tf_op jit(solution)/shard_map/ppermute | solution.py:174
  83.7 8.3 %collective-permute-start.6 = (bf16[128,1152]{1,0:T(8,128)(2,1)}, bf16[128,1152]{1,0:T(8,128)(2,1)S(1)}, u32[]{:S(2)}, u32[]{:S(2)}) collective-permute-start(bf16[128,1152]{1,0:T(8,128)(2,1)} %collective-permute-done.5.refs_7_), channel_id=1, source_target_pairs={{0,32},{32,64},{64,96},{96,128},{128,160},{160,192},{192,224},{224... | collective-permute-start | bytes 884744 | tf_op jit(solution)/shard_map/ppermute | solution.py:173
  88.0 1.0 copy-start.4
  88.1 1.0 %copy-start.6 = (bf16[128,1152]{1,0:T(8,128)(2,1)S(1)}, bf16[128,1152]{1,0:T(8,128)(2,1)}, u32[]{:S(2)}) copy-start(bf16[128,1152]{1,0:T(8,128)(2,1)} %copy-done.5) | copy-start | bytes 884740
  88.1 1.1 %copy-start.8 = (bf16[128,1152]{1,0:T(8,128)(2,1)S(1)}, bf16[128,1152]{1,0:T(8,128)(2,1)}, u32[]{:S(2)}) copy-start(bf16[128,1152]{1,0:T(8,128)(2,1)} %copy-done.7) | copy-start | bytes 884740
  92.2 10.7 %collective-permute-start.15 = (f32[144,1152]{1,0:T(8,128)S(1)}, f32[144,1152]{1,0:T(8,128)S(1)}, u32[]{:S(2)}, u32[]{:S(2)}) collective-permute-start(f32[144,1152]{1,0:T(8,128)S(1)} %last.3), channel_id=1, source_target_pairs={{0,16},{16,0},{1,17},{17,1},{2,18},{18,2},{3,19},{19,3},{4,20},{20... | collective-permute-start | bytes 1990664 | tf_op jit(solution)/shard_map/ppermute | solution.py:207

commit v7 on v6

--- a/solution.py
+++ b/solution.py
@@ -173,9 +173,7 @@
         p = lax.ppermute(p, LINE, step_pairs(1))
         q = lax.ppermute(q, LINE, step_pairs(1)) if hop < HOPS else None
         if hop == 6:
-            p = after(p, cost=2000000000)
-        if hop == 6:
-            q = after(q, cost=4000000000)
+            p, q = after(p, blocks[2], cost=2000000000), after(q, cost=4000000000)
         blocks[hop] = (p, q)
 
     to = lax.rem(z + (1 - 2 * core) * t + NZ, NZ).astype(jnp.int32).reshape(1)

time: 105 us -> 103 us (0.981)
  starting transfers between devices: 83.5 us -> 80.7 us
  waiting for transfers between devices: 7.1 us -> 9.62 us
    ppermute x5, waiting for transfers between devices: 5.48 us -> 8.64 us  [per_device(): p = lax.ppermute(p, LINE, step_pairs(1))]
    all_to_all x1, starting transfers between devices: 10.5 us -> 8.7 us  [per_device(): s = lax.all_to_all(spread, PLANE, 0, 0, tiled=False)]
    ppermute x4, starting transfers between devices: 12.1 us -> 10.6 us  [per_device(): q = lax.ppermute(q, LINE, step_pairs(1)) if hop < HOPS else None]
    ppermute x5, starting transfers between devices: 17.2 us -> 18.6 us  [per_device(): p = lax.ppermute(p, LINE, step_pairs(1))]
    unnamed x18 -> x14, local copies, waits for them, and re-layouts: 2.52 us -> 2.35 us
  transfers between devices with their start and end apart: 18 -> 18, of which waited for: 4 -> 5; matrix products, arithmetic and copies ran while one was open for 1% -> 1% of each run, Pallas kernels for 6% -> 6%
where the time goes in v7:
time: 103 us
  starting transfers between devices  80.7 us (78%)
  waiting for transfers between devices  9.62 us (9%)
  Pallas kernels  6.9 us (7%)
  local copies, waits for them, and re-layouts  2.86 us (3%)
  between operations  1.64 us (2%)
    ppermute x5, starting transfers between devices, per_device(): p = lax.ppermute(p, LINE, step_pairs(1))  18.6 us
    ppermute x4, starting transfers between devices, per_device(): q = lax.ppermute(q, LINE, step_pairs(1)) if hop < HOPS else None  10.6 us
    ppermute x1, starting transfers between devices, per_device(): theirs = lax.ppermute(last_products(1 - row, s, last, acc, 0), 'core', SWAP)  9.13 us
    ppermute x1, starting transfers between devices, per_device(): other = lax.ppermute(hidden, 'core', SWAP)  8.79 us
    all_to_all x1, starting transfers between devices, per_device(): s = lax.all_to_all(spread, PLANE, 0, 0, tiled=False)  8.7 us
    ppermute x5, waiting for transfers between devices, per_device(): p = lax.ppermute(p, LINE, step_pairs(1))  8.64 us
    pallas_call x7, Pallas kernels, call(): pl.pallas_call(kernel, out_shape=outs, in_specs=[smem() if a.dtype == jnp...  6.9 us
    all_to_all x1, starting transfers between devices, per_device(): parts = lax.all_to_all(part, PLANE, 0, 0, tiled=False)  6.77 us
  transfers between devices with their start and end apart: 18, of which 5 were waited for; matrix products, arithmetic and copies ran while one was open for 1% of the time, Pallas kernels for 6%

profile of v7, /device:TPU:1, one launch (start us, length us, event | category | flops | bytes accessed | tf_op | source)
XLA Modules:
  0.0 102.7 jit_solution(10408094223026118092)
XLA Ops:
  0.6 8.8 %collective-permute-start.5 = (bf16[128,1152]{1,0:T(8,128)(2,1)}, bf16[128,1152]{1,0:T(8,128)(2,1)S(1)}, u32[]{:S(2)}, u32[]{:S(2)}) collective-permute-start(bf16[128,1152]{1,0:T(8,128)(2,1)} %refs_1_.1), channel_id=1, source_target_pairs={{0,16},{16,0},{1,17},{17,1},{2,18},{18,2},{3,19},{19,3},{4,20},{20... | collective-permute-start | bytes 884744 | tf_op jit(solution)/shard_map/ppermute | solution.py:164
  9.4 6.6 %collective-permute-start.1 = (bf16[128,1152]{1,0:T(8,128)(2,1)}, bf16[128,1152]{1,0:T(8,128)(2,1)S(1)}, u32[]{:S(2)}, u32[]{:S(2)}) collective-permute-start(bf16[128,1152]{1,0:T(8,128)(2,1)} %refs_1_.1), channel_id=1, source_target_pairs={{0,96},{32,128},{64,160},{96,192},{128,224},{160,256},{192,288},{2... | collective-permute-start | bytes 884744 | tf_op jit(solution)/shard_map/ppermute | solution.py:170
  16.1 0.0 collective-permute-done.5
  16.1 4.7 %collective-permute-start.10 = (bf16[128,1152]{1,0:T(8,128)(2,1)S(1)}, bf16[128,1152]{1,0:T(8,128)(2,1)S(1)}, u32[]{:S(2)}, u32[]{:S(2)}) collective-permute-start(bf16[128,1152]{1,0:T(8,128)(2,1)S(1)} %collective-permute-done.5), channel_id=1, source_target_pairs={{0,96},{32,128},{64,160},{96,192},{128,224},{160,256},{192,288},{2... | collective-permute-start | bytes 884744 | tf_op jit(solution)/shard_map/ppermute | solution.py:170
  20.8 1.0 copy-done
  21.8 1.3 %copy-done.2 = bf16[128,4608]{1,0:T(8,128)(2,1)S(1)} copy-done((bf16[128,4608]{1,0:T(8,128)(2,1)S(1)}, bf16[128,4608]{1,0:T(8,128)(2,1)}, u32[]{:S(2)}) %copy-start.2) | copy-done | bytes 1179672
  23.1 1.9 %grams.1 = (f32[16,8,128]{2,1,0:T(8,128)}, f32[288,128]{1,0:T(8,128)S(1)}) custom-call(s32[1]{0:T(128)} %bitcast.1.to_ref, bf16[128,1152]{1,0:T(8,128)(2,1)S(1)} %copy-done, bf16[128,4608]{1,0:T(8,128)(2,1)S(1)} %copy-done.2), custom_call_target="tpu_custom_call" | custom-call | flops 188743680 | bytes 1687556 | tf_op jit(solution)/shard_map/grams/pallas_call | solution.py:59
  25.0 6.8 %all-to-all-start = ((f32[16,8,128]{2,1,0:T(8,128)}), f32[16,8,128]{2,1,0:T(8,128)S(1)}, u32[]{:S(2)}, u32[]{:S(2)}) async-start(f32[16,8,128]{2,1,0:T(8,128)} %get-tuple-element.6), calls=%async_computation | async-start | bytes 131072 | tf_op jit(solution)/shard_map/all_to_all | solution.py:195
  32.5 2.6 %collective-permute-start.6 = (bf16[256,1152]{1,0:T(8,128)(2,1)S(1)}, bf16[256,1152]{1,0:T(8,128)(2,1)S(1)}, u32[]{:S(2)}, u32[]{:S(2)}) collective-permute-start(bf16[256,1152]{1,0:T(8,128)(2,1)S(1)} %pad_maximum_fusion), channel_id=1, source_target_pairs={{0,32},{32,64},{64,96},{96,128},{128,160},{160,192},{192,224},{224... | collective-permute-start | bytes 1769480 | tf_op jit(solution)/shard_map/ppermute | solution.py:168
  35.1 0.0 collective-permute-done.1.refs_4_
  35.1 2.6 %collective-permute-start.2 = (bf16[128,1152]{1,0:T(8,128)(2,1)S(1)}, bf16[128,1152]{1,0:T(8,128)(2,1)S(1)}, u32[]{:S(2)}, u32[]{:S(2)}) collective-permute-start(bf16[128,1152]{1,0:T(8,128)(2,1)S(1)} %collective-permute-done.1.refs_4_), channel_id=1, source_target_pairs={{0,32},{32,64},{64,96},{96,128},{128,160},{160,192},{192,224},{224... | collective-permute-start | bytes 884744 | tf_op jit(solution)/shard_map/ppermute | solution.py:173
  37.8 0.0 collective-permute-done.10.refs_5_
  37.8 1.9 %collective-permute-start.11 = (bf16[128,1152]{1,0:T(8,128)(2,1)S(1)}, bf16[128,1152]{1,0:T(8,128)(2,1)}, u32[]{:S(2)}, u32[]{:S(2)}) collective-permute-start(bf16[128,1152]{1,0:T(8,128)(2,1)S(1)} %collective-permute-done.10.refs_5_), channel_id=1, source_target_pairs={{0,32},{32,64},{64,96},{96,128},{128,160},{160,192},{192,224},{224... | collective-permute-start | bytes 884744 | tf_op jit(solution)/shard_map/ppermute | solution.py:174
  39.7 0.0 all-to-all-done.parts_ref
  39.8 0.7 collective-permute-start
  40.5 6.2 %collective-permute-done.2.refs_1_ = bf16[128,1152]{1,0:T(8,128)(2,1)S(1)} collective-permute-done((bf16[128,1152]{1,0:T(8,128)(2,1)S(1)}, bf16[128,1152]{1,0:T(8,128)(2,1)S(1)}, u32[]{:S(2)}, u32[]{:S(2)}) %collective-permute-start.2) | collective-permute-done | bytes 294944 | tf_op jit(solution)/shard_map/ppermute | solution.py:173
  46.7 3.5 %collective-permute-start.3 = (bf16[128,1152]{1,0:T(8,128)(2,1)S(1)}, bf16[128,1152]{1,0:T(8,128)(2,1)}, u32[]{:S(2)}, u32[]{:S(2)}) collective-permute-start(bf16[128,1152]{1,0:T(8,128)(2,1)S(1)} %collective-permute-done.2.refs_1_), channel_id=1, source_target_pairs={{0,32},{32,64},{64,96},{96,128},{128,160},{160,192},{192,224},{224... | collective-permute-start | bytes 884744 | tf_op jit(solution)/shard_map/ppermute | solution.py:173
  50.2 0.0 collective-permute-done.6.refs_2_
  50.2 3.5 %collective-permute-start.7 = (bf16[256,1152]{1,0:T(8,128)(2,1)S(1)}, bf16[256,1152]{1,0:T(8,128)(2,1)S(1)}, u32[]{:S(2)}, u32[]{:S(2)}) collective-permute-start(bf16[256,1152]{1,0:T(8,128)(2,1)S(1)} %collective-permute-done.6.refs_2_), channel_id=1, source_target_pairs={{0,32},{32,64},{64,96},{96,128},{128,160},{160,192},{192,224},{224... | collective-permute-start | bytes 1769480 | tf_op jit(solution)/shard_map/ppermute | solution.py:168
  53.7 0.0 collective-permute-done.11.refs_2_
  53.7 1.9 %collective-permute-start.12 = (bf16[128,1152]{1,0:T(8,128)(2,1)}, bf16[128,1152]{1,0:T(8,128)(2,1)}, u32[]{:S(2)}, u32[]{:S(2)}) collective-permute-start(bf16[128,1152]{1,0:T(8,128)(2,1)} %collective-permute-done.11.refs_2_), channel_id=1, source_target_pairs={{0,32},{32,64},{64,96},{96,128},{128,160},{160,192},{192,224},{224... | collective-permute-start | bytes 884744 | tf_op jit(solution)/shard_map/ppermute | solution.py:174
  55.7 0.0 collective-permute-done.block_ref
  55.7 1.2 %spread.1 = bf16[16,288,128]{2,1,0:T(8,128)(2,1)} custom-call(bf16[288,128]{1,0:T(8,128)(2,1)S(1)} %collective-permute-done.block_ref), custom_call_target="tpu_custom_call" | custom-call | flops 10000000000 | bytes 1253376 | tf_op jit(solution)/shard_map/spread/pallas_call | solution.py:59
  56.9 8.7 %all-to-all-start.1 = ((bf16[16,288,128]{2,1,0:T(8,128)(2,1)}), bf16[16,288,128]{2,1,0:T(8,128)(2,1)S(1)}, u32[]{:S(2)}, u32[]{:S(2)}) async-start(bf16[16,288,128]{2,1,0:T(8,128)(2,1)} %spread.1), calls=%async_computation.1 | async-start | bytes 2359296 | tf_op jit(solution)/shard_map/all_to_all | solution.py:199
  65.6 0.0 collective-permute-done.3.refs_3_
  65.6 2.9 %collective-permute-start.4 = (bf16[128,1152]{1,0:T(8,128)(2,1)}, bf16[128,1152]{1,0:T(8,128)(2,1)S(1)}, u32[]{:S(2)}, u32[]{:S(2)}) collective-permute-start(bf16[128,1152]{1,0:T(8,128)(2,1)} %collective-permute-done.3.refs_3_), channel_id=1, source_target_pairs={{0,32},{32,64},{64,96},{96,128},{128,160},{160,192},{192,224},{224... | collective-permute-start | bytes 884744 | tf_op jit(solution)/shard_map/ppermute | solution.py:173
  68.6 0.0 collective-permute-done.12.refs_4_
  68.6 3.4 %collective-permute-start.13 = (bf16[128,1152]{1,0:T(8,128)(2,1)}, bf16[128,1152]{1,0:T(8,128)(2,1)}, u32[]{:S(2)}, u32[]{:S(2)}) collective-permute-start(bf16[128,1152]{1,0:T(8,128)(2,1)} %collective-permute-done.12.refs_4_), channel_id=1, source_target_pairs={{0,32},{32,64},{64,96},{96,128},{128,160},{160,192},{192,224},{224... | collective-permute-start | bytes 884744 | tf_op jit(solution)/shard_map/ppermute | solution.py:174
  72.0 1.6 %collective-permute-done.4.refs_0_ = bf16[128,1152]{1,0:T(8,128)(2,1)S(1)} collective-permute-done((bf16[128,1152]{1,0:T(8,128)(2,1)}, bf16[128,1152]{1,0:T(8,128)(2,1)S(1)}, u32[]{:S(2)}, u32[]{:S(2)}) %collective-permute-start.4) | collective-permute-done | bytes 294944 | tf_op jit(solution)/shard_map/ppermute | solution.py:173
  73.6 0.0 collective-permute-done.7.refs_1_.refs_3_
  73.6 4.1 %collective-permute-start.8 = (bf16[128,1152]{1,0:T(8,128)(2,1)S(1)}, bf16[128,1152]{1,0:T(8,128)(2,1)}, u32[]{:S(2)}, u32[]{:S(2)}) collective-permute-start(bf16[128,1152]{1,0:T(8,128)(2,1)S(1)} %after.2.refs_5_), channel_id=1, source_target_pairs={{0,32},{32,64},{64,96},{96,128},{128,160},{160,192},{192,224},{224... | collective-permute-start | bytes 884744 | tf_op jit(solution)/shard_map/ppermute | solution.py:173
  77.7 0.0 collective-permute-done.13.refs_0_
  77.8 3.4 %collective-permute-start.14 = (bf16[128,1152]{1,0:T(8,128)(2,1)}, bf16[128,1152]{1,0:T(8,128)(2,1)}, u32[]{:S(2)}, u32[]{:S(2)}) collective-permute-start(bf16[128,1152]{1,0:T(8,128)(2,1)} %after.3.refs_6_), channel_id=1, source_target_pairs={{0,32},{32,64},{64,96},{96,128},{128,160},{160,192},{192,224},{224... | collective-permute-start | bytes 884744 | tf_op jit(solution)/shard_map/ppermute | solution.py:174
  81.1 0.3 collective-permute-done.8.refs_7_
  81.4 5.3 %collective-permute-start.9 = (bf16[128,1152]{1,0:T(8,128)(2,1)}, bf16[128,1152]{1,0:T(8,128)(2,1)S(1)}, u32[]{:S(2)}, u32[]{:S(2)}) collective-permute-start(bf16[128,1152]{1,0:T(8,128)(2,1)} %collective-permute-done.8.refs_7_), channel_id=1, source_target_pairs={{0,32},{32,64},{64,96},{96,128},{128,160},{160,192},{192,224},{224... | collective-permute-start | bytes 884744 | tf_op jit(solution)/shard_map/ppermute | solution.py:173
  86.7 0.0 copy-start.4
  86.7 0.9 products.2.refs_9_
  87.7 0.0 collective-permute-done.14.refs_8_
  87.7 0.0 copy-done.4
  87.7 0.1 copy-done.6
  87.8 2.3 %products.3.refs_1_ = f32[288,1152]{1,0:T(8,128)S(1)} custom-call(bf16[16,288,128]{2,1,0:T(8,128)(2,1)S(1)} %all-to-all-done.1.refs_0_.s_ref, bf16[128,1152]{1,0:T(8,128)(2,1)S(1)} %copy-done.4, bf16[128,1152]{1,0:T(8,128)(2,1)} %collective-permute-done.11.refs_2_, bf16[128,1152]{1,0:T(8,128)(2,1)} %collective-permute-done.3.refs_3_, ...), custom_call_target="tpu_custom_call" | custom-call | flops 679477248 | bytes 6193152 | tf_op jit(solution)/shard_map/products/pallas_call | solution.py:59
  90.1 0.6 collective-permute-done.9.refs_0_
  90.7 0.2 last.3
  90.9 9.1 %collective-permute-start.15 = (f32[144,1152]{1,0:T(8,128)S(1)}, f32[144,1152]{1,0:T(8,128)S(1)}, u32[]{:S(2)}, u32[]{:S(2)}) collective-permute-start(f32[144,1152]{1,0:T(8,128)S(1)} %last.3), channel_id=1, source_target_pairs={{0,16},{16,0},{1,17},{17,1},{2,18},{18,2},{3,19},{19,3},{4,20},{20... | collective-permute-start | bytes 1990664 | tf_op jit(solution)/shard_map/ppermute | solution.py:205
  100.1 0.5 slice.3
  100.6 0.2 last.2
  100.8 0.9 collective-permute-done.15
  101.8 0.9 multiply_bitcast_fusion
  (14 shorter events, 0.1 us)
Async XLA Ops:
  0.6 15.4 %collective-permute-start.5 = (bf16[128,1152]{1,0:T(8,128)(2,1)}, bf16[128,1152]{1,0:T(8,128)(2,1)S(1)}, u32[]{:S(2)}, u32[]{:S(2)}) collective-permute-start(bf16[128,1152]{1,0:T(8,128)(2,1)} %refs_1_.1), channel_id=1, source_target_pairs={{0,16},{16,0},{1,17},{17,1},{2,18},{18,2},{3,19},{19,3},{4,20},{20... | collective-permute-start | bytes 884744 | tf_op jit(solution)/shard_map/ppermute | solution.py:164
  9.4 25.7 %collective-permute-start.1 = (bf16[128,1152]{1,0:T(8,128)(2,1)}, bf16[128,1152]{1,0:T(8,128)(2,1)S(1)}, u32[]{:S(2)}, u32[]{:S(2)}) collective-permute-start(bf16[128,1152]{1,0:T(8,128)(2,1)} %refs_1_.1), channel_id=1, source_target_pairs={{0,96},{32,128},{64,160},{96,192},{128,224},{160,256},{192,288},{2... | collective-permute-start | bytes 884744 | tf_op jit(solution)/shard_map/ppermute | solution.py:170
  16.1 21.7 %collective-permute-start.10 = (bf16[128,1152]{1,0:T(8,128)(2,1)S(1)}, bf16[128,1152]{1,0:T(8,128)(2,1)S(1)}, u32[]{:S(2)}, u32[]{:S(2)}) collective-permute-start(bf16[128,1152]{1,0:T(8,128)(2,1)S(1)} %collective-permute-done.5), channel_id=1, source_target_pairs={{0,96},{32,128},{64,160},{96,192},{128,224},{160,256},{192,288},{2... | collective-permute-start | bytes 884744 | tf_op jit(solution)/shard_map/ppermute | solution.py:170
  20.8 1.0 copy-start
  21.8 1.3 %copy-start.2 = (bf16[128,4608]{1,0:T(8,128)(2,1)S(1)}, bf16[128,4608]{1,0:T(8,128)(2,1)}, u32[]{:S(2)}) copy-start(bf16[128,4608]{1,0:T(8,128)(2,1)} %g_hbm.1) | copy-start | bytes 3538948
  23.1 9.4 %copy-start.1 = (bf16[128,1152]{1,0:T(8,128)(2,1)S(1)}, bf16[128,1152]{1,0:T(8,128)(2,1)}, u32[]{:S(2)}) copy-start(bf16[128,1152]{1,0:T(8,128)(2,1)} %refs_1_.1) | copy-start | bytes 884740
  25.0 14.7 %all-to-all-start = ((f32[16,8,128]{2,1,0:T(8,128)}), f32[16,8,128]{2,1,0:T(8,128)S(1)}, u32[]{:S(2)}, u32[]{:S(2)}) async-start(f32[16,8,128]{2,1,0:T(8,128)} %get-tuple-element.6), calls=%async_computation | async-start | bytes 131072 | tf_op jit(solution)/shard_map/all_to_all | solution.py:195
  32.5 17.7 %collective-permute-start.6 = (bf16[256,1152]{1,0:T(8,128)(2,1)S(1)}, bf16[256,1152]{1,0:T(8,128)(2,1)S(1)}, u32[]{:S(2)}, u32[]{:S(2)}) collective-permute-start(bf16[256,1152]{1,0:T(8,128)(2,1)S(1)} %pad_maximum_fusion), channel_id=1, source_target_pairs={{0,32},{32,64},{64,96},{96,128},{128,160},{160,192},{192,224},{224... | collective-permute-start | bytes 1769480 | tf_op jit(solution)/shard_map/ppermute | solution.py:168
  35.1 11.5 %collective-permute-start.2 = (bf16[128,1152]{1,0:T(8,128)(2,1)S(1)}, bf16[128,1152]{1,0:T(8,128)(2,1)S(1)}, u32[]{:S(2)}, u32[]{:S(2)}) collective-permute-start(bf16[128,1152]{1,0:T(8,128)(2,1)S(1)} %collective-permute-done.1.refs_4_), channel_id=1, source_target_pairs={{0,32},{32,64},{64,96},{96,128},{128,160},{160,192},{192,224},{224... | collective-permute-start | bytes 884744 | tf_op jit(solution)/shard_map/ppermute | solution.py:173
  37.8 15.9 %collective-permute-start.11 = (bf16[128,1152]{1,0:T(8,128)(2,1)S(1)}, bf16[128,1152]{1,0:T(8,128)(2,1)}, u32[]{:S(2)}, u32[]{:S(2)}) collective-permute-start(bf16[128,1152]{1,0:T(8,128)(2,1)S(1)} %collective-permute-done.10.refs_5_), channel_id=1, source_target_pairs={{0,32},{32,64},{64,96},{96,128},{128,160},{160,192},{192,224},{224... | collective-permute-start | bytes 884744 | tf_op jit(solution)/shard_map/ppermute | solution.py:174
  39.8 15.9 %collective-permute-start = (bf16[288,128]{1,0:T(8,128)(2,1)S(1)}, bf16[288,128]{1,0:T(8,128)(2,1)S(1)}, u32[]{:S(2)}, u32[]{:S(2)}) collective-permute-start(bf16[288,128]{1,0:T(8,128)(2,1)S(1)} %get-tuple-element.8), channel_id=1, source_target_pairs={{0,0},{1,33},{2,66},{3,99},{4,132},{5,165},{6,198},{7,231},{8,264}... | collective-permute-start | bytes 221192 | tf_op jit(solution)/shard_map/ppermute | solution.py:197
  46.7 10.2 %copy-start.3 = (bf16[128,1152]{1,0:T(8,128)(2,1)}, bf16[128,1152]{1,0:T(8,128)(2,1)S(1)}, u32[]{:S(2)}) copy-start(bf16[128,1152]{1,0:T(8,128)(2,1)S(1)} %collective-permute-done.2.refs_1_) | copy-start | bytes 884740
  46.7 18.9 %collective-permute-start.3 = (bf16[128,1152]{1,0:T(8,128)(2,1)S(1)}, bf16[128,1152]{1,0:T(8,128)(2,1)}, u32[]{:S(2)}, u32[]{:S(2)}) collective-permute-start(bf16[128,1152]{1,0:T(8,128)(2,1)S(1)} %collective-permute-done.2.refs_1_), channel_id=1, source_target_pairs={{0,32},{32,64},{64,96},{96,128},{128,160},{160,192},{192,224},{224... | collective-permute-start | bytes 884744 | tf_op jit(solution)/shard_map/ppermute | solution.py:173
  50.2 23.3 %collective-permute-start.7 = (bf16[256,1152]{1,0:T(8,128)(2,1)S(1)}, bf16[256,1152]{1,0:T(8,128)(2,1)S(1)}, u32[]{:S(2)}, u32[]{:S(2)}) collective-permute-start(bf16[256,1152]{1,0:T(8,128)(2,1)S(1)} %collective-permute-done.6.refs_2_), channel_id=1, source_target_pairs={{0,32},{32,64},{64,96},{96,128},{128,160},{160,192},{192,224},{224... | collective-permute-start | bytes 1769480 | tf_op jit(solution)/shard_map/ppermute | solution.py:168
  53.7 14.8 %collective-permute-start.12 = (bf16[128,1152]{1,0:T(8,128)(2,1)}, bf16[128,1152]{1,0:T(8,128)(2,1)}, u32[]{:S(2)}, u32[]{:S(2)}) collective-permute-start(bf16[128,1152]{1,0:T(8,128)(2,1)} %collective-permute-done.11.refs_2_), channel_id=1, source_target_pairs={{0,32},{32,64},{64,96},{96,128},{128,160},{160,192},{192,224},{224... | collective-permute-start | bytes 884744 | tf_op jit(solution)/shard_map/ppermute | solution.py:174
  56.9 29.8 %all-to-all-start.1 = ((bf16[16,288,128]{2,1,0:T(8,128)(2,1)}), bf16[16,288,128]{2,1,0:T(8,128)(2,1)S(1)}, u32[]{:S(2)}, u32[]{:S(2)}) async-start(bf16[16,288,128]{2,1,0:T(8,128)(2,1)} %spread.1), calls=%async_computation.1 | async-start | bytes 2359296 | tf_op jit(solution)/shard_map/all_to_all | solution.py:199
  65.6 8.0 %collective-permute-start.4 = (bf16[128,1152]{1,0:T(8,128)(2,1)}, bf16[128,1152]{1,0:T(8,128)(2,1)S(1)}, u32[]{:S(2)}, u32[]{:S(2)}) collective-permute-start(bf16[128,1152]{1,0:T(8,128)(2,1)} %collective-permute-done.3.refs_3_), channel_id=1, source_target_pairs={{0,32},{32,64},{64,96},{96,128},{128,160},{160,192},{192,224},{224... | collective-permute-start | bytes 884744 | tf_op jit(solution)/shard_map/ppermute | solution.py:173
  68.6 9.2 %collective-permute-start.13 = (bf16[128,1152]{1,0:T(8,128)(2,1)}, bf16[128,1152]{1,0:T(8,128)(2,1)}, u32[]{:S(2)}, u32[]{:S(2)}) collective-permute-start(bf16[128,1152]{1,0:T(8,128)(2,1)} %collective-permute-done.12.refs_4_), channel_id=1, source_target_pairs={{0,32},{32,64},{64,96},{96,128},{128,160},{160,192},{192,224},{224... | collective-permute-start | bytes 884744 | tf_op jit(solution)/shard_map/ppermute | solution.py:174
  73.6 4.2 %copy-start.5 = (bf16[128,1152]{1,0:T(8,128)(2,1)}, bf16[128,1152]{1,0:T(8,128)(2,1)S(1)}, u32[]{:S(2)}) copy-start(bf16[128,1152]{1,0:T(8,128)(2,1)S(1)} %after.2.refs_5_) | copy-start | bytes 884740
  73.6 7.8 %collective-permute-start.8 = (bf16[128,1152]{1,0:T(8,128)(2,1)S(1)}, bf16[128,1152]{1,0:T(8,128)(2,1)}, u32[]{:S(2)}, u32[]{:S(2)}) collective-permute-start(bf16[128,1152]{1,0:T(8,128)(2,1)S(1)} %after.2.refs_5_), channel_id=1, source_target_pairs={{0,32},{32,64},{64,96},{96,128},{128,160},{160,192},{192,224},{224... | collective-permute-start | bytes 884744 | tf_op jit(solution)/shard_map/ppermute | solution.py:173
  77.8 9.9 %collective-permute-start.14 = (bf16[128,1152]{1,0:T(8,128)(2,1)}, bf16[128,1152]{1,0:T(8,128)(2,1)}, u32[]{:S(2)}, u32[]{:S(2)}) collective-permute-start(bf16[128,1152]{1,0:T(8,128)(2,1)} %after.3.refs_6_), channel_id=1, source_target_pairs={{0,32},{32,64},{64,96},{96,128},{128,160},{160,192},{192,224},{224... | collective-permute-start | bytes 884744 | tf_op jit(solution)/shard_map/ppermute | solution.py:174
  81.4 9.3 %collective-permute-start.9 = (bf16[128,1152]{1,0:T(8,128)(2,1)}, bf16[128,1152]{1,0:T(8,128)(2,1)S(1)}, u32[]{:S(2)}, u32[]{:S(2)}) collective-permute-start(bf16[128,1152]{1,0:T(8,128)(2,1)} %collective-permute-done.8.refs_7_), channel_id=1, source_target_pairs={{0,32},{32,64},{64,96},{96,128},{128,160},{160,192},{192,224},{224... | collective-permute-start | bytes 884744 | tf_op jit(solution)/shard_map/ppermute | solution.py:173
  86.7 1.0 copy-start.4
  86.7 1.0 %copy-start.6 = (bf16[128,1152]{1,0:T(8,128)(2,1)S(1)}, bf16[128,1152]{1,0:T(8,128)(2,1)}, u32[]{:S(2)}) copy-start(bf16[128,1152]{1,0:T(8,128)(2,1)} %copy-done.5) | copy-start | bytes 884740
  90.9 10.9 %collective-permute-start.15 = (f32[144,1152]{1,0:T(8,128)S(1)}, f32[144,1152]{1,0:T(8,128)S(1)}, u32[]{:S(2)}, u32[]{:S(2)}) collective-permute-start(f32[144,1152]{1,0:T(8,128)S(1)} %last.3), channel_id=1, source_target_pairs={{0,16},{16,0},{1,17},{17,1},{2,18},{18,2},{3,19},{19,3},{4,20},{20... | collective-permute-start | bytes 1990664 | tf_op jit(solution)/shard_map/ppermute | solution.py:205

commit v8 on v7

--- a/solution.py
+++ b/solution.py
@@ -173,7 +173,7 @@
         p = lax.ppermute(p, LINE, step_pairs(1))
         q = lax.ppermute(q, LINE, step_pairs(1)) if hop < HOPS else None
         if hop == 6:
-            p, q = after(p, blocks[2], cost=2000000000), after(q, cost=4000000000)
+            p, q = after(p, blocks[2], cost=2000000000), after(q, cost=8000000000)
         blocks[hop] = (p, q)
 
     to = lax.rem(z + (1 - 2 * core) * t + NZ, NZ).astype(jnp.int32).reshape(1)
@@ -195,6 +195,7 @@
     parts = lax.all_to_all(part, PLANE, 0, 0, tiled=False)
     block, norm = clipped(parts)
     block = lax.ppermute(block, ALL, spread_pairs())
+    block = after(block, cost=4000000000)
     [spread] = call(spread_kernel, [jax.ShapeDtypeStruct((NT, CHIP, SEQ), jnp.bfloat16)], [block], "spread", 10000000000)
     s = lax.all_to_all(spread, PLANE, 0, 0, tiled=False)
 

time: 103 us -> 103 us (level)
  starting transfers between devices: 80.7 us -> 78.3 us
  waiting for transfers between devices: 9.62 us -> 11.8 us
    all_to_all x1, waiting for transfers between devices: 0.01 us -> 3.21 us  [per_device(): s = lax.all_to_all(spread, PLANE, 0, 0, tiled=False)]
    ppermute x5, starting transfers between devices: 18.6 us -> 16.1 us  [per_device(): p = lax.ppermute(p, LINE, step_pairs(1))]
    ppermute x1, starting transfers between devices: 9.13 us -> 6.84 us  [per_device(): theirs = lax.ppermute(last_products(1 - row, s, last, acc, 0), 'core', SWAP)]
    all_to_all x1, starting transfers between devices: 8.7 us -> 10.5 us  [per_device(): s = lax.all_to_all(spread, PLANE, 0, 0, tiled=False)]
    ppermute x4, starting transfers between devices: 10.6 us -> 11.8 us  [per_device(): q = lax.ppermute(q, LINE, step_pairs(1)) if hop < HOPS else None]
    ppermute x5, waiting for transfers between devices: 8.64 us -> 7.58 us  [per_device(): p = lax.ppermute(p, LINE, step_pairs(1))]
    unnamed x14 -> x18, local copies, waits for them, and re-layouts: 2.35 us -> 2.45 us
  transfers between devices with their start and end apart: 18 -> 18, of which waited for: 5 -> 4; matrix products, arithmetic and copies ran while one was open for 1% -> 1% of each run, Pallas kernels for 6% -> 6%
where the time goes in v8:
time: 103 us; the launch traced here: 102 us
  starting transfers between devices  78.3 us (76%)
  waiting for transfers between devices  11.8 us (11%)
  Pallas kernels  6.8 us (7%)
  local copies, waits for them, and re-layouts  2.97 us (3%)
  between operations  1.68 us (2%)
    ppermute x5, starting transfers between devices, per_device(): p = lax.ppermute(p, LINE, step_pairs(1))  16.1 us
    ppermute x4, starting transfers between devices, per_device(): q = lax.ppermute(q, LINE, step_pairs(1)) if hop < HOPS else None  11.8 us
    all_to_all x1, starting transfers between devices, per_device(): s = lax.all_to_all(spread, PLANE, 0, 0, tiled=False)  10.5 us
    ppermute x1, starting transfers between devices, per_device(): other = lax.ppermute(hidden, 'core', SWAP)  8.79 us
    ppermute x5, waiting for transfers between devices, per_device(): p = lax.ppermute(p, LINE, step_pairs(1))  7.58 us
    ppermute x1, starting transfers between devices, per_device(): theirs = lax.ppermute(last_products(1 - row, s, last, acc, 0), 'core', SWAP)  6.84 us
    pallas_call x7, Pallas kernels, call(): pl.pallas_call(kernel, out_shape=outs, in_specs=[smem() if a.dtype == jnp...  6.79 us
    all_to_all x1, starting transfers between devices, per_device(): parts = lax.all_to_all(part, PLANE, 0, 0, tiled=False)  6.77 us
  transfers between devices with their start and end apart: 18, of which 4 were waited for; matrix products, arithmetic and copies ran while one was open for 1% of the time, Pallas kernels for 6%

profile of v8, /device:TPU:1, one launch (start us, length us, event | category | flops | bytes accessed | tf_op | source)
XLA Modules:
  0.0 102.5 jit_solution(4700162429871519064)
XLA Ops:
  0.6 8.8 %collective-permute-start.5 = (bf16[128,1152]{1,0:T(8,128)(2,1)}, bf16[128,1152]{1,0:T(8,128)(2,1)S(1)}, u32[]{:S(2)}, u32[]{:S(2)}) collective-permute-start(bf16[128,1152]{1,0:T(8,128)(2,1)} %refs_1_.1), channel_id=1, source_target_pairs={{0,16},{16,0},{1,17},{17,1},{2,18},{18,2},{3,19},{19,3},{4,20},{20... | collective-permute-start | bytes 884744 | tf_op jit(solution)/shard_map/ppermute | solution.py:164
  9.4 6.6 %collective-permute-start.1 = (bf16[128,1152]{1,0:T(8,128)(2,1)}, bf16[128,1152]{1,0:T(8,128)(2,1)S(1)}, u32[]{:S(2)}, u32[]{:S(2)}) collective-permute-start(bf16[128,1152]{1,0:T(8,128)(2,1)} %refs_1_.1), channel_id=1, source_target_pairs={{0,96},{32,128},{64,160},{96,192},{128,224},{160,256},{192,288},{2... | collective-permute-start | bytes 884744 | tf_op jit(solution)/shard_map/ppermute | solution.py:170
  16.1 0.0 collective-permute-done.5
  16.1 4.7 %collective-permute-start.10 = (bf16[128,1152]{1,0:T(8,128)(2,1)S(1)}, bf16[128,1152]{1,0:T(8,128)(2,1)S(1)}, u32[]{:S(2)}, u32[]{:S(2)}) collective-permute-start(bf16[128,1152]{1,0:T(8,128)(2,1)S(1)} %collective-permute-done.5), channel_id=1, source_target_pairs={{0,96},{32,128},{64,160},{96,192},{128,224},{160,256},{192,288},{2... | collective-permute-start | bytes 884744 | tf_op jit(solution)/shard_map/ppermute | solution.py:170
  20.8 1.0 copy-done
  21.8 1.3 %copy-done.2 = bf16[128,4608]{1,0:T(8,128)(2,1)S(1)} copy-done((bf16[128,4608]{1,0:T(8,128)(2,1)S(1)}, bf16[128,4608]{1,0:T(8,128)(2,1)}, u32[]{:S(2)}) %copy-start.2) | copy-done | bytes 1179672
  23.1 1.9 %grams.1 = (f32[16,8,128]{2,1,0:T(8,128)}, f32[288,128]{1,0:T(8,128)S(1)}) custom-call(s32[1]{0:T(128)} %bitcast.1.to_ref, bf16[128,1152]{1,0:T(8,128)(2,1)S(1)} %copy-done, bf16[128,4608]{1,0:T(8,128)(2,1)S(1)} %copy-done.2), custom_call_target="tpu_custom_call" | custom-call | flops 188743680 | bytes 1687556 | tf_op jit(solution)/shard_map/grams/pallas_call | solution.py:59
  25.0 6.8 %all-to-all-start = ((f32[16,8,128]{2,1,0:T(8,128)}), f32[16,8,128]{2,1,0:T(8,128)S(1)}, u32[]{:S(2)}, u32[]{:S(2)}) async-start(f32[16,8,128]{2,1,0:T(8,128)} %get-tuple-element.6), calls=%async_computation | async-start | bytes 131072 | tf_op jit(solution)/shard_map/all_to_all | solution.py:195
  32.5 2.6 %collective-permute-start.6 = (bf16[256,1152]{1,0:T(8,128)(2,1)S(1)}, bf16[256,1152]{1,0:T(8,128)(2,1)S(1)}, u32[]{:S(2)}, u32[]{:S(2)}) collective-permute-start(bf16[256,1152]{1,0:T(8,128)(2,1)S(1)} %pad_maximum_fusion), channel_id=1, source_target_pairs={{0,32},{32,64},{64,96},{96,128},{128,160},{160,192},{192,224},{224... | collective-permute-start | bytes 1769480 | tf_op jit(solution)/shard_map/ppermute | solution.py:168
  35.1 0.0 collective-permute-done.1.refs_4_
  35.1 2.6 %collective-permute-start.2 = (bf16[128,1152]{1,0:T(8,128)(2,1)S(1)}, bf16[128,1152]{1,0:T(8,128)(2,1)S(1)}, u32[]{:S(2)}, u32[]{:S(2)}) collective-permute-start(bf16[128,1152]{1,0:T(8,128)(2,1)S(1)} %collective-permute-done.1.refs_4_), channel_id=1, source_target_pairs={{0,32},{32,64},{64,96},{96,128},{128,160},{160,192},{192,224},{224... | collective-permute-start | bytes 884744 | tf_op jit(solution)/shard_map/ppermute | solution.py:173
  37.8 0.0 collective-permute-done.10.refs_5_
  37.8 1.9 %collective-permute-start.11 = (bf16[128,1152]{1,0:T(8,128)(2,1)S(1)}, bf16[128,1152]{1,0:T(8,128)(2,1)S(1)}, u32[]{:S(2)}, u32[]{:S(2)}) collective-permute-start(bf16[128,1152]{1,0:T(8,128)(2,1)S(1)} %collective-permute-done.10.refs_5_), channel_id=1, source_target_pairs={{0,32},{32,64},{64,96},{96,128},{128,160},{160,192},{192,224},{224... | collective-permute-start | bytes 884744 | tf_op jit(solution)/shard_map/ppermute | solution.py:174
  39.7 0.0 all-to-all-done.parts_ref
  39.8 0.7 collective-permute-start
  40.5 6.1 %collective-permute-done.2.refs_1_ = bf16[128,1152]{1,0:T(8,128)(2,1)S(1)} collective-permute-done((bf16[128,1152]{1,0:T(8,128)(2,1)S(1)}, bf16[128,1152]{1,0:T(8,128)(2,1)S(1)}, u32[]{:S(2)}, u32[]{:S(2)}) %collective-permute-start.2) | collective-permute-done | bytes 294944 | tf_op jit(solution)/shard_map/ppermute | solution.py:173
  46.6 3.7 %collective-permute-start.3 = (bf16[128,1152]{1,0:T(8,128)(2,1)S(1)}, bf16[128,1152]{1,0:T(8,128)(2,1)}, u32[]{:S(2)}, u32[]{:S(2)}) collective-permute-start(bf16[128,1152]{1,0:T(8,128)(2,1)S(1)} %collective-permute-done.2.refs_1_), channel_id=1, source_target_pairs={{0,32},{32,64},{64,96},{96,128},{128,160},{160,192},{192,224},{224... | collective-permute-start | bytes 884744 | tf_op jit(solution)/shard_map/ppermute | solution.py:173
  50.2 0.0 collective-permute-done.11.refs_2_
  50.2 3.4 %collective-permute-start.12 = (bf16[128,1152]{1,0:T(8,128)(2,1)S(1)}, bf16[128,1152]{1,0:T(8,128)(2,1)}, u32[]{:S(2)}, u32[]{:S(2)}) collective-permute-start(bf16[128,1152]{1,0:T(8,128)(2,1)S(1)} %collective-permute-done.11.refs_2_), channel_id=1, source_target_pairs={{0,32},{32,64},{64,96},{96,128},{128,160},{160,192},{192,224},{224... | collective-permute-start | bytes 884744 | tf_op jit(solution)/shard_map/ppermute | solution.py:174
  53.6 0.0 collective-permute-done.refs_0_
  53.7 0.0 collective-permute-done.6.refs_2_
  53.7 2.8 %collective-permute-start.7 = (bf16[256,1152]{1,0:T(8,128)(2,1)S(1)}, bf16[256,1152]{1,0:T(8,128)(2,1)S(1)}, u32[]{:S(2)}, u32[]{:S(2)}) collective-permute-start(bf16[256,1152]{1,0:T(8,128)(2,1)S(1)} %collective-permute-done.6.refs_2_), channel_id=1, source_target_pairs={{0,32},{32,64},{64,96},{96,128},{128,160},{160,192},{192,224},{224... | collective-permute-start | bytes 1769480 | tf_op jit(solution)/shard_map/ppermute | solution.py:168
  56.5 0.0 collective-permute-done.3.refs_3_
  56.5 2.4 %collective-permute-start.4 = (bf16[128,1152]{1,0:T(8,128)(2,1)}, bf16[128,1152]{1,0:T(8,128)(2,1)S(1)}, u32[]{:S(2)}, u32[]{:S(2)}) collective-permute-start(bf16[128,1152]{1,0:T(8,128)(2,1)} %collective-permute-done.3.refs_3_), channel_id=1, source_target_pairs={{0,32},{32,64},{64,96},{96,128},{128,160},{160,192},{192,224},{224... | collective-permute-start | bytes 884744 | tf_op jit(solution)/shard_map/ppermute | solution.py:173
  59.0 0.0 collective-permute-done.12.refs_4_
  59.0 3.4 %collective-permute-start.13 = (bf16[128,1152]{1,0:T(8,128)(2,1)}, bf16[128,1152]{1,0:T(8,128)(2,1)}, u32[]{:S(2)}, u32[]{:S(2)}) collective-permute-start(bf16[128,1152]{1,0:T(8,128)(2,1)} %collective-permute-done.12.refs_4_), channel_id=1, source_target_pairs={{0,32},{32,64},{64,96},{96,128},{128,160},{160,192},{192,224},{224... | collective-permute-start | bytes 884744 | tf_op jit(solution)/shard_map/ppermute | solution.py:174
  62.4 1.2 %spread.1 = bf16[16,288,128]{2,1,0:T(8,128)(2,1)} custom-call(bf16[288,128]{1,0:T(8,128)(2,1)S(1)} %after.3.block_ref), custom_call_target="tpu_custom_call" | custom-call | flops 10000000000 | bytes 1253376 | tf_op jit(solution)/shard_map/spread/pallas_call | solution.py:59
  63.6 10.5 %all-to-all-start.1 = ((bf16[16,288,128]{2,1,0:T(8,128)(2,1)}), bf16[16,288,128]{2,1,0:T(8,128)(2,1)S(1)}, u32[]{:S(2)}, u32[]{:S(2)}) async-start(bf16[16,288,128]{2,1,0:T(8,128)(2,1)} %spread.1), calls=%async_computation.1 | async-start | bytes 2359296 | tf_op jit(solution)/shard_map/all_to_all | solution.py:200
  74.1 0.0 collective-permute-done.4.refs_0_
  74.1 0.0 collective-permute-done.7.refs_1_.refs_3_
  74.1 3.0 %collective-permute-start.8 = (bf16[128,1152]{1,0:T(8,128)(2,1)S(1)}, bf16[128,1152]{1,0:T(8,128)(2,1)}, u32[]{:S(2)}, u32[]{:S(2)}) collective-permute-start(bf16[128,1152]{1,0:T(8,128)(2,1)S(1)} %after.4.refs_5_), channel_id=1, source_target_pairs={{0,32},{32,64},{64,96},{96,128},{128,160},{160,192},{192,224},{224... | collective-permute-start | bytes 884744 | tf_op jit(solution)/shard_map/ppermute | solution.py:173
  77.2 0.0 collective-permute-done.13.refs_0_
  77.2 3.0 %collective-permute-start.14 = (bf16[128,1152]{1,0:T(8,128)(2,1)}, bf16[128,1152]{1,0:T(8,128)(2,1)}, u32[]{:S(2)}, u32[]{:S(2)}) collective-permute-start(bf16[128,1152]{1,0:T(8,128)(2,1)} %after.5.refs_6_), channel_id=1, source_target_pairs={{0,32},{32,64},{64,96},{96,128},{128,160},{160,192},{192,224},{224... | collective-permute-start | bytes 884744 | tf_op jit(solution)/shard_map/ppermute | solution.py:174
  80.2 1.5 %collective-permute-done.8.refs_7_ = bf16[128,1152]{1,0:T(8,128)(2,1)} collective-permute-done((bf16[128,1152]{1,0:T(8,128)(2,1)S(1)}, bf16[128,1152]{1,0:T(8,128)(2,1)}, u32[]{:S(2)}, u32[]{:S(2)}) %collective-permute-start.8) | collective-permute-done | bytes 294944 | tf_op jit(solution)/shard_map/ppermute | solution.py:173
  81.7 4.4 %collective-permute-start.9 = (bf16[128,1152]{1,0:T(8,128)(2,1)}, bf16[128,1152]{1,0:T(8,128)(2,1)S(1)}, u32[]{:S(2)}, u32[]{:S(2)}) collective-permute-start(bf16[128,1152]{1,0:T(8,128)(2,1)} %collective-permute-done.8.refs_7_), channel_id=1, source_target_pairs={{0,32},{32,64},{64,96},{96,128},{128,160},{160,192},{192,224},{224... | collective-permute-start | bytes 884744 | tf_op jit(solution)/shard_map/ppermute | solution.py:173
  86.1 3.2 %all-to-all-done.1.refs_0_.s_ref = bf16[16,288,128]{2,1,0:T(8,128)(2,1)S(1)} async-done(((bf16[16,288,128]{2,1,0:T(8,128)(2,1)}), bf16[16,288,128]{2,1,0:T(8,128)(2,1)S(1)}, u32[]{:S(2)}, u32[]{:S(2)}) %all-to-all-start.1) | async-done | bytes 1179680 | tf_op jit(solution)/shard_map/all_to_all | solution.py:200
  89.3 0.9 products.2.refs_9_
  90.2 0.0 collective-permute-done.14.refs_8_
  90.3 0.0 copy-done.4
  90.3 0.1 copy-done.6
  90.4 0.1 copy-done.8
  90.5 2.2 %products.3.refs_1_ = f32[288,1152]{1,0:T(8,128)S(1)} custom-call(bf16[16,288,128]{2,1,0:T(8,128)(2,1)S(1)} %all-to-all-done.1.refs_0_.s_ref, bf16[128,1152]{1,0:T(8,128)(2,1)S(1)} %copy-done.4, bf16[128,1152]{1,0:T(8,128)(2,1)S(1)} %copy-done.6, bf16[128,1152]{1,0:T(8,128)(2,1)} %collective-permute-done.3.refs_3_, ...), custom_call_target="tpu_custom_call" | custom-call | flops 679477248 | bytes 6193152 | tf_op jit(solution)/shard_map/products/pallas_call | solution.py:59
  92.7 0.2 last.3
  93.0 6.8 %collective-permute-start.15 = (f32[144,1152]{1,0:T(8,128)S(1)}, f32[144,1152]{1,0:T(8,128)S(1)}, u32[]{:S(2)}, u32[]{:S(2)}) collective-permute-start(f32[144,1152]{1,0:T(8,128)S(1)} %last.3), channel_id=1, source_target_pairs={{0,16},{16,0},{1,17},{17,1},{2,18},{18,2},{3,19},{19,3},{4,20},{20... | collective-permute-start | bytes 1990664 | tf_op jit(solution)/shard_map/ppermute | solution.py:206
  99.8 0.5 slice.3
  100.3 0.2 last.2
  100.6 0.9 collective-permute-done.15
  101.5 0.9 multiply_bitcast_fusion
  (19 shorter events, 0.1 us)
Async XLA Ops:
  0.6 15.4 %collective-permute-start.5 = (bf16[128,1152]{1,0:T(8,128)(2,1)}, bf16[128,1152]{1,0:T(8,128)(2,1)S(1)}, u32[]{:S(2)}, u32[]{:S(2)}) collective-permute-start(bf16[128,1152]{1,0:T(8,128)(2,1)} %refs_1_.1), channel_id=1, source_target_pairs={{0,16},{16,0},{1,17},{17,1},{2,18},{18,2},{3,19},{19,3},{4,20},{20... | collective-permute-start | bytes 884744 | tf_op jit(solution)/shard_map/ppermute | solution.py:164
  9.4 25.7 %collective-permute-start.1 = (bf16[128,1152]{1,0:T(8,128)(2,1)}, bf16[128,1152]{1,0:T(8,128)(2,1)S(1)}, u32[]{:S(2)}, u32[]{:S(2)}) collective-permute-start(bf16[128,1152]{1,0:T(8,128)(2,1)} %refs_1_.1), channel_id=1, source_target_pairs={{0,96},{32,128},{64,160},{96,192},{128,224},{160,256},{192,288},{2... | collective-permute-start | bytes 884744 | tf_op jit(solution)/shard_map/ppermute | solution.py:170
  16.1 21.7 %collective-permute-start.10 = (bf16[128,1152]{1,0:T(8,128)(2,1)S(1)}, bf16[128,1152]{1,0:T(8,128)(2,1)S(1)}, u32[]{:S(2)}, u32[]{:S(2)}) collective-permute-start(bf16[128,1152]{1,0:T(8,128)(2,1)S(1)} %collective-permute-done.5), channel_id=1, source_target_pairs={{0,96},{32,128},{64,160},{96,192},{128,224},{160,256},{192,288},{2... | collective-permute-start | bytes 884744 | tf_op jit(solution)/shard_map/ppermute | solution.py:170
  20.8 1.0 copy-start
  21.8 1.3 %copy-start.2 = (bf16[128,4608]{1,0:T(8,128)(2,1)S(1)}, bf16[128,4608]{1,0:T(8,128)(2,1)}, u32[]{:S(2)}) copy-start(bf16[128,4608]{1,0:T(8,128)(2,1)} %g_hbm.1) | copy-start | bytes 3538948
  23.1 9.4 %copy-start.1 = (bf16[128,1152]{1,0:T(8,128)(2,1)S(1)}, bf16[128,1152]{1,0:T(8,128)(2,1)}, u32[]{:S(2)}) copy-start(bf16[128,1152]{1,0:T(8,128)(2,1)} %refs_1_.1) | copy-start | bytes 884740
  25.0 14.7 %all-to-all-start = ((f32[16,8,128]{2,1,0:T(8,128)}), f32[16,8,128]{2,1,0:T(8,128)S(1)}, u32[]{:S(2)}, u32[]{:S(2)}) async-start(f32[16,8,128]{2,1,0:T(8,128)} %get-tuple-element.6), calls=%async_computation | async-start | bytes 131072 | tf_op jit(solution)/shard_map/all_to_all | solution.py:195
  32.5 21.2 %collective-permute-start.6 = (bf16[256,1152]{1,0:T(8,128)(2,1)S(1)}, bf16[256,1152]{1,0:T(8,128)(2,1)S(1)}, u32[]{:S(2)}, u32[]{:S(2)}) collective-permute-start(bf16[256,1152]{1,0:T(8,128)(2,1)S(1)} %pad_maximum_fusion), channel_id=1, source_target_pairs={{0,32},{32,64},{64,96},{96,128},{128,160},{160,192},{192,224},{224... | collective-permute-start | bytes 1769480 | tf_op jit(solution)/shard_map/ppermute | solution.py:168
  35.1 11.4 %collective-permute-start.2 = (bf16[128,1152]{1,0:T(8,128)(2,1)S(1)}, bf16[128,1152]{1,0:T(8,128)(2,1)S(1)}, u32[]{:S(2)}, u32[]{:S(2)}) collective-permute-start(bf16[128,1152]{1,0:T(8,128)(2,1)S(1)} %collective-permute-done.1.refs_4_), channel_id=1, source_target_pairs={{0,32},{32,64},{64,96},{96,128},{128,160},{160,192},{192,224},{224... | collective-permute-start | bytes 884744 | tf_op jit(solution)/shard_map/ppermute | solution.py:173
  37.8 12.4 %collective-permute-start.11 = (bf16[128,1152]{1,0:T(8,128)(2,1)S(1)}, bf16[128,1152]{1,0:T(8,128)(2,1)S(1)}, u32[]{:S(2)}, u32[]{:S(2)}) collective-permute-start(bf16[128,1152]{1,0:T(8,128)(2,1)S(1)} %collective-permute-done.10.refs_5_), channel_id=1, source_target_pairs={{0,32},{32,64},{64,96},{96,128},{128,160},{160,192},{192,224},{224... | collective-permute-start | bytes 884744 | tf_op jit(solution)/shard_map/ppermute | solution.py:174
  39.8 13.9 %collective-permute-start = (bf16[288,128]{1,0:T(8,128)(2,1)S(1)}, bf16[288,128]{1,0:T(8,128)(2,1)S(1)}, u32[]{:S(2)}, u32[]{:S(2)}) collective-permute-start(bf16[288,128]{1,0:T(8,128)(2,1)S(1)} %get-tuple-element.8), channel_id=1, source_target_pairs={{0,0},{1,33},{2,66},{3,99},{4,132},{5,165},{6,198},{7,231},{8,264}... | collective-permute-start | bytes 221192 | tf_op jit(solution)/shard_map/ppermute | solution.py:197
  46.6 7.1 %copy-start.3 = (bf16[128,1152]{1,0:T(8,128)(2,1)}, bf16[128,1152]{1,0:T(8,128)(2,1)S(1)}, u32[]{:S(2)}) copy-start(bf16[128,1152]{1,0:T(8,128)(2,1)S(1)} %collective-permute-done.2.refs_1_) | copy-start | bytes 884740
  46.6 10.0 %collective-permute-start.3 = (bf16[128,1152]{1,0:T(8,128)(2,1)S(1)}, bf16[128,1152]{1,0:T(8,128)(2,1)}, u32[]{:S(2)}, u32[]{:S(2)}) collective-permute-start(bf16[128,1152]{1,0:T(8,128)(2,1)S(1)} %collective-permute-done.2.refs_1_), channel_id=1, source_target_pairs={{0,32},{32,64},{64,96},{96,128},{128,160},{160,192},{192,224},{224... | collective-permute-start | bytes 884744 | tf_op jit(solution)/shard_map/ppermute | solution.py:173
  50.2 3.4 %copy-start.5 = (bf16[128,1152]{1,0:T(8,128)(2,1)}, bf16[128,1152]{1,0:T(8,128)(2,1)S(1)}, u32[]{:S(2)}) copy-start(bf16[128,1152]{1,0:T(8,128)(2,1)S(1)} %collective-permute-done.11.refs_2_) | copy-start | bytes 884740
  50.2 8.8 %collective-permute-start.12 = (bf16[128,1152]{1,0:T(8,128)(2,1)S(1)}, bf16[128,1152]{1,0:T(8,128)(2,1)}, u32[]{:S(2)}, u32[]{:S(2)}) collective-permute-start(bf16[128,1152]{1,0:T(8,128)(2,1)S(1)} %collective-permute-done.11.refs_2_), channel_id=1, source_target_pairs={{0,32},{32,64},{64,96},{96,128},{128,160},{160,192},{192,224},{224... | collective-permute-start | bytes 884744 | tf_op jit(solution)/shard_map/ppermute | solution.py:174
  53.7 20.4 %collective-permute-start.7 = (bf16[256,1152]{1,0:T(8,128)(2,1)S(1)}, bf16[256,1152]{1,0:T(8,128)(2,1)S(1)}, u32[]{:S(2)}, u32[]{:S(2)}) collective-permute-start(bf16[256,1152]{1,0:T(8,128)(2,1)S(1)} %collective-permute-done.6.refs_2_), channel_id=1, source_target_pairs={{0,32},{32,64},{64,96},{96,128},{128,160},{160,192},{192,224},{224... | collective-permute-start | bytes 1769480 | tf_op jit(solution)/shard_map/ppermute | solution.py:168
  56.5 17.5 %collective-permute-start.4 = (bf16[128,1152]{1,0:T(8,128)(2,1)}, bf16[128,1152]{1,0:T(8,128)(2,1)S(1)}, u32[]{:S(2)}, u32[]{:S(2)}) collective-permute-start(bf16[128,1152]{1,0:T(8,128)(2,1)} %collective-permute-done.3.refs_3_), channel_id=1, source_target_pairs={{0,32},{32,64},{64,96},{96,128},{128,160},{160,192},{192,224},{224... | collective-permute-start | bytes 884744 | tf_op jit(solution)/shard_map/ppermute | solution.py:173
  59.0 18.1 %collective-permute-start.13 = (bf16[128,1152]{1,0:T(8,128)(2,1)}, bf16[128,1152]{1,0:T(8,128)(2,1)}, u32[]{:S(2)}, u32[]{:S(2)}) collective-permute-start(bf16[128,1152]{1,0:T(8,128)(2,1)} %collective-permute-done.12.refs_4_), channel_id=1, source_target_pairs={{0,32},{32,64},{64,96},{96,128},{128,160},{160,192},{192,224},{224... | collective-permute-start | bytes 884744 | tf_op jit(solution)/shard_map/ppermute | solution.py:174
  63.6 25.7 %all-to-all-start.1 = ((bf16[16,288,128]{2,1,0:T(8,128)(2,1)}), bf16[16,288,128]{2,1,0:T(8,128)(2,1)S(1)}, u32[]{:S(2)}, u32[]{:S(2)}) async-start(bf16[16,288,128]{2,1,0:T(8,128)(2,1)} %spread.1), calls=%async_computation.1 | async-start | bytes 2359296 | tf_op jit(solution)/shard_map/all_to_all | solution.py:200
  74.1 3.1 %copy-start.7 = (bf16[128,1152]{1,0:T(8,128)(2,1)}, bf16[128,1152]{1,0:T(8,128)(2,1)S(1)}, u32[]{:S(2)}) copy-start(bf16[128,1152]{1,0:T(8,128)(2,1)S(1)} %after.4.refs_5_) | copy-start | bytes 884740
  74.1 7.6 %collective-permute-start.8 = (bf16[128,1152]{1,0:T(8,128)(2,1)S(1)}, bf16[128,1152]{1,0:T(8,128)(2,1)}, u32[]{:S(2)}, u32[]{:S(2)}) collective-permute-start(bf16[128,1152]{1,0:T(8,128)(2,1)S(1)} %after.4.refs_5_), channel_id=1, source_target_pairs={{0,32},{32,64},{64,96},{96,128},{128,160},{160,192},{192,224},{224... | collective-permute-start | bytes 884744 | tf_op jit(solution)/shard_map/ppermute | solution.py:173
  77.2 13.1 %collective-permute-start.14 = (bf16[128,1152]{1,0:T(8,128)(2,1)}, bf16[128,1152]{1,0:T(8,128)(2,1)}, u32[]{:S(2)}, u32[]{:S(2)}) collective-permute-start(bf16[128,1152]{1,0:T(8,128)(2,1)} %after.5.refs_6_), channel_id=1, source_target_pairs={{0,32},{32,64},{64,96},{96,128},{128,160},{160,192},{192,224},{224... | collective-permute-start | bytes 884744 | tf_op jit(solution)/shard_map/ppermute | solution.py:174
  81.7 11.0 %collective-permute-start.9 = (bf16[128,1152]{1,0:T(8,128)(2,1)}, bf16[128,1152]{1,0:T(8,128)(2,1)S(1)}, u32[]{:S(2)}, u32[]{:S(2)}) collective-permute-start(bf16[128,1152]{1,0:T(8,128)(2,1)} %collective-permute-done.8.refs_7_), channel_id=1, source_target_pairs={{0,32},{32,64},{64,96},{96,128},{128,160},{160,192},{192,224},{224... | collective-permute-start | bytes 884744 | tf_op jit(solution)/shard_map/ppermute | solution.py:173
  89.3 1.0 copy-start.4
  89.3 1.0 %copy-start.6 = (bf16[128,1152]{1,0:T(8,128)(2,1)S(1)}, bf16[128,1152]{1,0:T(8,128)(2,1)}, u32[]{:S(2)}) copy-start(bf16[128,1152]{1,0:T(8,128)(2,1)} %copy-done.5) | copy-start | bytes 884740
  89.3 1.1 %copy-start.8 = (bf16[128,1152]{1,0:T(8,128)(2,1)S(1)}, bf16[128,1152]{1,0:T(8,128)(2,1)}, u32[]{:S(2)}) copy-start(bf16[128,1152]{1,0:T(8,128)(2,1)} %copy-done.7) | copy-start | bytes 884740
  93.0 8.6 %collective-permute-start.15 = (f32[144,1152]{1,0:T(8,128)S(1)}, f32[144,1152]{1,0:T(8,128)S(1)}, u32[]{:S(2)}, u32[]{:S(2)}) collective-permute-start(f32[144,1152]{1,0:T(8,128)S(1)} %last.3), channel_id=1, source_target_pairs={{0,16},{16,0},{1,17},{17,1},{2,18},{18,2},{3,19},{19,3},{4,20},{20... | collective-permute-start | bytes 1990664 | tf_op jit(solution)/shard_map/ppermute | solution.py:206
